TPU v7x, 256 devices: a whole 4x4x8 slice. The times are simulated.
256 devices in a mesh: station: 64 (over x, z, core), sample: 4 (over y).
Axes of the slice: x: 4, y: 4, z: 8, core: 2. Of those that a mesh axis runs over, the one named last changes fastest.
Arguments:
- flux: bfloat16 [16, 2048, 3584], P('sample', 'station'), may hold values from -6 to 6
- coeff: float32 [2048, 3584], P('station'), may hold values from 0.02 to 0.24
- diff_steps: int32 [16], P('sample'), may hold values from 3 to 6, as said below
- footprint: bfloat16 [1024, 4, 16384], P('station'), may hold values from -0.03125 to 0.03125
- tile_src: int32 [1024, 4, 1], replicated, may hold values from 0 to 63; in each aligned block of 64 rows (0 to 63, 64 to 127, ..., all dimensions but the last counted through in order) at most 2 rows name the same one
- tile_local: int32 [1024, 4], replicated, may hold values from 0 to 6
- tile_count: int32 [1024], P('station'), may hold values from 1 to 4
Outputs:
- observed: float32 [1024, 16], P('station')
Inputs may be any that keep to these rules, and one draw needn't show every extreme that they name: `tile_src`: in each aligned block of 64 rows (the slots of one index's stations, stations and slots in order), no band appears more than 2 times, and some band appears exactly 2 times. `diff_steps`: some sample takes 6 steps and another takes 3.
All inputs are finite; a program needn't handle non-finite values.
Results may differ from a plain program's by a relative error of at most 0.0029.
Values may be sent and summed in bfloat16 or wider, within the bound.
No kernel may reach another device: no remote copies, remote signals or barrier semaphores. Data moves between devices by JAX's collectives and lax.ppermute only.
A program may use at most 128 MiB of HBM per device.

v0:
```python
import functools

import jax
import jax.numpy as jnp
from jax import lax
from jax.experimental import pallas as pl
from jax.experimental.pallas import tpu as pltpu
from jax.sharding import PartitionSpec as P

TILE_LON = 512
TILES_DEV = 7
KT = 4
ITERS = 6
CAP = 2
HALO = 8
PARTS = 4
CORES = 2
LANES = 128
VMEM = pltpu.VMEM
SMEM = pltpu.SMEM


def spec(space):
    return pl.BlockSpec(memory_space=space)


def pack_kernel(src_ref, prints_ref, sent_ref, place_ref, held_ref, slot_ref):
    slots = prints_ref.shape[0]
    bands = sent_ref.shape[0]

    def clear(i, carry):
        held_ref[i] = 0
        slot_ref[2 * i] = 0
        slot_ref[2 * i + 1] = 0
        return carry

    lax.fori_loop(0, bands, clear, 0, unroll=8)

    def assign(station, carry):
        for k in range(KT):
            band = src_ref[k, station]
            rank = jnp.minimum(held_ref[band], CAP - 1)
            held_ref[band] = rank + 1
            place_ref[KT * station + k] = CAP * band + rank
            slot_ref[CAP * band + rank] = KT * station + k
        return carry

    lax.fori_loop(0, slots // KT, assign, 0)

    def fill(i, carry):
        first = prints_ref[slot_ref[2 * i]]
        second = prints_ref[slot_ref[2 * i + 1]]
        sent_ref[i] = jnp.concatenate([first, second], axis=0)
        return carry

    lax.fori_loop(0, bands, fill, 0, unroll=8)


def edge_kernel(flux_ref, coef_ref, last_ref, first_ref):
    samples, rows, _ = flux_ref.shape
    for ref, low in ((last_ref, rows - HALO), (first_ref, 0)):
        ref[0:samples] = flux_ref[:, low : low + HALO]
        coef = coef_ref[low : low + HALO]
        head = coef.astype(jnp.bfloat16)
        ref[samples] = head
        ref[samples + 1] = (coef - head.astype(jnp.float32)).astype(jnp.bfloat16)


def diffuse_kernel(
    pair, own_ref, steps_ref, flux_ref, above_ref, below_ref, coef_ref,
    out0_ref, out1_ref, out2_ref, out3_ref, even_ref, odd_ref, coefs_ref,
):
    own = own_ref[0]
    samples, rows, lon = flux_ref.shape
    strips = lon // LANES
    tall = rows + 2 * HALO
    edge = jnp.zeros((HALO, LANES), jnp.float32)
    lane = lax.broadcasted_iota(jnp.int32, (8, LANES), 1)
    first_lane = lane == 0
    last_lane = lane == LANES - 1

    for strip in range(strips):
        at = slice(strip * LANES, (strip + 1) * LANES)
        for ref, low in ((above_ref, 0), (below_ref, HALO + rows)):
            coefs_ref[strip, low : low + HALO] = ref[samples, :, at].astype(jnp.float32) + ref[
                samples + 1, :, at
            ].astype(jnp.float32)
        coefs_ref[strip, HALO : HALO + rows] = coef_ref[:, at]
        for low in (0, HALO + tall):
            odd_ref[strip, low : low + HALO] = edge
            for side in range(2):
                even_ref[side, strip, low : low + HALO] = edge

    def update(old_ref, new_ref, tile):
        at = HALO + 8 * tile

        def load(strip):
            return old_ref[strip % strips, at : at + 8]

        before = pltpu.roll(load(strips - 1), 1, 1)
        center = load(0)
        ahead = pltpu.roll(center, LANES - 1, 1)
        for strip in range(strips):
            behind = pltpu.roll(center, 1, 1)
            following = load(strip + 1)
            after = pltpu.roll(following, LANES - 1, 1)
            west = jnp.where(first_lane, before, behind)
            east = jnp.where(last_lane, after, ahead)
            north = old_ref[strip, at - 1 : at + 7]
            south = old_ref[strip, at + 1 : at + 9]
            lap = (north + south + east + west) - 4.0 * center
            new_ref[strip, at : at + 8] = center + coefs_ref[strip, 8 * tile : 8 * tile + 8] * lap
            before, center, ahead = behind, following, after

    def step(old_ref, new_ref, last):
        @pl.when(jnp.logical_not(last))
        def _():
            update(old_ref, new_ref, 0)
            update(old_ref, new_ref, tall // 8 - 1)

        for tile in range(1, tall // 8 - 1):
            update(old_ref, new_ref, tile)

    def begin(sample, ref):
        for strip in range(strips):
            at = slice(strip * LANES, (strip + 1) * LANES)
            ref[strip, HALO : 2 * HALO] = above_ref[sample, :, at].astype(jnp.float32)
            ref[strip, 2 * HALO : 2 * HALO + rows] = flux_ref[sample, :, at].astype(jnp.float32)
            ref[strip, 2 * HALO + rows : HALO + tall] = below_ref[sample, :, at].astype(jnp.float32)

    def evolve(side, carry):
        sample = 2 * pair + side
        even = even_ref.at[side]
        count = jnp.minimum(steps_ref[sample], ITERS)
        half = lax.div(count, 2)

        @pl.when(lax.rem(count, 2) == 1)
        def _():
            begin(sample, odd_ref)
            step(odd_ref, even, half == 0)

        @pl.when(lax.rem(count, 2) == 0)
        def _():
            begin(sample, even)

        def two(k, carry):
            step(even, odd_ref, False)
            step(odd_ref, even, k == half - 1)
            return carry

        lax.fori_loop(0, half, two, 0)
        return carry

    lax.fori_loop(0, 2, evolve, 0)

    for turn, out_ref in enumerate((out0_ref, out1_ref, out2_ref, out3_ref)):
        low = pl.multiple_of(2 * HALO + 8 * lax.rem(own + turn, PARTS), 8)
        for strip in range(strips):
            both = [even_ref[side, strip, pl.ds(low, 8)] for side in range(2)]
            out_ref[:, strip * LANES : (strip + 1) * LANES] = jnp.concatenate(both, axis=0).astype(jnp.bfloat16)


def dots_kernel(own_ref, core_ref, loc_ref, prints_ref, *refs):
    parts = refs[: CORES * PARTS * 2]
    out_ref, sums_ref = refs[CORES * PARTS * 2 :]
    peers, _, width = prints_ref.shape
    core = core_ref[0]
    each = PARTS * 2
    for group in range(CORES):
        side = core if group == 0 else 1 - core
        prints = prints_ref[:, pl.ds(pl.multiple_of(16 * side, 16), 16)].reshape(peers * 16, width)
        for low in range(0, TILES_DEV, 2):
            tiles = range(low, min(low + 2, TILES_DEV))
            cells = jnp.concatenate(
                [
                    part[:, tile * width : (tile + 1) * width]
                    for tile in tiles
                    for part in parts[group * each : (group + 1) * each]
                ],
                axis=0,
            )
            sums = lax.dot_general(prints, cells, (((1,), (1,)), ((), ())), preferred_element_type=jnp.float32)
            for i, tile in enumerate(tiles):
                sums_ref[group, tile] = sums[:, i * LANES : (i + 1) * LANES].reshape(peers, CAP, 8, LANES)
    same = lax.rem(lax.broadcasted_iota(jnp.int32, (8, LANES), 1), 8) == lax.broadcasted_iota(
        jnp.int32, (8, LANES), 0
    )
    shift = 32 * own_ref[0]

    def pick(two, carry):
        rows = []
        for i in range(2):
            peer = 2 * two + i
            for side in range(CORES):
                group = jnp.where(core == side, 0, 1)
                for slot in range(CAP):
                    loc = loc_ref[(peer * CORES + side) * CAP + slot]
                    rows.append(
                        jnp.sum(jnp.where(same, sums_ref[group, loc, peer, slot], 0.0), axis=0, keepdims=True)
                    )
        out_ref[pl.ds(pl.multiple_of(two * 8, 8), 8)] = pltpu.roll(jnp.concatenate(rows, axis=0), shift, 1)
        return carry

    lax.fori_loop(0, peers // 2, pick, 0, unroll=2)


def station_kernel(place_ref, count_ref, back_ref, out_ref, sums_ref):
    stations = sums_ref.shape[0]
    for station in range(stations):
        total = back_ref[pl.ds(place_ref[KT * station], 1)]
        for k in range(1, KT):
            row = back_ref[pl.ds(place_ref[KT * station + k], 1)]
            total = total + jnp.where(k < count_ref[station], row, 0.0)
        sums_ref[station : station + 1] = jnp.where(0 < count_ref[station], total, 0.0)
    lane = lax.broadcasted_iota(jnp.int32, (LANES, 16), 0)
    sample = lax.broadcasted_iota(jnp.int32, (LANES, 16), 1)
    fold = (lax.div(lane, 8) == sample).astype(jnp.float32)
    out_ref[...] = jnp.dot(
        sums_ref[...], fold, precision=lax.Precision.HIGHEST, preferred_element_type=jnp.float32
    )


def body(flux, coeff, diff_steps, footprint, tile_src, tile_local, tile_count):
    samples, rows, lon = flux.shape
    stations = footprint.shape[0]
    slots = stations * KT
    bands = lax.axis_size("station")
    peers = bands // CORES
    band = lax.axis_index("station")
    part = lax.axis_index("sample")
    own = part.astype(jnp.int32).reshape(1)
    cells = rows * TILE_LON // PARTS
    down = [(i, i + 1) for i in range(bands - 1)]
    up = [(i + 1, i) for i in range(bands - 1)]
    beside = [(i, i ^ 1) for i in range(bands)]
    same_core = [[CORES * i + core for i in range(peers)] for core in range(CORES)]

    last, first = pl.pallas_call(
        edge_kernel,
        out_shape=[jax.ShapeDtypeStruct((samples + 2, HALO, lon), jnp.bfloat16)] * 2,
        in_specs=[spec(VMEM)] * 2,
        out_specs=[spec(VMEM)] * 2,
        name="edges",
    )(flux, coeff)
    above = lax.ppermute(last, "station", down)
    below = lax.ppermute(first, "station", up)

    src_all = tile_src[:, :, 0].T
    my_src = lax.dynamic_slice_in_dim(src_all, band * stations, stations, axis=1)
    prints = lax.dynamic_slice_in_dim(footprint, part * cells, cells, axis=2).reshape(slots, 8, TILE_LON)
    sent, place = pl.pallas_call(
        pack_kernel,
        out_shape=(
            jax.ShapeDtypeStruct((bands, 8 * CAP, TILE_LON), jnp.bfloat16),
            jax.ShapeDtypeStruct((slots,), jnp.int32),
        ),
        in_specs=[spec(SMEM), spec(VMEM)],
        out_specs=(spec(VMEM), spec(SMEM)),
        scratch_shapes=[SMEM((bands,), jnp.int32), SMEM((CAP * bands,), jnp.int32)],
        name="pack",
    )(my_src, prints)
    sent, _, _ = lax.optimization_barrier((sent, above, below))
    arrived = lax.all_to_all(
        sent.reshape(peers, CORES * CAP * 8, TILE_LON),
        "station", split_axis=0, concat_axis=0, axis_index_groups=same_core, tiled=True,
    )

    core = lax.rem(band, CORES).astype(jnp.int32)
    mine, theirs = [None] * (2 * PARTS), [None] * (2 * PARTS)
    for pair in range(samples // 2):
        finals = pl.pallas_call(
            functools.partial(diffuse_kernel, pair),
            out_shape=[jax.ShapeDtypeStruct((16, lon), jnp.bfloat16)] * PARTS,
            in_specs=[spec(SMEM), spec(SMEM)] + [spec(VMEM)] * 4,
            out_specs=[spec(VMEM)] * PARTS,
            scratch_shapes=[
                VMEM((2, lon // LANES, rows + 4 * HALO, LANES), jnp.float32),
                VMEM((lon // LANES, rows + 4 * HALO, LANES), jnp.float32),
                VMEM((lon // LANES, rows + 2 * HALO, LANES), jnp.float32),
            ],
            compiler_params=pltpu.CompilerParams(vmem_limit_bytes=24 * 2**20),
            name="diffuse",
        )(own, diff_steps, flux, above, below, coeff)
        for j in range(PARTS):
            turn = (PARTS - j) % PARTS
            part_j = finals[0]
            if turn:
                part_j = lax.ppermute(finals[turn], "sample", [(i, (i + turn) % PARTS) for i in range(PARTS)])
            mine[2 * j + pair] = part_j
            theirs[2 * j + pair] = lax.ppermute(part_j, "station", beside)

    order = jnp.arange(stations * bands, dtype=jnp.int32) % stations
    code = (order[None, :] * KT + jnp.arange(KT, dtype=jnp.int32)[:, None]) * 8 + tile_local.T
    picks = []
    for side in range(CORES):
        named = src_all == (band - core + side)
        first = jnp.min(jnp.min(jnp.where(named, code, slots * 8), axis=0).reshape(bands, stations), axis=1)
        last = jnp.max(jnp.max(jnp.where(named, code, 0), axis=0).reshape(bands, stations), axis=1)
        picks += [first & 7, last & 7]
    loc = lax.dynamic_index_in_dim(jnp.stack(picks, axis=1).reshape(peers, CORES, CORES * CAP), core, 1, keepdims=False)

    values = pl.pallas_call(
        dots_kernel,
        out_shape=jax.ShapeDtypeStruct((bands * CAP, LANES), jnp.float32),
        in_specs=[spec(SMEM)] * 3 + [spec(VMEM)] * (1 + 2 * CORES * PARTS),
        out_specs=spec(VMEM),
        scratch_shapes=[VMEM((CORES, TILES_DEV, peers, CAP, 8, LANES), jnp.float32)],
        compiler_params=pltpu.CompilerParams(vmem_limit_bytes=24 * 2**20),
        name="dots",
    )(own, core.reshape(1), loc.reshape(-1), arrived, *mine, *theirs)

    back = lax.all_to_all(
        values.reshape(peers, CORES * CAP, LANES),
        "station", split_axis=0, concat_axis=0, axis_index_groups=same_core, tiled=True,
    )
    share = pl.pallas_call(
        station_kernel,
        out_shape=jax.ShapeDtypeStruct((stations, 16), jnp.float32),
        in_specs=[spec(SMEM), spec(SMEM), spec(VMEM)],
        out_specs=spec(VMEM),
        scratch_shapes=[VMEM((stations, LANES), jnp.float32)],
        name="stations",
    )(place, tile_count, back.reshape(bands * CAP, LANES))
    others = [lax.ppermute(share, "sample", [(i, i ^ flip) for i in range(PARTS)]) for flip in (1, 2, 3)]
    return (share + others[0]) + (others[1] + others[2])


def solution(mesh):
    in_specs = (
        P("sample", "station", None),
        P("station", None),
        P("sample"),
        P("station", None, None),
        P(),
        P(),
        P("station"),
    )
    return jax.shard_map(body, mesh=mesh, in_specs=in_specs, out_specs=P("station", None), check_vma=False)
```

profile of v0, /device:TPU:8, one launch (start us, length us, event | category | flops | bytes accessed | tf_op | source)
XLA Modules:
  0.0 93.8 jit_solution(10553705578734069432)
XLA Ops:
  0.0 2.3 %edges.1 = (bf16[6,8,3584]{2,1,0:T(8,128)(2,1)}, bf16[6,8,3584]{2,1,0:T(8,128)(2,1)}) custom-call(bf16[4,32,3584]{2,1,0:T(8,128)(2,1)} %flux_ref.5, f32[32,3584]{1,0:T(8,128)} %coef_ref.5), custom_call_target="tpu_custom_call" | custom-call | tf_op jit(solution)/shard_map/edges/pallas_call | solution.py:238
  2.4 2.5 %collective-permute-start = (bf16[6,8,3584]{2,1,0:T(8,128)(2,1)}, bf16[6,8,3584]{2,1,0:T(8,128)(2,1)}, u32[]{:S(2)}, u32[]{:S(2)}) collective-permute-start(bf16[6,8,3584]{2,1,0:T(8,128)(2,1)} %get-tuple-element.20), channel_id=1, source_target_pairs={{0,4},{4,8},{8,12},{12,16},{16,20},{20,24},{24,28},{28,32},{32,36}... | collective-permute-start | bytes 1032200 | tf_op jit(solution)/shard_map/ppermute | solution.py:245
  4.8 1.3 %collective-permute-start.1 = (bf16[6,8,3584]{2,1,0:T(8,128)(2,1)}, bf16[6,8,3584]{2,1,0:T(8,128)(2,1)}, u32[]{:S(2)}, u32[]{:S(2)}) collective-permute-start(bf16[6,8,3584]{2,1,0:T(8,128)(2,1)} %get-tuple-element.21), channel_id=1, source_target_pairs={{4,0},{8,4},{12,8},{16,12},{20,16},{24,20},{28,24},{32,28},{36,32}... | collective-permute-start | bytes 1032200 | tf_op jit(solution)/shard_map/ppermute | solution.py:246
  6.1 1.0 %constant_dynamic-slice_fusion = bf16[16,4,4096]{2,1,0:T(4,128)(2,1)} fusion(bf16[16,4,16384]{2,1,0:T(4,128)(2,1)S(1)} %copy-done, s32[]{:T(128)S(6)} %select_n.35), kind=kLoop, calls=%fused_computation.21 | loop fusion | bytes 1048580 | tf_op jit(solution)/shard_map/dynamic_slice | solution.py:250
  7.1 2.3 %reshape.110.prints_ref = bf16[64,8,512]{2,1,0:T(8,128)(2,1)} reshape(bf16[16,4,4096]{2,1,0:T(4,128)(2,1)} %constant_dynamic-slice_fusion) | data formatting | bytes 1048576 | tf_op jit(solution)/shard_map/reshape | solution.py:250
  9.4 0.7 constant_dynamic-slice_fusion.1
  10.1 2.9 %pack.1 = (bf16[64,16,512]{2,1,0:T(8,128)(2,1)}, s32[64]{0:T(128)}) custom-call(s32[4,16]{1,0:T(4,128)} %bitcast.33, bf16[64,8,512]{2,1,0:T(8,128)(2,1)} %reshape.110.prints_ref), custom_call_target="tpu_custom_call" | custom-call | tf_op jit(solution)/shard_map/pack/pallas_call | solution.py:251
  13.0 0.0 collective-permute-done.1.below_ref
  13.0 14.5 %all-to-all-start = ((bf16[32,32,512]{2,1,0:T(8,128)(2,1)}), bf16[32,32,512]{2,1,0:T(8,128)(2,1)}, u32[]{:S(2)}, u32[]{:S(2)}) async-start(bf16[32,32,512]{2,1,0:T(8,128)(2,1)} %bitcast.31), calls=%async_computation | async-start | bytes 2097152 | tf_op jit(solution)/shard_map/all_to_all | solution.py:263
  27.5 0.1 select_reduce_fusion
  27.6 0.1 reshape.116
  27.7 0.7 reshape.115
  28.4 0.1 reshape.113
  28.4 0.9 reduce_min.39
  29.3 0.1 reduce_min.37
  29.4 0.1 reshape.114
  29.5 0.1 reduce_max.39
  29.6 0.1 reduce_max.37
  29.8 6.3 %diffuse.3 = (bf16[16,3584]{1,0:T(8,128)(2,1)S(1)}, bf16[16,3584]{1,0:T(8,128)(2,1)S(1)}, bf16[16,3584]{1,0:T(8,128)(2,1)S(1)}, bf16[16,3584]{1,0:T(8,128)(2,1)S(1)}) custom-call(s32[1]{0:T(128)} %bitcast.2.own_ref, s32[4]{0:T(128)S(1)} %copy-done.9, bf16[4,32,3584]{2,1,0:T(8,128)(2,1)S(1)} %copy-done.1, bf16[6,8,3584]{2,1,0:T(8,128)(2,1)} %collective-permute-done.above_ref, ...), custom_call_target="tpu_custom_call" | custom-call | tf_op jit(solution)/shard_map/diffuse/pallas_call | solution.py:271
  36.1 0.1 collective-permute-start.3
  36.2 2.4 %collective-permute-start.5 = (bf16[16,3584]{1,0:T(8,128)(2,1)S(1)}, bf16[16,3584]{1,0:T(8,128)(2,1)}, u32[]{:S(2)}, u32[]{:S(2)}) collective-permute-start(bf16[16,3584]{1,0:T(8,128)(2,1)S(1)} %get-tuple-element.28), channel_id=1, source_target_pairs={{0,2},{1,3},{2,0},{3,1},{4,6},{5,7},{6,4},{7,5},{8,10},{9,11},{10,... | collective-permute-start | bytes 344072 | tf_op jit(solution)/shard_map/ppermute | solution.py:288
  38.6 2.5 %collective-permute-start.7 = (bf16[16,3584]{1,0:T(8,128)(2,1)S(1)}, bf16[16,3584]{1,0:T(8,128)(2,1)}, u32[]{:S(2)}, u32[]{:S(2)}) collective-permute-start(bf16[16,3584]{1,0:T(8,128)(2,1)S(1)} %get-tuple-element.30), channel_id=1, source_target_pairs={{0,1},{1,2},{2,3},{3,0},{4,5},{5,6},{6,7},{7,4},{8,9},{9,10},{10,1... | collective-permute-start | bytes 344072 | tf_op jit(solution)/shard_map/ppermute | solution.py:288
  41.1 5.8 %diffuse.2 = (bf16[16,3584]{1,0:T(8,128)(2,1)S(1)}, bf16[16,3584]{1,0:T(8,128)(2,1)S(1)}, bf16[16,3584]{1,0:T(8,128)(2,1)S(1)}, bf16[16,3584]{1,0:T(8,128)(2,1)S(1)}) custom-call(s32[1]{0:T(128)} %bitcast.2.own_ref, s32[4]{0:T(128)S(1)} %copy-done.9, bf16[4,32,3584]{2,1,0:T(8,128)(2,1)S(1)} %copy-done.1, bf16[6,8,3584]{2,1,0:T(8,128)(2,1)} %collective-permute-done.above_ref, ...), custom_call_target="tpu_custom_call" | custom-call | tf_op jit(solution)/shard_map/diffuse/pallas_call | solution.py:271
  46.9 0.1 collective-permute-start.2
  47.0 0.5 collective-permute-start.4
  47.5 0.0 collective-permute-done.3.refs_3_
  47.5 2.5 %collective-permute-start.6 = (bf16[16,3584]{1,0:T(8,128)(2,1)S(1)}, bf16[16,3584]{1,0:T(8,128)(2,1)S(1)}, u32[]{:S(2)}, u32[]{:S(2)}) collective-permute-start(bf16[16,3584]{1,0:T(8,128)(2,1)S(1)} %get-tuple-element.29), channel_id=1, source_target_pairs={{0,1},{1,2},{2,3},{3,0},{4,5},{5,6},{6,7},{7,4},{8,9},{9,10},{10,1... | collective-permute-start | bytes 344072 | tf_op jit(solution)/shard_map/ppermute | solution.py:288
  50.0 0.0 collective-permute-start.9
  50.0 0.5 collective-permute-start.8
  50.5 0.6 copy-done.7
  51.1 2.3 %collective-permute-done.2.refs_2_ = bf16[16,3584]{1,0:T(8,128)(2,1)S(1)} collective-permute-done((bf16[16,3584]{1,0:T(8,128)(2,1)S(1)}, bf16[16,3584]{1,0:T(8,128)(2,1)S(1)}, u32[]{:S(2)}, u32[]{:S(2)}) %collective-permute-start.2) | collective-permute-done | bytes 114720 | tf_op jit(solution)/shard_map/ppermute | solution.py:288
  53.5 0.0 collective-permute-start.11
  53.5 0.6 copy-done.5
  54.1 0.0 collective-permute-done.4.refs_4_
  54.1 0.5 collective-permute-start.13
  54.6 0.5 collective-permute-done.6.refs_6_
  55.1 0.0 collective-permute-start.15
  55.1 0.0 collective-permute-done.9.refs_9_
  55.1 0.5 collective-permute-start.10
  55.6 0.0 collective-permute-done.8.refs_8_
  55.6 0.1 collective-permute-start.12
  55.7 0.4 collective-permute-start.14
  56.1 0.1 and.79
  56.2 0.1 copy.19
  56.3 0.1 and.77
  56.4 0.1 copy.18
  56.5 0.1 and.73
  56.6 0.1 copy.16
  56.7 0.1 and.75
  56.8 0.1 copy.17
  56.9 0.1 copy.20
  57.0 0.1 reshape.117.loc_ref
  57.2 0.9 copy-done.4
  58.1 0.9 copy-done.6
  59.0 0.9 copy-done.8
  59.9 3.4 %dots.1 = f32[128,128]{1,0:T(8,128)S(1)} custom-call(s32[1]{0:T(128)} %bitcast.2.own_ref, s32[1]{0:T(128)} %bitcast.3.core_ref, s32[128]{0:T(128)S(1)} %reshape.117.loc_ref, bf16[32,32,512]{2,1,0:T(8,128)(2,1)} %all-to-all-done.prints_ref, bf16[16,3584]{1,0:T(8,128)(2,1)S(1)} %copy-done.8, bf16[16,3584]{1,0:T(8,128)(2,1)S(1)} %copy-done.4, ...), custom_call_target="tpu_custom_call" | custom-call | tf_op jit(solution)/shard_map/dots/pallas_call | solution.py:302
  63.3 19.6 %all_to_all.10 = f32[32,4,128]{2,1,0:T(4,128)} all-to-all(f32[32,4,128]{2,1,0:T(4,128)S(1)} %bitcast.30), channel_id=1, replica_groups={{0,8,16,24,32,40,48,56,64,72,80,88,96,104,112,120,128,136,144,152,160,1..., dimensions={0} | all-to-all | bytes 131072 | tf_op jit(solution)/shard_map/all_to_all | solution.py:312
  82.9 1.7 %stations.1 = f32[16,16]{1,0:T(8,128)} custom-call(s32[64]{0:T(128)} %get-tuple-element.18.place_ref, s32[16]{0:T(128)} %count_ref.1, f32[128,128]{1,0:T(8,128)} %bitcast.32), custom_call_target="tpu_custom_call" | custom-call | tf_op jit(solution)/shard_map/stations/pallas_call | solution.py:316
  84.6 0.9 collective-permute-start.18
  85.5 3.1 %collective-permute-start.17 = (f32[16,16]{1,0:T(8,128)}, f32[16,16]{1,0:T(8,128)S(1)}, u32[]{:S(2)}, u32[]{:S(2)}) collective-permute-start(f32[16,16]{1,0:T(8,128)} %stations.1), channel_id=1, source_target_pairs={{0,2},{1,3},{2,0},{3,1},{4,6},{5,7},{6,4},{7,5},{8,10},{9,11},{10,... | collective-permute-start | bytes 3080 | tf_op jit(solution)/shard_map/ppermute | solution.py:324
  88.7 0.1 collective-permute-start.16
  88.7 2.2 %collective-permute-done.17 = f32[16,16]{1,0:T(8,128)S(1)} collective-permute-done((f32[16,16]{1,0:T(8,128)}, f32[16,16]{1,0:T(8,128)S(1)}, u32[]{:S(2)}, u32[]{:S(2)}) %collective-permute-start.17) | collective-permute-done | bytes 1056 | tf_op jit(solution)/shard_map/ppermute | solution.py:324
  90.9 1.6 %collective-permute-done.16 = f32[16,16]{1,0:T(8,128)S(1)} collective-permute-done((f32[16,16]{1,0:T(8,128)}, f32[16,16]{1,0:T(8,128)S(1)}, u32[]{:S(2)}, u32[]{:S(2)}) %collective-permute-start.16) | collective-permute-done | bytes 1056 | tf_op jit(solution)/shard_map/ppermute | solution.py:324
  92.5 1.3 %add_add_fusion = f32[16,16]{1,0:T(8,128)} fusion(f32[16,16]{1,0:T(8,128)S(1)} %collective-permute-done.17, f32[16,16]{1,0:T(8,128)S(1)} %collective-permute-done.18, f32[16,16]{1,0:T(8,128)} %stations.1, f32[16,16]{1,0:T(8,128)S(1)} %collective-permute-done.16), kind=kLoop, calls=%fused_computation.7 | loop fusion | flops 768 | bytes 5120 | tf_op jit(solution)/shard_map/add | solution.py:325
  (37 shorter events, 0.1 us)
Async XLA Ops:
  0.0 6.1 %copy-start = (bf16[16,4,16384]{2,1,0:T(4,128)(2,1)S(1)}, bf16[16,4,16384]{2,1,0:T(4,128)(2,1)}, u32[]{:S(2)}) copy-start(bf16[16,4,16384]{2,1,0:T(4,128)(2,1)} %param.10) | copy-start | bytes 6291460
  0.0 9.4 %copy-start.10 = (s32[1024,4,1]{0,2,1:T(1,128)S(1)}, s32[1024,4,1]{0,2,1:T(1,128)}, u32[]{:S(2)}) copy-start(s32[1024,4,1]{0,2,1:T(1,128)} %param.11) | copy-start | bytes 49156
  2.4 10.6 %collective-permute-start = (bf16[6,8,3584]{2,1,0:T(8,128)(2,1)}, bf16[6,8,3584]{2,1,0:T(8,128)(2,1)}, u32[]{:S(2)}, u32[]{:S(2)}) collective-permute-start(bf16[6,8,3584]{2,1,0:T(8,128)(2,1)} %get-tuple-element.20), channel_id=1, source_target_pairs={{0,4},{4,8},{8,12},{12,16},{16,20},{20,24},{24,28},{28,32},{32,36}... | collective-permute-start | bytes 1032200 | tf_op jit(solution)/shard_map/ppermute | solution.py:245
  4.8 8.2 %collective-permute-start.1 = (bf16[6,8,3584]{2,1,0:T(8,128)(2,1)}, bf16[6,8,3584]{2,1,0:T(8,128)(2,1)}, u32[]{:S(2)}, u32[]{:S(2)}) collective-permute-start(bf16[6,8,3584]{2,1,0:T(8,128)(2,1)} %get-tuple-element.21), channel_id=1, source_target_pairs={{4,0},{8,4},{12,8},{16,12},{20,16},{24,20},{28,24},{32,28},{36,32}... | collective-permute-start | bytes 1032200 | tf_op jit(solution)/shard_map/ppermute | solution.py:246
  7.1 20.4 %copy-start.11 = (s32[1024,4]{0,1:T(4,128)S(1)}, s32[1024,4]{0,1:T(4,128)}, u32[]{:S(2)}) copy-start(s32[1024,4]{0,1:T(4,128)} %param.12) | copy-start | bytes 49156
  7.1 22.6 %copy-start.1 = (bf16[4,32,3584]{2,1,0:T(8,128)(2,1)S(1)}, bf16[4,32,3584]{2,1,0:T(8,128)(2,1)}, u32[]{:S(2)}) copy-start(bf16[4,32,3584]{2,1,0:T(8,128)(2,1)} %flux_ref.5) | copy-start | bytes 2752516
  7.1 22.6 %copy-start.2 = (f32[32,3584]{1,0:T(8,128)S(1)}, f32[32,3584]{1,0:T(8,128)}, u32[]{:S(2)}) copy-start(f32[32,3584]{1,0:T(8,128)} %coef_ref.5) | copy-start | bytes 1376260
  7.1 22.6 %copy-start.9 = (s32[4]{0:T(128)S(1)}, s32[4]{0:T(128)}, u32[]{:S(2)}) copy-start(s32[4]{0:T(128)} %steps_ref.3) | copy-start | bytes 52
  13.0 44.2 %all-to-all-start = ((bf16[32,32,512]{2,1,0:T(8,128)(2,1)}), bf16[32,32,512]{2,1,0:T(8,128)(2,1)}, u32[]{:S(2)}, u32[]{:S(2)}) async-start(bf16[32,32,512]{2,1,0:T(8,128)(2,1)} %bitcast.31), calls=%async_computation | async-start | bytes 2097152 | tf_op jit(solution)/shard_map/all_to_all | solution.py:263
  36.1 13.9 %copy-start.3 = (bf16[16,3584]{1,0:T(8,128)(2,1)}, bf16[16,3584]{1,0:T(8,128)(2,1)S(1)}, u32[]{:S(2)}) copy-start(bf16[16,3584]{1,0:T(8,128)(2,1)S(1)} %get-tuple-element.24.refs_1_) | copy-start | bytes 344068
  36.1 11.4 %collective-permute-start.3 = (bf16[16,3584]{1,0:T(8,128)(2,1)S(1)}, bf16[16,3584]{1,0:T(8,128)(2,1)S(1)}, u32[]{:S(2)}, u32[]{:S(2)}) collective-permute-start(bf16[16,3584]{1,0:T(8,128)(2,1)S(1)} %get-tuple-element.26), channel_id=1, source_target_pairs={{0,3},{1,0},{2,1},{3,2},{4,7},{5,4},{6,5},{7,6},{8,11},{9,8},{10,9... | collective-permute-start | bytes 344072 | tf_op jit(solution)/shard_map/ppermute | solution.py:288
  36.2 13.8 %collective-permute-start.5 = (bf16[16,3584]{1,0:T(8,128)(2,1)S(1)}, bf16[16,3584]{1,0:T(8,128)(2,1)}, u32[]{:S(2)}, u32[]{:S(2)}) collective-permute-start(bf16[16,3584]{1,0:T(8,128)(2,1)S(1)} %get-tuple-element.28), channel_id=1, source_target_pairs={{0,2},{1,3},{2,0},{3,1},{4,6},{5,7},{6,4},{7,5},{8,10},{9,11},{10,... | collective-permute-start | bytes 344072 | tf_op jit(solution)/shard_map/ppermute | solution.py:288
  38.6 11.4 %collective-permute-start.7 = (bf16[16,3584]{1,0:T(8,128)(2,1)S(1)}, bf16[16,3584]{1,0:T(8,128)(2,1)}, u32[]{:S(2)}, u32[]{:S(2)}) collective-permute-start(bf16[16,3584]{1,0:T(8,128)(2,1)S(1)} %get-tuple-element.30), channel_id=1, source_target_pairs={{0,1},{1,2},{2,3},{3,0},{4,5},{5,6},{6,7},{7,4},{8,9},{9,10},{10,1... | collective-permute-start | bytes 344072 | tf_op jit(solution)/shard_map/ppermute | solution.py:288
  46.9 6.6 %collective-permute-start.2 = (bf16[16,3584]{1,0:T(8,128)(2,1)S(1)}, bf16[16,3584]{1,0:T(8,128)(2,1)S(1)}, u32[]{:S(2)}, u32[]{:S(2)}) collective-permute-start(bf16[16,3584]{1,0:T(8,128)(2,1)S(1)} %get-tuple-element.25), channel_id=1, source_target_pairs={{0,3},{1,0},{2,1},{3,2},{4,7},{5,4},{6,5},{7,6},{8,11},{9,8},{10,9... | collective-permute-start | bytes 344072 | tf_op jit(solution)/shard_map/ppermute | solution.py:288
  47.0 7.1 %collective-permute-start.4 = (bf16[16,3584]{1,0:T(8,128)(2,1)S(1)}, bf16[16,3584]{1,0:T(8,128)(2,1)S(1)}, u32[]{:S(2)}, u32[]{:S(2)}) collective-permute-start(bf16[16,3584]{1,0:T(8,128)(2,1)S(1)} %get-tuple-element.27), channel_id=1, source_target_pairs={{0,2},{1,3},{2,0},{3,1},{4,6},{5,7},{6,4},{7,5},{8,10},{9,11},{10,... | collective-permute-start | bytes 344072 | tf_op jit(solution)/shard_map/ppermute | solution.py:288
  47.5 7.6 %collective-permute-start.6 = (bf16[16,3584]{1,0:T(8,128)(2,1)S(1)}, bf16[16,3584]{1,0:T(8,128)(2,1)S(1)}, u32[]{:S(2)}, u32[]{:S(2)}) collective-permute-start(bf16[16,3584]{1,0:T(8,128)(2,1)S(1)} %get-tuple-element.29), channel_id=1, source_target_pairs={{0,1},{1,2},{2,3},{3,0},{4,5},{5,6},{6,7},{7,4},{8,9},{9,10},{10,1... | collective-permute-start | bytes 344072 | tf_op jit(solution)/shard_map/ppermute | solution.py:288
  50.0 5.1 %collective-permute-start.9 = (bf16[16,3584]{1,0:T(8,128)(2,1)S(1)}, bf16[16,3584]{1,0:T(8,128)(2,1)S(1)}, u32[]{:S(2)}, u32[]{:S(2)}) collective-permute-start(bf16[16,3584]{1,0:T(8,128)(2,1)S(1)} %get-tuple-element.24.refs_1_), channel_id=1, source_target_pairs={{0,4},{4,0},{8,12},{12,8},{16,20},{20,16},{24,28},{28,24},{32,36},... | collective-permute-start | bytes 344072 | tf_op jit(solution)/shard_map/ppermute | solution.py:290
  50.0 5.6 %collective-permute-start.8 = (bf16[16,3584]{1,0:T(8,128)(2,1)S(1)}, bf16[16,3584]{1,0:T(8,128)(2,1)S(1)}, u32[]{:S(2)}, u32[]{:S(2)}) collective-permute-start(bf16[16,3584]{1,0:T(8,128)(2,1)S(1)} %get-tuple-element.23.refs_0_), channel_id=1, source_target_pairs={{0,4},{4,0},{8,12},{12,8},{16,20},{20,16},{24,28},{28,24},{32,36},... | collective-permute-start | bytes 344072 | tf_op jit(solution)/shard_map/ppermute | solution.py:290
  50.5 0.6 copy-start.7
  53.5 2.2 %collective-permute-start.11 = (bf16[16,3584]{1,0:T(8,128)(2,1)S(1)}, bf16[16,3584]{1,0:T(8,128)(2,1)S(1)}, u32[]{:S(2)}, u32[]{:S(2)}) collective-permute-start(bf16[16,3584]{1,0:T(8,128)(2,1)S(1)} %collective-permute-done.3.refs_3_), channel_id=1, source_target_pairs={{0,4},{4,0},{8,12},{12,8},{16,20},{20,16},{24,28},{28,24},{32,36},... | collective-permute-start | bytes 344072 | tf_op jit(solution)/shard_map/ppermute | solution.py:290
  53.5 0.6 copy-start.5
  54.1 3.0 %collective-permute-start.13 = (bf16[16,3584]{1,0:T(8,128)(2,1)}, bf16[16,3584]{1,0:T(8,128)(2,1)S(1)}, u32[]{:S(2)}, u32[]{:S(2)}) collective-permute-start(bf16[16,3584]{1,0:T(8,128)(2,1)} %collective-permute-done.5.refs_5_), channel_id=1, source_target_pairs={{0,4},{4,0},{8,12},{12,8},{16,20},{20,16},{24,28},{28,24},{32,36},... | collective-permute-start | bytes 344072 | tf_op jit(solution)/shard_map/ppermute | solution.py:290
  55.1 2.0 %collective-permute-start.15 = (bf16[16,3584]{1,0:T(8,128)(2,1)}, bf16[16,3584]{1,0:T(8,128)(2,1)S(1)}, u32[]{:S(2)}, u32[]{:S(2)}) collective-permute-start(bf16[16,3584]{1,0:T(8,128)(2,1)} %collective-permute-done.7.refs_7_), channel_id=1, source_target_pairs={{0,4},{4,0},{8,12},{12,8},{16,20},{20,16},{24,28},{28,24},{32,36},... | collective-permute-start | bytes 344072 | tf_op jit(solution)/shard_map/ppermute | solution.py:290
  55.1 2.0 %collective-permute-start.10 = (bf16[16,3584]{1,0:T(8,128)(2,1)S(1)}, bf16[16,3584]{1,0:T(8,128)(2,1)S(1)}, u32[]{:S(2)}, u32[]{:S(2)}) collective-permute-start(bf16[16,3584]{1,0:T(8,128)(2,1)S(1)} %collective-permute-done.2.refs_2_), channel_id=1, source_target_pairs={{0,4},{4,0},{8,12},{12,8},{16,20},{20,16},{24,28},{28,24},{32,36},... | collective-permute-start | bytes 344072 | tf_op jit(solution)/shard_map/ppermute | solution.py:290
  55.6 1.5 %collective-permute-start.12 = (bf16[16,3584]{1,0:T(8,128)(2,1)S(1)}, bf16[16,3584]{1,0:T(8,128)(2,1)S(1)}, u32[]{:S(2)}, u32[]{:S(2)}) collective-permute-start(bf16[16,3584]{1,0:T(8,128)(2,1)S(1)} %collective-permute-done.4.refs_4_), channel_id=1, source_target_pairs={{0,4},{4,0},{8,12},{12,8},{16,20},{20,16},{24,28},{28,24},{32,36},... | collective-permute-start | bytes 344072 | tf_op jit(solution)/shard_map/ppermute | solution.py:290
  55.7 1.4 %collective-permute-start.14 = (bf16[16,3584]{1,0:T(8,128)(2,1)S(1)}, bf16[16,3584]{1,0:T(8,128)(2,1)S(1)}, u32[]{:S(2)}, u32[]{:S(2)}) collective-permute-start(bf16[16,3584]{1,0:T(8,128)(2,1)S(1)} %collective-permute-done.6.refs_6_), channel_id=1, source_target_pairs={{0,4},{4,0},{8,12},{12,8},{16,20},{20,16},{24,28},{28,24},{32,36},... | collective-permute-start | bytes 344072 | tf_op jit(solution)/shard_map/ppermute | solution.py:290
  57.2 0.9 copy-start.4
  58.1 0.9 copy-start.6
  59.0 0.9 copy-start.8
  84.6 4.1 %collective-permute-start.18 = (f32[16,16]{1,0:T(8,128)}, f32[16,16]{1,0:T(8,128)S(1)}, u32[]{:S(2)}, u32[]{:S(2)}) collective-permute-start(f32[16,16]{1,0:T(8,128)} %stations.1), channel_id=1, source_target_pairs={{0,3},{1,2},{2,1},{3,0},{4,7},{5,6},{6,5},{7,4},{8,11},{9,10},{10,... | collective-permute-start | bytes 3080 | tf_op jit(solution)/shard_map/ppermute | solution.py:324
  85.5 5.4 %collective-permute-start.17 = (f32[16,16]{1,0:T(8,128)}, f32[16,16]{1,0:T(8,128)S(1)}, u32[]{:S(2)}, u32[]{:S(2)}) collective-permute-start(f32[16,16]{1,0:T(8,128)} %stations.1), channel_id=1, source_target_pairs={{0,2},{1,3},{2,0},{3,1},{4,6},{5,7},{6,4},{7,5},{8,10},{9,11},{10,... | collective-permute-start | bytes 3080 | tf_op jit(solution)/shard_map/ppermute | solution.py:324
  88.7 3.9 %collective-permute-start.16 = (f32[16,16]{1,0:T(8,128)}, f32[16,16]{1,0:T(8,128)S(1)}, u32[]{:S(2)}, u32[]{:S(2)}) collective-permute-start(f32[16,16]{1,0:T(8,128)} %stations.1), channel_id=1, source_target_pairs={{0,1},{1,0},{2,3},{3,2},{4,5},{5,4},{6,7},{7,6},{8,9},{9,8},{10,11... | collective-permute-start | bytes 3080 | tf_op jit(solution)/shard_map/ppermute | solution.py:324
where the time goes:
time: 93.9 us; the launch traced here: 93.8 us
  starting transfers between devices  32.4 us (35%)
  Pallas kernels  22.4 us (24%)
  blocking collectives  19.6 us (21%)
  local copies, waits for them, and re-layouts  9.77 us (10%)
  waiting for transfers between devices  6.62 us (7%)
  other arithmetic  2.64 us (3%)
    all_to_all x1, blocking collectives, body(): lax.all_to_all(values.reshape(peers, CORES * CAP, LANES), 'station', spli...  19.6 us
    all_to_all x1, starting transfers between devices, body(): lax.all_to_all(sent.reshape(peers, CORES * CAP * 8, TILE_LON), 'station',...  14.5 us
    pallas_call x2, Pallas kernels, body(): pl.pallas_call(functools.partial(diffuse_kernel, pair), out_shape=[jax.Sh...  12.1 us
    ppermute x6, starting transfers between devices, body(): lax.ppermute(finals[turn], 'sample', [(i, (i + turn) % PARTS) for i in ra...  8.08 us
    ppermute x3, starting transfers between devices, body(): lax.ppermute(share, 'sample', [(i, i ^ flip) for i in range(PARTS)])  4.09 us
    unnamed x24, local copies, waits for them, and re-layouts  4 us
    ppermute x3, waiting for transfers between devices, body(): lax.ppermute(share, 'sample', [(i, i ^ flip) for i in range(PARTS)])  3.8 us
    pallas_call x1, Pallas kernels, body(): pl.pallas_call(dots_kernel, out_shape=jax.ShapeDtypeStruct((bands * CAP,...  3.44 us
  transfers between devices with their start and end apart: 20, of which 4 were waited for; matrix products, arithmetic and copies ran while one was open for 8% of the time, Pallas kernels for 16%

commit v1 on v0

--- a/solution.py
+++ b/solution.py
@@ -14,7 +14,6 @@
 CAP = 2
 HALO = 8
 PARTS = 4
-CORES = 2
 LANES = 128
 VMEM = pltpu.VMEM
 SMEM = pltpu.SMEM
@@ -24,14 +23,15 @@
     return pl.BlockSpec(memory_space=space)
 
 
-def pack_kernel(src_ref, prints_ref, sent_ref, place_ref, held_ref, slot_ref):
-    slots = prints_ref.shape[0]
-    bands = sent_ref.shape[0]
+def pack_kernel(part_ref, src_ref, prints_ref, sent_ref, place_ref, held_ref, slot_ref, hot_ref):
+    bands, _, width = sent_ref.shape
+    stations = prints_ref.shape[0]
+    slots = stations * KT
 
     def clear(i, carry):
         held_ref[i] = 0
-        slot_ref[2 * i] = 0
-        slot_ref[2 * i + 1] = 0
+        for rank in range(CAP):
+            slot_ref[CAP * i + rank] = -(1 << 20)
         return carry
 
     lax.fori_loop(0, bands, clear, 0, unroll=8)
@@ -45,15 +45,25 @@
             slot_ref[CAP * band + rank] = KT * station + k
         return carry
 
-    lax.fori_loop(0, slots // KT, assign, 0)
-
-    def fill(i, carry):
-        first = prints_ref[slot_ref[2 * i]]
-        second = prints_ref[slot_ref[2 * i + 1]]
-        sent_ref[i] = jnp.concatenate([first, second], axis=0)
-        return carry
-
-    lax.fori_loop(0, bands, fill, 0, unroll=8)
+    lax.fori_loop(0, stations, assign, 0)
+
+    row = lax.broadcasted_iota(jnp.int32, (8, width), 0)
+    offset = lax.broadcasted_iota(jnp.int32, (8, width), 1) - slots * row
+
+    def heat(i, carry):
+        rows = [jnp.where(offset == slot_ref[CAP * i + rank], 1.0, 0.0) for rank in range(CAP)]
+        hot_ref[i] = jnp.concatenate(rows, axis=0).astype(jnp.bfloat16)
+        return carry
+
+    lax.fori_loop(0, bands, heat, 0, unroll=8)
+
+    flat = prints_ref[...].reshape(slots, 8 * width)
+    cells = jnp.concatenate([flat[:, r * width : (r + 1) * width] for r in range(8)], axis=0)
+    some = bands // 4
+    for low in range(0, bands, some):
+        hot = hot_ref[low : low + some].reshape(some * 16, slots * 8)
+        moved = jnp.dot(hot, cells, preferred_element_type=jnp.float32).astype(jnp.bfloat16)
+        sent_ref[low : low + some] = moved.reshape(some, 16, width)
 
 
 def edge_kernel(flux_ref, coef_ref, last_ref, first_ref):
@@ -160,48 +170,34 @@
             out_ref[:, strip * LANES : (strip + 1) * LANES] = jnp.concatenate(both, axis=0).astype(jnp.bfloat16)
 
 
-def dots_kernel(own_ref, core_ref, loc_ref, prints_ref, *refs):
-    parts = refs[: CORES * PARTS * 2]
-    out_ref, sums_ref = refs[CORES * PARTS * 2 :]
+def dots_kernel(own_ref, loc_ref, prints_ref, *refs):
+    parts = refs[: PARTS * 2]
+    out_ref, sums_ref = refs[PARTS * 2 :]
     peers, _, width = prints_ref.shape
-    core = core_ref[0]
-    each = PARTS * 2
-    for group in range(CORES):
-        side = core if group == 0 else 1 - core
-        prints = prints_ref[:, pl.ds(pl.multiple_of(16 * side, 16), 16)].reshape(peers * 16, width)
-        for low in range(0, TILES_DEV, 2):
-            tiles = range(low, min(low + 2, TILES_DEV))
-            cells = jnp.concatenate(
-                [
-                    part[:, tile * width : (tile + 1) * width]
-                    for tile in tiles
-                    for part in parts[group * each : (group + 1) * each]
-                ],
-                axis=0,
-            )
-            sums = lax.dot_general(prints, cells, (((1,), (1,)), ((), ())), preferred_element_type=jnp.float32)
-            for i, tile in enumerate(tiles):
-                sums_ref[group, tile] = sums[:, i * LANES : (i + 1) * LANES].reshape(peers, CAP, 8, LANES)
+    slots = peers * CAP
+    prints = prints_ref[...].reshape(slots * 8, width)
+    for low in range(0, TILES_DEV, 2):
+        tiles = range(low, min(low + 2, TILES_DEV))
+        cells = jnp.concatenate(
+            [part[:, tile * width : (tile + 1) * width] for tile in tiles for part in parts], axis=0
+        )
+        sums = lax.dot_general(prints, cells, (((1,), (1,)), ((), ())), preferred_element_type=jnp.float32)
+        for i, tile in enumerate(tiles):
+            sums_ref[tile] = sums[:, i * LANES : (i + 1) * LANES].reshape(slots, 8, LANES)
     same = lax.rem(lax.broadcasted_iota(jnp.int32, (8, LANES), 1), 8) == lax.broadcasted_iota(
         jnp.int32, (8, LANES), 0
     )
     shift = 32 * own_ref[0]
 
-    def pick(two, carry):
-        rows = []
-        for i in range(2):
-            peer = 2 * two + i
-            for side in range(CORES):
-                group = jnp.where(core == side, 0, 1)
-                for slot in range(CAP):
-                    loc = loc_ref[(peer * CORES + side) * CAP + slot]
-                    rows.append(
-                        jnp.sum(jnp.where(same, sums_ref[group, loc, peer, slot], 0.0), axis=0, keepdims=True)
-                    )
-        out_ref[pl.ds(pl.multiple_of(two * 8, 8), 8)] = pltpu.roll(jnp.concatenate(rows, axis=0), shift, 1)
-        return carry
-
-    lax.fori_loop(0, peers // 2, pick, 0, unroll=2)
+    def pick(group, carry):
+        at = pl.multiple_of(group * 8, 8)
+        rows = [
+            jnp.sum(jnp.where(same, sums_ref[loc_ref[at + i], at + i], 0.0), axis=0, keepdims=True) for i in range(8)
+        ]
+        out_ref[pl.ds(at, 8)] = pltpu.roll(jnp.concatenate(rows, axis=0), shift, 1)
+        return carry
+
+    lax.fori_loop(0, slots // 8, pick, 0, unroll=2)
 
 
 def station_kernel(place_ref, count_ref, back_ref, out_ref, sums_ref):
@@ -225,15 +221,12 @@
     stations = footprint.shape[0]
     slots = stations * KT
     bands = lax.axis_size("station")
-    peers = bands // CORES
     band = lax.axis_index("station")
     part = lax.axis_index("sample")
     own = part.astype(jnp.int32).reshape(1)
     cells = rows * TILE_LON // PARTS
     down = [(i, i + 1) for i in range(bands - 1)]
     up = [(i + 1, i) for i in range(bands - 1)]
-    beside = [(i, i ^ 1) for i in range(bands)]
-    same_core = [[CORES * i + core for i in range(peers)] for core in range(CORES)]
 
     last, first = pl.pallas_call(
         edge_kernel,
@@ -247,26 +240,33 @@
 
     src_all = tile_src[:, :, 0].T
     my_src = lax.dynamic_slice_in_dim(src_all, band * stations, stations, axis=1)
-    prints = lax.dynamic_slice_in_dim(footprint, part * cells, cells, axis=2).reshape(slots, 8, TILE_LON)
     sent, place = pl.pallas_call(
         pack_kernel,
         out_shape=(
             jax.ShapeDtypeStruct((bands, 8 * CAP, TILE_LON), jnp.bfloat16),
             jax.ShapeDtypeStruct((slots,), jnp.int32),
         ),
-        in_specs=[spec(SMEM), spec(VMEM)],
-        out_specs=(spec(VMEM), spec(SMEM)),
-        scratch_shapes=[SMEM((bands,), jnp.int32), SMEM((CAP * bands,), jnp.int32)],
+        grid_spec=pltpu.PrefetchScalarGridSpec(
+            num_scalar_prefetch=2,
+            grid=(1,),
+            in_specs=[pl.BlockSpec((stations, KT, cells), lambda i, part, src: (0, 0, part[0]))],
+            out_specs=(
+                pl.BlockSpec((bands, 8 * CAP, TILE_LON), lambda i, part, src: (0, 0, 0)),
+                spec(SMEM),
+            ),
+            scratch_shapes=[
+                SMEM((bands,), jnp.int32),
+                SMEM((CAP * bands,), jnp.int32),
+                VMEM((bands, 8 * CAP, 8 * slots), jnp.bfloat16),
+            ],
+        ),
+        compiler_params=pltpu.CompilerParams(vmem_limit_bytes=24 * 2**20),
         name="pack",
-    )(my_src, prints)
+    )(own, my_src, footprint)
     sent, _, _ = lax.optimization_barrier((sent, above, below))
-    arrived = lax.all_to_all(
-        sent.reshape(peers, CORES * CAP * 8, TILE_LON),
-        "station", split_axis=0, concat_axis=0, axis_index_groups=same_core, tiled=True,
-    )
-
-    core = lax.rem(band, CORES).astype(jnp.int32)
-    mine, theirs = [None] * (2 * PARTS), [None] * (2 * PARTS)
+    arrived = lax.all_to_all(sent, "station", split_axis=0, concat_axis=0, tiled=True)
+
+    parts = [None] * (2 * PARTS)
     for pair in range(samples // 2):
         finals = pl.pallas_call(
             functools.partial(diffuse_kernel, pair),
@@ -283,36 +283,30 @@
         )(own, diff_steps, flux, above, below, coeff)
         for j in range(PARTS):
             turn = (PARTS - j) % PARTS
-            part_j = finals[0]
+            parts[2 * j + pair] = finals[0]
             if turn:
-                part_j = lax.ppermute(finals[turn], "sample", [(i, (i + turn) % PARTS) for i in range(PARTS)])
-            mine[2 * j + pair] = part_j
-            theirs[2 * j + pair] = lax.ppermute(part_j, "station", beside)
+                parts[2 * j + pair] = lax.ppermute(
+                    finals[turn], "sample", [(i, (i + turn) % PARTS) for i in range(PARTS)]
+                )
 
     order = jnp.arange(stations * bands, dtype=jnp.int32) % stations
     code = (order[None, :] * KT + jnp.arange(KT, dtype=jnp.int32)[:, None]) * 8 + tile_local.T
-    picks = []
-    for side in range(CORES):
-        named = src_all == (band - core + side)
-        first = jnp.min(jnp.min(jnp.where(named, code, slots * 8), axis=0).reshape(bands, stations), axis=1)
-        last = jnp.max(jnp.max(jnp.where(named, code, 0), axis=0).reshape(bands, stations), axis=1)
-        picks += [first & 7, last & 7]
-    loc = lax.dynamic_index_in_dim(jnp.stack(picks, axis=1).reshape(peers, CORES, CORES * CAP), core, 1, keepdims=False)
+    named = src_all == band
+    first = jnp.min(jnp.min(jnp.where(named, code, slots * 8), axis=0).reshape(bands, stations), axis=1)
+    last = jnp.max(jnp.max(jnp.where(named, code, 0), axis=0).reshape(bands, stations), axis=1)
+    loc = jnp.stack([first & 7, last & 7], axis=1)
 
     values = pl.pallas_call(
         dots_kernel,
         out_shape=jax.ShapeDtypeStruct((bands * CAP, LANES), jnp.float32),
-        in_specs=[spec(SMEM)] * 3 + [spec(VMEM)] * (1 + 2 * CORES * PARTS),
+        in_specs=[spec(SMEM)] * 2 + [spec(VMEM)] * (1 + 2 * PARTS),
         out_specs=spec(VMEM),
-        scratch_shapes=[VMEM((CORES, TILES_DEV, peers, CAP, 8, LANES), jnp.float32)],
+        scratch_shapes=[VMEM((TILES_DEV, bands * CAP, 8, LANES), jnp.float32)],
         compiler_params=pltpu.CompilerParams(vmem_limit_bytes=24 * 2**20),
         name="dots",
-    )(own, core.reshape(1), loc.reshape(-1), arrived, *mine, *theirs)
-
-    back = lax.all_to_all(
-        values.reshape(peers, CORES * CAP, LANES),
-        "station", split_axis=0, concat_axis=0, axis_index_groups=same_core, tiled=True,
-    )
+    )(own, loc.reshape(-1), arrived, *parts)
+
+    back = lax.all_to_all(values.reshape(bands, CAP, LANES), "station", split_axis=0, concat_axis=0, tiled=True)
     share = pl.pallas_call(
         station_kernel,
         out_shape=jax.ShapeDtypeStruct((stations, 16), jnp.float32),

time: 93.9 us -> 89.5 us (0.953)
  local copies, waits for them, and re-layouts: 9.77 us -> 5.03 us
  waiting for transfers between devices: 6.62 us -> 10.2 us
  Pallas kernels: 22.4 us -> 21 us
  starting transfers between devices: 32.4 us -> 31.1 us
  other arithmetic: 2.64 us -> 1.59 us
    ppermute x6, waiting for transfers between devices: 2.79 us -> 7.02 us  [body(): lax.ppermute(finals[turn], 'sample', [(i, (i + turn) % PARTS) for i in ra...]
    reshape x1 -> x0, local copies, waits for them, and re-layouts: 2.31 us -> none  [body(): lax.dynamic_slice_in_dim(footprint, part * cells, cells, axis=2)]
    ppermute x8 -> x0, starting transfers between devices: 2.03 us -> none  [body(): theirs[2 * j + pair] = lax.ppermute(part_j, 'station', beside)]
    all_to_all x1, starting transfers between devices: 14.5 us -> 15.8 us  [body(): lax.all_to_all(sent, 'station', split_axis=0, concat_axis=0, tiled=True)]
    dynamic_slice x2 -> x0, local copies, waits for them, and re-layouts: 1.08 us -> none  [the longest x1 1 us: body(): lax.dynamic_slice_in_dim(footprint, part * cells, cells, axis=2)]
    unnamed x24 -> x20, local copies, waits for them, and re-layouts: 4 us -> 3.89 us
  transfers between devices with their start and end apart: 20 -> 12, of which waited for: 4 -> 7; matrix products, arithmetic and copies ran while one was open for 8% -> 2% of each run, Pallas kernels for 16% -> 16%
where the time goes in v1:
time: 89.5 us; the launch traced here: 89.1 us
  starting transfers between devices  31.1 us (35%)
  Pallas kernels  21 us (23%)
  blocking collectives  20 us (22%)
  waiting for transfers between devices  10.2 us (11%)
  local copies, waits for them, and re-layouts  5.03 us (6%)
  other arithmetic  1.59 us (2%)
    all_to_all x1, blocking collectives, body(): lax.all_to_all(values.reshape(bands, CAP, LANES), 'station', split_axis=0...  20 us
    all_to_all x1, starting transfers between devices, body(): lax.all_to_all(sent, 'station', split_axis=0, concat_axis=0, tiled=True)  15.8 us
    pallas_call x2, Pallas kernels, body(): pl.pallas_call(functools.partial(diffuse_kernel, pair), out_shape=[jax.Sh...  12.3 us
    ppermute x6, starting transfers between devices, body(): lax.ppermute(finals[turn], 'sample', [(i, (i + turn) % PARTS) for i in ra...  7.58 us
    ppermute x6, waiting for transfers between devices, body(): lax.ppermute(finals[turn], 'sample', [(i, (i + turn) % PARTS) for i in ra...  7.02 us
    ppermute x3, starting transfers between devices, body(): lax.ppermute(share, 'sample', [(i, i ^ flip) for i in range(PARTS)])  4.7 us
    unnamed x20, local copies, waits for them, and re-layouts  3.89 us
    ppermute x3, waiting for transfers between devices, body(): lax.ppermute(share, 'sample', [(i, i ^ flip) for i in range(PARTS)])  3.16 us
  transfers between devices with their start and end apart: 12, of which 7 were waited for; matrix products, arithmetic and copies ran while one was open for 2% of the time, Pallas kernels for 16%

profile of v1, /device:TPU:8, one launch (start us, length us, event | category | flops | bytes accessed | tf_op | source)
XLA Modules:
  0.0 89.1 jit_solution(12543207031575601107)
XLA Ops:
  0.0 2.2 %edges.1 = (bf16[6,8,3584]{2,1,0:T(8,128)(2,1)}, bf16[6,8,3584]{2,1,0:T(8,128)(2,1)}) custom-call(bf16[4,32,3584]{2,1,0:T(8,128)(2,1)} %flux_ref.5, f32[32,3584]{1,0:T(8,128)} %coef_ref.5), custom_call_target="tpu_custom_call" | custom-call | tf_op jit(solution)/shard_map/edges/pallas_call | solution.py:231
  2.2 1.7 %collective-permute-start = (bf16[6,8,3584]{2,1,0:T(8,128)(2,1)}, bf16[6,8,3584]{2,1,0:T(8,128)(2,1)S(1)}, u32[]{:S(2)}, u32[]{:S(2)}) collective-permute-start(bf16[6,8,3584]{2,1,0:T(8,128)(2,1)} %get-tuple-element.20), channel_id=1, source_target_pairs={{0,4},{4,8},{8,12},{12,16},{16,20},{20,24},{24,28},{28,32},{32,36}... | collective-permute-start | bytes 1032200 | tf_op jit(solution)/shard_map/ppermute | solution.py:238
  4.0 1.3 %collective-permute-start.1 = (bf16[6,8,3584]{2,1,0:T(8,128)(2,1)}, bf16[6,8,3584]{2,1,0:T(8,128)(2,1)S(1)}, u32[]{:S(2)}, u32[]{:S(2)}) collective-permute-start(bf16[6,8,3584]{2,1,0:T(8,128)(2,1)} %get-tuple-element.21), channel_id=1, source_target_pairs={{4,0},{8,4},{12,8},{16,12},{20,16},{24,20},{28,24},{32,28},{36,32}... | collective-permute-start | bytes 1032200 | tf_op jit(solution)/shard_map/ppermute | solution.py:239
  5.3 0.8 constant_dynamic-slice_fusion
  6.0 0.0 copy-start.2
  6.1 1.6 %copy-done.2 = bf16[16,4,16384]{2,1,0:T(4,128)(2,1)S(1)} copy-done((bf16[16,4,16384]{2,1,0:T(4,128)(2,1)S(1)}, bf16[16,4,16384]{2,1,0:T(4,128)(2,1)}, u32[]{:S(2)}) %copy-start.2) | copy-done | bytes 2097176
  7.6 0.0 copy-start
  7.6 0.0 copy-start.1
  7.6 0.0 copy-start.4
  7.6 2.2 %pack.1 = (bf16[64,16,512]{2,1,0:T(8,128)(2,1)S(1)}, s32[64]{0:T(128)S(1)}) custom-call(s32[1]{0:T(128)} %bitcast.part_ref.own_ref, s32[4,16]{1,0:T(4,128)S(1)} %bitcast.21, bf16[16,4,16384]{2,1,0:T(4,128)(2,1)S(1)} %copy-done.2), custom_call_target="tpu_custom_call" | custom-call | tf_op jit(solution)/shard_map/pack/pallas_call | solution.py:243
  9.8 0.0 copy-start.3
  9.8 1.0 %copy-done.3 = bf16[64,16,512]{2,1,0:T(8,128)(2,1)} copy-done((bf16[64,16,512]{2,1,0:T(8,128)(2,1)}, bf16[64,16,512]{2,1,0:T(8,128)(2,1)S(1)}, u32[]{:S(2)}) %copy-start.3) | copy-done | bytes 1048600
  10.8 0.0 copy-start.5
  10.8 0.0 copy-start.8
  10.8 0.0 copy-start.9
  10.8 0.0 collective-permute-done.above_ref
  10.8 0.0 collective-permute-done.1.below_ref
  10.8 15.8 %all-to-all-start = ((bf16[64,16,512]{2,1,0:T(8,128)(2,1)}), bf16[64,16,512]{2,1,0:T(8,128)(2,1)S(1)}, u32[]{:S(2)}, u32[]{:S(2)}) async-start(bf16[64,16,512]{2,1,0:T(8,128)(2,1)} %copy-done.3), calls=%async_computation | async-start | bytes 2097152 | tf_op jit(solution)/shard_map/all_to_all | solution.py:267
  26.6 0.0 copy-done.5
  26.7 0.0 copy-done
  26.7 0.0 copy-done.1
  26.7 0.0 copy-done.4
  26.7 6.4 %diffuse.2 = (bf16[16,3584]{1,0:T(8,128)(2,1)S(1)}, bf16[16,3584]{1,0:T(8,128)(2,1)S(1)}, bf16[16,3584]{1,0:T(8,128)(2,1)S(1)}, bf16[16,3584]{1,0:T(8,128)(2,1)}) custom-call(s32[1]{0:T(128)} %bitcast.part_ref.own_ref, s32[4]{0:T(128)S(1)} %copy-done.4, bf16[4,32,3584]{2,1,0:T(8,128)(2,1)S(1)} %copy-done, ...), custom_call_target="tpu_custom_call" | custom-call | tf_op jit(solution)/shard_map/diffuse/pallas_call | solution.py:271
  33.1 0.0 copy-start.6
  33.1 0.6 copy-done.6
  33.7 0.0 copy-start.7
  33.7 0.6 copy-done.7
  34.4 0.0 collective-permute-start.2
  34.4 0.0 copy-done.8
  34.4 0.0 copy-done.9
  34.4 0.1 reshape.55
  34.5 0.1 reshape.54
  34.6 0.1 reduce_max.19
  34.7 0.1 reduce_min.19
  34.8 5.9 %diffuse.3 = (bf16[16,3584]{1,0:T(8,128)(2,1)S(1)}, bf16[16,3584]{1,0:T(8,128)(2,1)}, bf16[16,3584]{1,0:T(8,128)(2,1)}, bf16[16,3584]{1,0:T(8,128)(2,1)}) custom-call(s32[1]{0:T(128)} %bitcast.part_ref.own_ref, s32[4]{0:T(128)S(1)} %copy-done.4, bf16[4,32,3584]{2,1,0:T(8,128)(2,1)S(1)} %copy-done, bf16[6,8,3584]{2,1,0:T(8,128)(2,1)S(1)} %collective-permute-done.above_ref, ...), custom_call_target="tpu_custom_call" | custom-call | tf_op jit(solution)/shard_map/diffuse/pallas_call | solution.py:271
  40.8 3.5 %collective-permute-start.3 = (bf16[16,3584]{1,0:T(8,128)(2,1)}, bf16[16,3584]{1,0:T(8,128)(2,1)S(1)}, u32[]{:S(2)}, u32[]{:S(2)}) collective-permute-start(bf16[16,3584]{1,0:T(8,128)(2,1)} %get-tuple-element.26), channel_id=1, source_target_pairs={{0,3},{1,0},{2,1},{3,2},{4,7},{5,4},{6,5},{7,6},{8,11},{9,8},{10,9... | collective-permute-start | bytes 344072 | tf_op jit(solution)/shard_map/ppermute | solution.py:288
  44.2 0.0 collective-permute-start.4
  44.2 3.5 %collective-permute-start.5 = (bf16[16,3584]{1,0:T(8,128)(2,1)}, bf16[16,3584]{1,0:T(8,128)(2,1)S(1)}, u32[]{:S(2)}, u32[]{:S(2)}) collective-permute-start(bf16[16,3584]{1,0:T(8,128)(2,1)} %get-tuple-element.28), channel_id=1, source_target_pairs={{0,2},{1,3},{2,0},{3,1},{4,6},{5,7},{6,4},{7,5},{8,10},{9,11},{10,... | collective-permute-start | bytes 344072 | tf_op jit(solution)/shard_map/ppermute | solution.py:288
  47.7 0.0 collective-permute-start.6
  47.7 0.0 collective-permute-done.2.refs_2_
  47.7 0.6 collective-permute-start.7
  48.4 0.1 copy.11
  48.5 0.1 reshape.56.loc_ref
  48.6 0.0 collective-permute-done.3.refs_3_
  48.6 3.1 %collective-permute-done.4.refs_4_ = bf16[16,3584]{1,0:T(8,128)(2,1)S(1)} collective-permute-done((bf16[16,3584]{1,0:T(8,128)(2,1)}, bf16[16,3584]{1,0:T(8,128)(2,1)S(1)}, u32[]{:S(2)}, u32[]{:S(2)}) %collective-permute-start.4) | collective-permute-done | bytes 114720 | tf_op jit(solution)/shard_map/ppermute | solution.py:288
  51.7 1.2 %collective-permute-done.5.refs_5_ = bf16[16,3584]{1,0:T(8,128)(2,1)S(1)} collective-permute-done((bf16[16,3584]{1,0:T(8,128)(2,1)}, bf16[16,3584]{1,0:T(8,128)(2,1)S(1)}, u32[]{:S(2)}, u32[]{:S(2)}) %collective-permute-start.5) | collective-permute-done | bytes 114720 | tf_op jit(solution)/shard_map/ppermute | solution.py:288
  52.9 1.5 %collective-permute-done.6.refs_6_ = bf16[16,3584]{1,0:T(8,128)(2,1)S(1)} collective-permute-done((bf16[16,3584]{1,0:T(8,128)(2,1)}, bf16[16,3584]{1,0:T(8,128)(2,1)S(1)}, u32[]{:S(2)}, u32[]{:S(2)}) %collective-permute-start.6) | collective-permute-done | bytes 114720 | tf_op jit(solution)/shard_map/ppermute | solution.py:288
  54.4 1.2 %collective-permute-done.7.refs_7_ = bf16[16,3584]{1,0:T(8,128)(2,1)S(1)} collective-permute-done((bf16[16,3584]{1,0:T(8,128)(2,1)}, bf16[16,3584]{1,0:T(8,128)(2,1)S(1)}, u32[]{:S(2)}, u32[]{:S(2)}) %collective-permute-start.7) | collective-permute-done | bytes 114720 | tf_op jit(solution)/shard_map/ppermute | solution.py:288
  55.6 0.0 all-to-all-done.prints_ref
  55.6 2.6 %dots.1 = f32[128,128]{1,0:T(8,128)S(1)} custom-call(s32[1]{0:T(128)} %bitcast.part_ref.own_ref, s32[128]{0:T(128)S(1)} %reshape.56.loc_ref, bf16[64,16,512]{2,1,0:T(8,128)(2,1)S(1)} %all-to-all-done.prints_ref, bf16[16,3584]{1,0:T(8,128)(2,1)S(1)} %get-tuple-element.23.refs_0_, bf16[16,3584]{1,0:T(8,128)(2,1)S(1)} %get-tuple-element.24.refs_1_, ...), custom_call_target="tpu_custom_call" | custom-call | tf_op jit(solution)/shard_map/dots/pallas_call | solution.py:299
  58.2 20.0 %all_to_all.10 = f32[64,2,128]{2,1,0:T(2,128)} all-to-all(f32[64,2,128]{2,1,0:T(2,128)S(1)} %bitcast.20), channel_id=1, replica_groups=mesh['station'=64,'sample'=4] {'station'}, dimensions={0} | all-to-all | bytes 131072 | tf_op jit(solution)/shard_map/all_to_all | solution.py:309
  78.2 1.7 %stations.1 = f32[16,16]{1,0:T(8,128)} custom-call(s32[64]{0:T(128)} %copy-done.5, s32[16]{0:T(128)} %count_ref.1, f32[128,128]{1,0:T(8,128)} %bitcast.22), custom_call_target="tpu_custom_call" | custom-call | tf_op jit(solution)/shard_map/stations/pallas_call | solution.py:310
  79.9 1.9 %collective-permute-start.9 = (f32[16,16]{1,0:T(8,128)}, f32[16,16]{1,0:T(8,128)S(1)}, u32[]{:S(2)}, u32[]{:S(2)}) collective-permute-start(f32[16,16]{1,0:T(8,128)} %stations.1), channel_id=1, source_target_pairs={{0,2},{1,3},{2,0},{3,1},{4,6},{5,7},{6,4},{7,5},{8,10},{9,11},{10,... | collective-permute-start | bytes 3080 | tf_op jit(solution)/shard_map/ppermute | solution.py:318
  81.9 2.1 %collective-permute-start.10 = (f32[16,16]{1,0:T(8,128)}, f32[16,16]{1,0:T(8,128)S(1)}, u32[]{:S(2)}, u32[]{:S(2)}) collective-permute-start(f32[16,16]{1,0:T(8,128)} %stations.1), channel_id=1, source_target_pairs={{0,3},{1,2},{2,1},{3,0},{4,7},{5,6},{6,5},{7,4},{8,11},{9,10},{10,... | collective-permute-start | bytes 3080 | tf_op jit(solution)/shard_map/ppermute | solution.py:318
  83.9 0.7 collective-permute-start.8
  84.6 0.7 collective-permute-done.9
  85.3 0.5 collective-permute-done.10
  85.8 2.0 %collective-permute-done.8 = f32[16,16]{1,0:T(8,128)S(1)} collective-permute-done((f32[16,16]{1,0:T(8,128)}, f32[16,16]{1,0:T(8,128)S(1)}, u32[]{:S(2)}, u32[]{:S(2)}) %collective-permute-start.8) | collective-permute-done | bytes 1056 | tf_op jit(solution)/shard_map/ppermute | solution.py:318
  87.8 1.3 %add_add_fusion = f32[16,16]{1,0:T(8,128)} fusion(f32[16,16]{1,0:T(8,128)S(1)} %collective-permute-done.9, f32[16,16]{1,0:T(8,128)S(1)} %collective-permute-done.10, f32[16,16]{1,0:T(8,128)} %stations.1, f32[16,16]{1,0:T(8,128)S(1)} %collective-permute-done.8), kind=kLoop, calls=%fused_computation.5 | loop fusion | flops 768 | bytes 5120 | tf_op jit(solution)/shard_map/add | solution.py:319
  (4 shorter events, 0.1 us)
Async XLA Ops:
  2.2 8.6 %collective-permute-start = (bf16[6,8,3584]{2,1,0:T(8,128)(2,1)}, bf16[6,8,3584]{2,1,0:T(8,128)(2,1)S(1)}, u32[]{:S(2)}, u32[]{:S(2)}) collective-permute-start(bf16[6,8,3584]{2,1,0:T(8,128)(2,1)} %get-tuple-element.20), channel_id=1, source_target_pairs={{0,4},{4,8},{8,12},{12,16},{16,20},{20,24},{24,28},{28,32},{32,36}... | collective-permute-start | bytes 1032200 | tf_op jit(solution)/shard_map/ppermute | solution.py:238
  4.0 6.8 %collective-permute-start.1 = (bf16[6,8,3584]{2,1,0:T(8,128)(2,1)}, bf16[6,8,3584]{2,1,0:T(8,128)(2,1)S(1)}, u32[]{:S(2)}, u32[]{:S(2)}) collective-permute-start(bf16[6,8,3584]{2,1,0:T(8,128)(2,1)} %get-tuple-element.21), channel_id=1, source_target_pairs={{4,0},{8,4},{12,8},{16,12},{20,16},{24,20},{28,24},{32,28},{36,32}... | collective-permute-start | bytes 1032200 | tf_op jit(solution)/shard_map/ppermute | solution.py:239
  6.0 1.6 %copy-start.2 = (bf16[16,4,16384]{2,1,0:T(4,128)(2,1)S(1)}, bf16[16,4,16384]{2,1,0:T(4,128)(2,1)}, u32[]{:S(2)}) copy-start(bf16[16,4,16384]{2,1,0:T(4,128)(2,1)} %prints_ref.1) | copy-start | bytes 6291460
  7.6 19.0 %copy-start = (bf16[4,32,3584]{2,1,0:T(8,128)(2,1)S(1)}, bf16[4,32,3584]{2,1,0:T(8,128)(2,1)}, u32[]{:S(2)}) copy-start(bf16[4,32,3584]{2,1,0:T(8,128)(2,1)} %flux_ref.5) | copy-start | bytes 2752516
  7.6 19.0 %copy-start.1 = (f32[32,3584]{1,0:T(8,128)S(1)}, f32[32,3584]{1,0:T(8,128)}, u32[]{:S(2)}) copy-start(f32[32,3584]{1,0:T(8,128)} %coef_ref.5) | copy-start | bytes 1376260
  7.6 19.0 %copy-start.4 = (s32[4]{0:T(128)S(1)}, s32[4]{0:T(128)}, u32[]{:S(2)}) copy-start(s32[4]{0:T(128)} %steps_ref.3) | copy-start | bytes 52
  9.8 1.0 %copy-start.3 = (bf16[64,16,512]{2,1,0:T(8,128)(2,1)}, bf16[64,16,512]{2,1,0:T(8,128)(2,1)S(1)}, u32[]{:S(2)}) copy-start(bf16[64,16,512]{2,1,0:T(8,128)(2,1)S(1)} %get-tuple-element.22) | copy-start | bytes 3145732
  10.8 15.8 %copy-start.5 = (s32[64]{0:T(128)}, s32[64]{0:T(128)S(1)}, u32[]{:S(2)}) copy-start(s32[64]{0:T(128)S(1)} %get-tuple-element.18.place_ref) | copy-start | bytes 772
  10.8 23.6 %copy-start.8 = (s32[1024,4,1]{0,2,1:T(1,128)S(1)}, s32[1024,4,1]{0,2,1:T(1,128)}, u32[]{:S(2)}) copy-start(s32[1024,4,1]{0,2,1:T(1,128)} %param.11) | copy-start | bytes 49156
  10.8 23.6 %copy-start.9 = (s32[1024,4]{0,1:T(4,128)S(1)}, s32[1024,4]{0,1:T(4,128)}, u32[]{:S(2)}) copy-start(s32[1024,4]{0,1:T(4,128)} %param.12) | copy-start | bytes 49156
  10.8 44.8 %all-to-all-start = ((bf16[64,16,512]{2,1,0:T(8,128)(2,1)}), bf16[64,16,512]{2,1,0:T(8,128)(2,1)S(1)}, u32[]{:S(2)}, u32[]{:S(2)}) async-start(bf16[64,16,512]{2,1,0:T(8,128)(2,1)} %copy-done.3), calls=%async_computation | async-start | bytes 2097152 | tf_op jit(solution)/shard_map/all_to_all | solution.py:267
  33.1 0.7 copy-start.6
  33.7 0.6 copy-start.7
  34.4 13.4 %collective-permute-start.2 = (bf16[16,3584]{1,0:T(8,128)(2,1)}, bf16[16,3584]{1,0:T(8,128)(2,1)S(1)}, u32[]{:S(2)}, u32[]{:S(2)}) collective-permute-start(bf16[16,3584]{1,0:T(8,128)(2,1)} %get-tuple-element.25), channel_id=1, source_target_pairs={{0,3},{1,0},{2,1},{3,2},{4,7},{5,4},{6,5},{7,6},{8,11},{9,8},{10,9... | collective-permute-start | bytes 344072 | tf_op jit(solution)/shard_map/ppermute | solution.py:288
  40.8 7.8 %collective-permute-start.3 = (bf16[16,3584]{1,0:T(8,128)(2,1)}, bf16[16,3584]{1,0:T(8,128)(2,1)S(1)}, u32[]{:S(2)}, u32[]{:S(2)}) collective-permute-start(bf16[16,3584]{1,0:T(8,128)(2,1)} %get-tuple-element.26), channel_id=1, source_target_pairs={{0,3},{1,0},{2,1},{3,2},{4,7},{5,4},{6,5},{7,6},{8,11},{9,8},{10,9... | collective-permute-start | bytes 344072 | tf_op jit(solution)/shard_map/ppermute | solution.py:288
  44.2 7.5 %collective-permute-start.4 = (bf16[16,3584]{1,0:T(8,128)(2,1)}, bf16[16,3584]{1,0:T(8,128)(2,1)S(1)}, u32[]{:S(2)}, u32[]{:S(2)}) collective-permute-start(bf16[16,3584]{1,0:T(8,128)(2,1)} %copy-done.7), channel_id=1, source_target_pairs={{0,2},{1,3},{2,0},{3,1},{4,6},{5,7},{6,4},{7,5},{8,10},{9,11},{10,... | collective-permute-start | bytes 344072 | tf_op jit(solution)/shard_map/ppermute | solution.py:288
  44.2 8.7 %collective-permute-start.5 = (bf16[16,3584]{1,0:T(8,128)(2,1)}, bf16[16,3584]{1,0:T(8,128)(2,1)S(1)}, u32[]{:S(2)}, u32[]{:S(2)}) collective-permute-start(bf16[16,3584]{1,0:T(8,128)(2,1)} %get-tuple-element.28), channel_id=1, source_target_pairs={{0,2},{1,3},{2,0},{3,1},{4,6},{5,7},{6,4},{7,5},{8,10},{9,11},{10,... | collective-permute-start | bytes 344072 | tf_op jit(solution)/shard_map/ppermute | solution.py:288
  47.7 6.7 %collective-permute-start.6 = (bf16[16,3584]{1,0:T(8,128)(2,1)}, bf16[16,3584]{1,0:T(8,128)(2,1)S(1)}, u32[]{:S(2)}, u32[]{:S(2)}) collective-permute-start(bf16[16,3584]{1,0:T(8,128)(2,1)} %copy-done.6), channel_id=1, source_target_pairs={{0,1},{1,2},{2,3},{3,0},{4,5},{5,6},{6,7},{7,4},{8,9},{9,10},{10,1... | collective-permute-start | bytes 344072 | tf_op jit(solution)/shard_map/ppermute | solution.py:288
  47.7 7.9 %collective-permute-start.7 = (bf16[16,3584]{1,0:T(8,128)(2,1)}, bf16[16,3584]{1,0:T(8,128)(2,1)S(1)}, u32[]{:S(2)}, u32[]{:S(2)}) collective-permute-start(bf16[16,3584]{1,0:T(8,128)(2,1)} %get-tuple-element.30), channel_id=1, source_target_pairs={{0,1},{1,2},{2,3},{3,0},{4,5},{5,6},{6,7},{7,4},{8,9},{9,10},{10,1... | collective-permute-start | bytes 344072 | tf_op jit(solution)/shard_map/ppermute | solution.py:288
  79.9 5.4 %collective-permute-start.9 = (f32[16,16]{1,0:T(8,128)}, f32[16,16]{1,0:T(8,128)S(1)}, u32[]{:S(2)}, u32[]{:S(2)}) collective-permute-start(f32[16,16]{1,0:T(8,128)} %stations.1), channel_id=1, source_target_pairs={{0,2},{1,3},{2,0},{3,1},{4,6},{5,7},{6,4},{7,5},{8,10},{9,11},{10,... | collective-permute-start | bytes 3080 | tf_op jit(solution)/shard_map/ppermute | solution.py:318
  81.9 3.9 %collective-permute-start.10 = (f32[16,16]{1,0:T(8,128)}, f32[16,16]{1,0:T(8,128)S(1)}, u32[]{:S(2)}, u32[]{:S(2)}) collective-permute-start(f32[16,16]{1,0:T(8,128)} %stations.1), channel_id=1, source_target_pairs={{0,3},{1,2},{2,1},{3,0},{4,7},{5,6},{6,5},{7,4},{8,11},{9,10},{10,... | collective-permute-start | bytes 3080 | tf_op jit(solution)/shard_map/ppermute | solution.py:318
  83.9 3.9 %collective-permute-start.8 = (f32[16,16]{1,0:T(8,128)}, f32[16,16]{1,0:T(8,128)S(1)}, u32[]{:S(2)}, u32[]{:S(2)}) collective-permute-start(f32[16,16]{1,0:T(8,128)} %stations.1), channel_id=1, source_target_pairs={{0,1},{1,0},{2,3},{3,2},{4,5},{5,4},{6,7},{7,6},{8,9},{9,8},{10,11... | collective-permute-start | bytes 3080 | tf_op jit(solution)/shard_map/ppermute | solution.py:318

commit v2 on v1

--- a/solution.py
+++ b/solution.py
@@ -1,5 +1,3 @@
-import functools
-
 import jax
 import jax.numpy as jnp
 from jax import lax
@@ -17,16 +15,28 @@
 LANES = 128
 VMEM = pltpu.VMEM
 SMEM = pltpu.SMEM
+HBM = pltpu.HBM
 
 
 def spec(space):
     return pl.BlockSpec(memory_space=space)
 
 
-def pack_kernel(part_ref, src_ref, prints_ref, sent_ref, place_ref, held_ref, slot_ref, hot_ref):
+def pack_kernel(
+    part_ref, band_ref, src_hbm, prints_hbm, sent_hbm, place_ref,
+    src_ref, held_ref, slot_ref, prints_ref, hot_ref, sent_ref, sems,
+):
     bands, _, width = sent_ref.shape
-    stations = prints_ref.shape[0]
+    stations, _, cells = prints_ref.shape
     slots = stations * KT
+    low = pl.multiple_of(part_ref[0] * cells, cells)
+    prints_in = pltpu.make_async_copy(prints_hbm.at[:, :, pl.ds(low, cells)], prints_ref, sems.at[0])
+    prints_in.start()
+    first = band_ref[0] * stations
+    low = pl.multiple_of(lax.div(first, LANES) * LANES, LANES)
+    src_in = pltpu.make_async_copy(src_hbm.at[:, :, pl.ds(low, LANES)], src_ref, sems.at[1])
+    src_in.start()
+    first = lax.rem(first, LANES)
 
     def clear(i, carry):
         held_ref[i] = 0
@@ -35,10 +45,11 @@
         return carry
 
     lax.fori_loop(0, bands, clear, 0, unroll=8)
+    src_in.wait()
 
     def assign(station, carry):
         for k in range(KT):
-            band = src_ref[k, station]
+            band = src_ref[k, 0, first + station]
             rank = jnp.minimum(held_ref[band], CAP - 1)
             held_ref[band] = rank + 1
             place_ref[KT * station + k] = CAP * band + rank
@@ -57,13 +68,20 @@
 
     lax.fori_loop(0, bands, heat, 0, unroll=8)
 
-    flat = prints_ref[...].reshape(slots, 8 * width)
-    cells = jnp.concatenate([flat[:, r * width : (r + 1) * width] for r in range(8)], axis=0)
+    prints_in.wait()
+    flat = prints_ref[...].reshape(slots, cells)
+    stacked = jnp.concatenate([flat[:, r * width : (r + 1) * width] for r in range(8)], axis=0)
     some = bands // 4
-    for low in range(0, bands, some):
-        hot = hot_ref[low : low + some].reshape(some * 16, slots * 8)
-        moved = jnp.dot(hot, cells, preferred_element_type=jnp.float32).astype(jnp.bfloat16)
-        sent_ref[low : low + some] = moved.reshape(some, 16, width)
+    copies = []
+    for turn in range(4):
+        at = slice(turn * some, (turn + 1) * some)
+        hot = hot_ref[at].reshape(some * 16, slots * 8)
+        moved = jnp.dot(hot, stacked, preferred_element_type=jnp.float32).astype(jnp.bfloat16)
+        sent_ref[at] = moved.reshape(some, 16, width)
+        copies.append(pltpu.make_async_copy(sent_ref.at[at], sent_hbm.at[at], sems.at[2 + turn]))
+        copies[-1].start()
+    for copy in copies:
+        copy.wait()
 
 
 def edge_kernel(flux_ref, coef_ref, last_ref, first_ref):
@@ -77,8 +95,8 @@
 
 
 def diffuse_kernel(
-    pair, own_ref, steps_ref, flux_ref, above_ref, below_ref, coef_ref,
-    out0_ref, out1_ref, out2_ref, out3_ref, even_ref, odd_ref, coefs_ref,
+    own_ref, steps_ref, flux_ref, above_ref, below_ref, coef_ref,
+    out0_hbm, out1_hbm, out2_hbm, out3_hbm, even_ref, odd_ref, coefs_ref, out_ref, sems,
 ):
     own = own_ref[0]
     samples, rows, lon = flux_ref.shape
@@ -98,8 +116,8 @@
         coefs_ref[strip, HALO : HALO + rows] = coef_ref[:, at]
         for low in (0, HALO + tall):
             odd_ref[strip, low : low + HALO] = edge
-            for side in range(2):
-                even_ref[side, strip, low : low + HALO] = edge
+            for sample in range(samples):
+                even_ref[sample, strip, low : low + HALO] = edge
 
     def update(old_ref, new_ref, tile):
         at = HALO + 8 * tile
@@ -138,9 +156,8 @@
             ref[strip, 2 * HALO : 2 * HALO + rows] = flux_ref[sample, :, at].astype(jnp.float32)
             ref[strip, 2 * HALO + rows : HALO + tall] = below_ref[sample, :, at].astype(jnp.float32)
 
-    def evolve(side, carry):
-        sample = 2 * pair + side
-        even = even_ref.at[side]
+    def evolve(sample, carry):
+        even = even_ref.at[sample]
         count = jnp.minimum(steps_ref[sample], ITERS)
         half = lax.div(count, 2)
 
@@ -161,20 +178,28 @@
         lax.fori_loop(0, half, two, 0)
         return carry
 
-    lax.fori_loop(0, 2, evolve, 0)
-
-    for turn, out_ref in enumerate((out0_ref, out1_ref, out2_ref, out3_ref)):
+    lax.fori_loop(0, samples, evolve, 0)
+
+    copies = []
+    for turn, out_hbm in ((2, out2_hbm), (1, out1_hbm), (3, out3_hbm), (0, out0_hbm)):
         low = pl.multiple_of(2 * HALO + 8 * lax.rem(own + turn, PARTS), 8)
-        for strip in range(strips):
-            both = [even_ref[side, strip, pl.ds(low, 8)] for side in range(2)]
-            out_ref[:, strip * LANES : (strip + 1) * LANES] = jnp.concatenate(both, axis=0).astype(jnp.bfloat16)
+        for pair in range(samples // 2):
+            for strip in range(strips):
+                both = [even_ref[2 * pair + side, strip, pl.ds(low, 8)] for side in range(2)]
+                out_ref[turn, 16 * pair : 16 * pair + 16, strip * LANES : (strip + 1) * LANES] = jnp.concatenate(
+                    both, axis=0
+                ).astype(jnp.bfloat16)
+        copies.append(pltpu.make_async_copy(out_ref.at[turn], out_hbm, sems.at[turn]))
+        copies[-1].start()
+    for copy in copies:
+        copy.wait()
 
 
 def dots_kernel(own_ref, loc_ref, prints_ref, *refs):
-    parts = refs[: PARTS * 2]
-    out_ref, sums_ref = refs[PARTS * 2 :]
-    peers, _, width = prints_ref.shape
-    slots = peers * CAP
+    parts = refs[:PARTS]
+    out_ref, sums_ref = refs[PARTS:]
+    bands, _, width = prints_ref.shape
+    slots = bands * CAP
     prints = prints_ref[...].reshape(slots * 8, width)
     for low in range(0, TILES_DEV, 2):
         tiles = range(low, min(low + 2, TILES_DEV))
@@ -239,55 +264,47 @@
     below = lax.ppermute(first, "station", up)
 
     src_all = tile_src[:, :, 0].T
-    my_src = lax.dynamic_slice_in_dim(src_all, band * stations, stations, axis=1)
     sent, place = pl.pallas_call(
         pack_kernel,
         out_shape=(
             jax.ShapeDtypeStruct((bands, 8 * CAP, TILE_LON), jnp.bfloat16),
             jax.ShapeDtypeStruct((slots,), jnp.int32),
         ),
-        grid_spec=pltpu.PrefetchScalarGridSpec(
-            num_scalar_prefetch=2,
-            grid=(1,),
-            in_specs=[pl.BlockSpec((stations, KT, cells), lambda i, part, src: (0, 0, part[0]))],
-            out_specs=(
-                pl.BlockSpec((bands, 8 * CAP, TILE_LON), lambda i, part, src: (0, 0, 0)),
-                spec(SMEM),
-            ),
-            scratch_shapes=[
-                SMEM((bands,), jnp.int32),
-                SMEM((CAP * bands,), jnp.int32),
-                VMEM((bands, 8 * CAP, 8 * slots), jnp.bfloat16),
-            ],
-        ),
+        in_specs=[spec(SMEM), spec(SMEM), spec(HBM), spec(HBM)],
+        out_specs=(spec(HBM), spec(SMEM)),
+        scratch_shapes=[
+            SMEM((KT, 1, LANES), jnp.int32),
+            SMEM((bands,), jnp.int32),
+            SMEM((CAP * bands,), jnp.int32),
+            VMEM((stations, KT, cells), jnp.bfloat16),
+            VMEM((bands, 8 * CAP, 8 * slots), jnp.bfloat16),
+            VMEM((bands, 8 * CAP, TILE_LON), jnp.bfloat16),
+            pltpu.SemaphoreType.DMA((6,)),
+        ],
         compiler_params=pltpu.CompilerParams(vmem_limit_bytes=24 * 2**20),
         name="pack",
-    )(own, my_src, footprint)
+    )(own, band.astype(jnp.int32).reshape(1), tile_src.transpose(1, 2, 0), footprint)
     sent, _, _ = lax.optimization_barrier((sent, above, below))
     arrived = lax.all_to_all(sent, "station", split_axis=0, concat_axis=0, tiled=True)
 
-    parts = [None] * (2 * PARTS)
-    for pair in range(samples // 2):
-        finals = pl.pallas_call(
-            functools.partial(diffuse_kernel, pair),
-            out_shape=[jax.ShapeDtypeStruct((16, lon), jnp.bfloat16)] * PARTS,
-            in_specs=[spec(SMEM), spec(SMEM)] + [spec(VMEM)] * 4,
-            out_specs=[spec(VMEM)] * PARTS,
-            scratch_shapes=[
-                VMEM((2, lon // LANES, rows + 4 * HALO, LANES), jnp.float32),
-                VMEM((lon // LANES, rows + 4 * HALO, LANES), jnp.float32),
-                VMEM((lon // LANES, rows + 2 * HALO, LANES), jnp.float32),
-            ],
-            compiler_params=pltpu.CompilerParams(vmem_limit_bytes=24 * 2**20),
-            name="diffuse",
-        )(own, diff_steps, flux, above, below, coeff)
-        for j in range(PARTS):
-            turn = (PARTS - j) % PARTS
-            parts[2 * j + pair] = finals[0]
-            if turn:
-                parts[2 * j + pair] = lax.ppermute(
-                    finals[turn], "sample", [(i, (i + turn) % PARTS) for i in range(PARTS)]
-                )
+    finals = pl.pallas_call(
+        diffuse_kernel,
+        out_shape=[jax.ShapeDtypeStruct((samples * 8, lon), jnp.bfloat16)] * PARTS,
+        in_specs=[spec(SMEM), spec(SMEM)] + [spec(VMEM)] * 4,
+        out_specs=[spec(HBM)] * PARTS,
+        scratch_shapes=[
+            VMEM((samples, lon // LANES, rows + 4 * HALO, LANES), jnp.float32),
+            VMEM((lon // LANES, rows + 4 * HALO, LANES), jnp.float32),
+            VMEM((lon // LANES, rows + 2 * HALO, LANES), jnp.float32),
+            VMEM((PARTS, samples * 8, lon), jnp.bfloat16),
+            pltpu.SemaphoreType.DMA((PARTS,)),
+        ],
+        compiler_params=pltpu.CompilerParams(vmem_limit_bytes=24 * 2**20),
+        name="diffuse",
+    )(own, diff_steps, flux, above, below, coeff)
+    parts = [finals[0]] + [
+        lax.ppermute(finals[turn], "sample", [(i, (i + turn) % PARTS) for i in range(PARTS)]) for turn in (3, 2, 1)
+    ]
 
     order = jnp.arange(stations * bands, dtype=jnp.int32) % stations
     code = (order[None, :] * KT + jnp.arange(KT, dtype=jnp.int32)[:, None]) * 8 + tile_local.T
@@ -299,7 +316,7 @@
     values = pl.pallas_call(
         dots_kernel,
         out_shape=jax.ShapeDtypeStruct((bands * CAP, LANES), jnp.float32),
-        in_specs=[spec(SMEM)] * 2 + [spec(VMEM)] * (1 + 2 * PARTS),
+        in_specs=[spec(SMEM)] * 2 + [spec(VMEM)] * (1 + PARTS),
         out_specs=spec(VMEM),
         scratch_shapes=[VMEM((TILES_DEV, bands * CAP, 8, LANES), jnp.float32)],
         compiler_params=pltpu.CompilerParams(vmem_limit_bytes=24 * 2**20),

time: 89.5 us -> 86.2 us (0.963)
  waiting for transfers between devices: 10.2 us -> 16.5 us
  blocking collectives: 20 us -> 16.3 us
  local copies, waits for them, and re-layouts: 5.03 us -> 2.71 us
  starting transfers between devices: 31.1 us -> 28.9 us
  Pallas kernels: 21 us -> 19.1 us
    all_to_all x1, blocking collectives: 20 us -> 16.3 us  [body(): lax.all_to_all(values.reshape(bands, CAP, LANES), 'station', split_axis=0...]
    all_to_all x1, waiting for transfers between devices: 0.01 us -> 3.7 us  [body(): lax.all_to_all(sent, 'station', split_axis=0, concat_axis=0, tiled=True)]
    pallas_call x2 -> x1, Pallas kernels: 12.3 us -> 9.21 us  [body(): pl.pallas_call(diffuse_kernel, out_shape=[jax.ShapeDtypeStruct((samples *...]
    ppermute x6 -> x3, starting transfers between devices: 7.58 us -> 5.52 us  [body(): lax.ppermute(finals[turn], 'sample', [(i, (i + turn) % PARTS) for i in ra...]
    ppermute x6 -> x3, waiting for transfers between devices: 7.02 us -> 8.99 us  [body(): lax.ppermute(finals[turn], 'sample', [(i, (i + turn) % PARTS) for i in ra...]
    unnamed x20 -> x16, local copies, waits for them, and re-layouts: 3.89 us -> 2.33 us
    pallas_call x1, Pallas kernels: 2.17 us -> 3.38 us  [body(): pl.pallas_call(pack_kernel, out_shape=(jax.ShapeDtypeStruct((bands, 8 * C...]
  transfers between devices with their start and end apart: 12 -> 9, of which waited for: 7 -> 7; matrix products, arithmetic and copies ran while one was open for 2% -> 1% of each run, Pallas kernels for 16% -> 15%
where the time goes in v2:
time: 86.2 us; the launch traced here: 85.3 us
  starting transfers between devices  28.9 us (34%)
  Pallas kernels  19.1 us (22%)
  waiting for transfers between devices  16.5 us (19%)
  blocking collectives  16.3 us (19%)
  local copies, waits for them, and re-layouts  2.71 us (3%)
  other arithmetic  1.59 us (2%)
    all_to_all x1, blocking collectives, body(): lax.all_to_all(values.reshape(bands, CAP, LANES), 'station', split_axis=0...  16.3 us
    all_to_all x1, starting transfers between devices, body(): lax.all_to_all(sent, 'station', split_axis=0, concat_axis=0, tiled=True)  15.7 us
    pallas_call x1, Pallas kernels, body(): pl.pallas_call(diffuse_kernel, out_shape=[jax.ShapeDtypeStruct((samples *...  9.21 us
    ppermute x3, waiting for transfers between devices, body(): lax.ppermute(finals[turn], 'sample', [(i, (i + turn) % PARTS) for i in ra...  8.99 us
    ppermute x3, starting transfers between devices, body(): lax.ppermute(finals[turn], 'sample', [(i, (i + turn) % PARTS) for i in ra...  5.52 us
    ppermute x3, starting transfers between devices, body(): lax.ppermute(share, 'sample', [(i, i ^ flip) for i in range(PARTS)])  4.7 us
    ppermute x3, waiting for transfers between devices, body(): lax.ppermute(share, 'sample', [(i, i ^ flip) for i in range(PARTS)])  3.83 us
    all_to_all x1, waiting for transfers between devices, body(): lax.all_to_all(sent, 'station', split_axis=0, concat_axis=0, tiled=True)  3.7 us
  transfers between devices with their start and end apart: 9, of which 7 were waited for; matrix products, arithmetic and copies ran while one was open for 1% of the time, Pallas kernels for 15%

profile of v2, /device:TPU:8, one launch (start us, length us, event | category | flops | bytes accessed | tf_op | source)
XLA Modules:
  0.0 85.3 jit_solution(9506047829193882324)
XLA Ops:
  0.0 2.2 %edges.1 = (bf16[6,8,3584]{2,1,0:T(8,128)(2,1)}, bf16[6,8,3584]{2,1,0:T(8,128)(2,1)}) custom-call(bf16[4,32,3584]{2,1,0:T(8,128)(2,1)} %flux_ref.3, f32[32,3584]{1,0:T(8,128)} %coef_ref.3), custom_call_target="tpu_custom_call" | custom-call | tf_op jit(solution)/shard_map/edges/pallas_call | solution.py:256
  2.2 1.7 %collective-permute-start = (bf16[6,8,3584]{2,1,0:T(8,128)(2,1)}, bf16[6,8,3584]{2,1,0:T(8,128)(2,1)S(1)}, u32[]{:S(2)}, u32[]{:S(2)}) collective-permute-start(bf16[6,8,3584]{2,1,0:T(8,128)(2,1)} %get-tuple-element.16), channel_id=1, source_target_pairs={{0,4},{4,8},{8,12},{12,16},{16,20},{20,24},{24,28},{28,32},{32,36}... | collective-permute-start | bytes 1032200 | tf_op jit(solution)/shard_map/ppermute | solution.py:263
  4.0 1.3 %collective-permute-start.1 = (bf16[6,8,3584]{2,1,0:T(8,128)(2,1)}, bf16[6,8,3584]{2,1,0:T(8,128)(2,1)S(1)}, u32[]{:S(2)}, u32[]{:S(2)}) collective-permute-start(bf16[6,8,3584]{2,1,0:T(8,128)(2,1)} %get-tuple-element.17), channel_id=1, source_target_pairs={{4,0},{8,4},{12,8},{16,12},{20,16},{24,20},{28,24},{32,28},{36,32}... | collective-permute-start | bytes 1032200 | tf_op jit(solution)/shard_map/ppermute | solution.py:264
  5.3 0.0 copy-start.1
  5.3 1.6 %copy-done.1 = bf16[16,4,16384]{2,1,0:T(4,128)(2,1)S(1)} copy-done((bf16[16,4,16384]{2,1,0:T(4,128)(2,1)S(1)}, bf16[16,4,16384]{2,1,0:T(4,128)(2,1)}, u32[]{:S(2)}) %copy-start.1) | copy-done | bytes 2097176
  6.9 0.0 copy-start.3
  6.9 0.7 copy-done.3
  7.6 0.0 copy-start.4
  7.6 0.0 copy-start.7
  7.6 0.0 copy-start
  7.6 0.0 copy-start.2
  7.6 0.0 copy-start.5
  7.6 3.4 %pack.1 = (bf16[64,16,512]{2,1,0:T(8,128)(2,1)}, s32[64]{0:T(128)S(1)}) custom-call(s32[1]{0:T(128)} %bitcast.part_ref.own_ref, s32[1]{0:T(128)} %bitcast.1.band_ref, s32[4,1,1024]{2,1,0:T(1,128)S(1)} %bitcast.20, bf16[16,4,16384]{2,1,0:T(4,128)(2,1)S(1)} %copy-done.1), custom_call_target="tpu_custom_call" | custom-call | tf_op jit(solution)/shard_map/pack/pallas_call | solution.py:267
  11.0 0.0 copy-start.6
  11.0 0.0 collective-permute-done.above_ref
  11.0 0.0 collective-permute-done.1.below_ref
  11.0 15.7 %all-to-all-start = ((bf16[64,16,512]{2,1,0:T(8,128)(2,1)}), bf16[64,16,512]{2,1,0:T(8,128)(2,1)S(1)}, u32[]{:S(2)}, u32[]{:S(2)}) async-start(bf16[64,16,512]{2,1,0:T(8,128)(2,1)} %get-tuple-element.18), calls=%async_computation | async-start | bytes 2097152 | tf_op jit(solution)/shard_map/all_to_all | solution.py:288
  26.7 0.0 copy-done.4
  26.7 0.0 copy-done.7
  26.8 0.1 reshape.55
  26.9 0.1 reshape.54
  26.9 0.1 reduce_max.19
  27.1 0.0 copy-done.6
  27.1 0.1 reduce_min.19
  27.2 0.0 copy-done
  27.2 0.0 copy-done.2
  27.2 0.0 copy-done.5
  27.2 9.2 %diffuse.1 = (bf16[32,3584]{1,0:T(8,128)(2,1)S(1)}, bf16[32,3584]{1,0:T(8,128)(2,1)}, bf16[32,3584]{1,0:T(8,128)(2,1)}, bf16[32,3584]{1,0:T(8,128)(2,1)}) custom-call(s32[1]{0:T(128)} %bitcast.part_ref.own_ref, s32[4]{0:T(128)S(1)} %copy-done.5, bf16[4,32,3584]{2,1,0:T(8,128)(2,1)S(1)} %copy-done, bf16[6,8,3584]{2,1,0:T(8,128)(2,1)S(1)} %collective-permute-done.above_ref, ...), custom_call_target="tpu_custom_call" | custom-call | tf_op jit(solution)/shard_map/diffuse/pallas_call | solution.py:290
  36.4 2.9 %collective-permute-start.2 = (bf16[32,3584]{1,0:T(8,128)(2,1)}, bf16[32,3584]{1,0:T(8,128)(2,1)S(1)}, u32[]{:S(2)}, u32[]{:S(2)}) collective-permute-start(bf16[32,3584]{1,0:T(8,128)(2,1)} %get-tuple-element.20), channel_id=1, source_target_pairs={{0,3},{1,0},{2,1},{3,2},{4,7},{5,4},{6,5},{7,6},{8,11},{9,8},{10,9... | collective-permute-start | bytes 688136 | tf_op jit(solution)/shard_map/ppermute | solution.py:306
  39.3 0.3 collective-permute-start.3
  39.6 2.3 %collective-permute-start.4 = (bf16[32,3584]{1,0:T(8,128)(2,1)}, bf16[32,3584]{1,0:T(8,128)(2,1)S(1)}, u32[]{:S(2)}, u32[]{:S(2)}) collective-permute-start(bf16[32,3584]{1,0:T(8,128)(2,1)} %get-tuple-element.22), channel_id=1, source_target_pairs={{0,1},{1,2},{2,3},{3,0},{4,5},{5,6},{6,7},{7,4},{8,9},{9,10},{10,1... | collective-permute-start | bytes 688136 | tf_op jit(solution)/shard_map/ppermute | solution.py:306
  42.0 0.1 copy.11
  42.1 0.1 reshape.56.loc_ref
  42.2 3.4 %collective-permute-done.2.refs_1_ = bf16[32,3584]{1,0:T(8,128)(2,1)S(1)} collective-permute-done((bf16[32,3584]{1,0:T(8,128)(2,1)}, bf16[32,3584]{1,0:T(8,128)(2,1)S(1)}, u32[]{:S(2)}, u32[]{:S(2)}) %collective-permute-start.2) | collective-permute-done | bytes 229408 | tf_op jit(solution)/shard_map/ppermute | solution.py:306
  45.6 4.7 %collective-permute-done.3.refs_2_ = bf16[32,3584]{1,0:T(8,128)(2,1)S(1)} collective-permute-done((bf16[32,3584]{1,0:T(8,128)(2,1)}, bf16[32,3584]{1,0:T(8,128)(2,1)S(1)}, u32[]{:S(2)}, u32[]{:S(2)}) %collective-permute-start.3) | collective-permute-done | bytes 229408 | tf_op jit(solution)/shard_map/ppermute | solution.py:306
  50.3 0.9 %collective-permute-done.4.refs_3_ = bf16[32,3584]{1,0:T(8,128)(2,1)S(1)} collective-permute-done((bf16[32,3584]{1,0:T(8,128)(2,1)}, bf16[32,3584]{1,0:T(8,128)(2,1)S(1)}, u32[]{:S(2)}, u32[]{:S(2)}) %collective-permute-start.4) | collective-permute-done | bytes 229408 | tf_op jit(solution)/shard_map/ppermute | solution.py:306
  51.2 3.7 %all-to-all-done.prints_ref = bf16[64,16,512]{2,1,0:T(8,128)(2,1)S(1)} async-done(((bf16[64,16,512]{2,1,0:T(8,128)(2,1)}), bf16[64,16,512]{2,1,0:T(8,128)(2,1)S(1)}, u32[]{:S(2)}, u32[]{:S(2)}) %all-to-all-start) | async-done | bytes 1048608 | tf_op jit(solution)/shard_map/all_to_all | solution.py:288
  54.9 2.6 %dots.1 = f32[128,128]{1,0:T(8,128)S(1)} custom-call(s32[1]{0:T(128)} %bitcast.part_ref.own_ref, s32[128]{0:T(128)S(1)} %reshape.56.loc_ref, bf16[64,16,512]{2,1,0:T(8,128)(2,1)S(1)} %all-to-all-done.prints_ref, bf16[32,3584]{1,0:T(8,128)(2,1)S(1)} %get-tuple-element.19.refs_0_, bf16[32,3584]{1,0:T(8,128)(2,1)S(1)} %collective-permute-done.2.refs_1_, ...), custom_call_target="tpu_custom_call" | custom-call | tf_op jit(solution)/shard_map/dots/pallas_call | solution.py:316
  57.5 16.3 %all_to_all.10 = f32[64,2,128]{2,1,0:T(2,128)} all-to-all(f32[64,2,128]{2,1,0:T(2,128)S(1)} %bitcast.19), channel_id=1, replica_groups=mesh['station'=64,'sample'=4] {'station'}, dimensions={0} | all-to-all | bytes 131072 | tf_op jit(solution)/shard_map/all_to_all | solution.py:326
  73.8 1.7 %stations.1 = f32[16,16]{1,0:T(8,128)} custom-call(s32[64]{0:T(128)} %copy-done.6, s32[16]{0:T(128)} %count_ref.1, f32[128,128]{1,0:T(8,128)} %bitcast.21), custom_call_target="tpu_custom_call" | custom-call | tf_op jit(solution)/shard_map/stations/pallas_call | solution.py:327
  75.5 2.6 %collective-permute-start.6 = (f32[16,16]{1,0:T(8,128)}, f32[16,16]{1,0:T(8,128)S(1)}, u32[]{:S(2)}, u32[]{:S(2)}) collective-permute-start(f32[16,16]{1,0:T(8,128)} %stations.1), channel_id=1, source_target_pairs={{0,2},{1,3},{2,0},{3,1},{4,6},{5,7},{6,4},{7,5},{8,10},{9,11},{10,... | collective-permute-start | bytes 3080 | tf_op jit(solution)/shard_map/ppermute | solution.py:335
  78.1 2.0 %collective-permute-start.7 = (f32[16,16]{1,0:T(8,128)}, f32[16,16]{1,0:T(8,128)S(1)}, u32[]{:S(2)}, u32[]{:S(2)}) collective-permute-start(f32[16,16]{1,0:T(8,128)} %stations.1), channel_id=1, source_target_pairs={{0,3},{1,2},{2,1},{3,0},{4,7},{5,6},{6,5},{7,4},{8,11},{9,10},{10,... | collective-permute-start | bytes 3080 | tf_op jit(solution)/shard_map/ppermute | solution.py:335
  80.2 0.0 collective-permute-start.5
  80.2 0.7 collective-permute-done.6
  80.9 1.2 %collective-permute-done.7 = f32[16,16]{1,0:T(8,128)S(1)} collective-permute-done((f32[16,16]{1,0:T(8,128)}, f32[16,16]{1,0:T(8,128)S(1)}, u32[]{:S(2)}, u32[]{:S(2)}) %collective-permute-start.7) | collective-permute-done | bytes 1056 | tf_op jit(solution)/shard_map/ppermute | solution.py:335
  82.0 2.0 %collective-permute-done.5 = f32[16,16]{1,0:T(8,128)S(1)} collective-permute-done((f32[16,16]{1,0:T(8,128)}, f32[16,16]{1,0:T(8,128)S(1)}, u32[]{:S(2)}, u32[]{:S(2)}) %collective-permute-start.5) | collective-permute-done | bytes 1056 | tf_op jit(solution)/shard_map/ppermute | solution.py:335
  84.0 1.3 %add_add_fusion = f32[16,16]{1,0:T(8,128)} fusion(f32[16,16]{1,0:T(8,128)S(1)} %collective-permute-done.6, f32[16,16]{1,0:T(8,128)S(1)} %collective-permute-done.7, f32[16,16]{1,0:T(8,128)} %stations.1, f32[16,16]{1,0:T(8,128)S(1)} %collective-permute-done.5), kind=kLoop, calls=%fused_computation.5 | loop fusion | flops 768 | bytes 5120 | tf_op jit(solution)/shard_map/add | solution.py:336
  (4 shorter events, 0.1 us)
Async XLA Ops:
  2.2 8.8 %collective-permute-start = (bf16[6,8,3584]{2,1,0:T(8,128)(2,1)}, bf16[6,8,3584]{2,1,0:T(8,128)(2,1)S(1)}, u32[]{:S(2)}, u32[]{:S(2)}) collective-permute-start(bf16[6,8,3584]{2,1,0:T(8,128)(2,1)} %get-tuple-element.16), channel_id=1, source_target_pairs={{0,4},{4,8},{8,12},{12,16},{16,20},{20,24},{24,28},{28,32},{32,36}... | collective-permute-start | bytes 1032200 | tf_op jit(solution)/shard_map/ppermute | solution.py:263
  4.0 7.1 %collective-permute-start.1 = (bf16[6,8,3584]{2,1,0:T(8,128)(2,1)}, bf16[6,8,3584]{2,1,0:T(8,128)(2,1)S(1)}, u32[]{:S(2)}, u32[]{:S(2)}) collective-permute-start(bf16[6,8,3584]{2,1,0:T(8,128)(2,1)} %get-tuple-element.17), channel_id=1, source_target_pairs={{4,0},{8,4},{12,8},{16,12},{20,16},{24,20},{28,24},{32,28},{36,32}... | collective-permute-start | bytes 1032200 | tf_op jit(solution)/shard_map/ppermute | solution.py:264
  5.3 1.6 %copy-start.1 = (bf16[16,4,16384]{2,1,0:T(4,128)(2,1)S(1)}, bf16[16,4,16384]{2,1,0:T(4,128)(2,1)}, u32[]{:S(2)}) copy-start(bf16[16,4,16384]{2,1,0:T(4,128)(2,1)} %prints_hbm.1) | copy-start | bytes 6291460
  6.9 0.7 copy-start.3
  7.6 19.1 %copy-start.4 = (s32[1024,4,1]{0,2,1:T(1,128)S(1)}, s32[1024,4,1]{0,2,1:T(1,128)}, u32[]{:S(2)}) copy-start(s32[1024,4,1]{0,2,1:T(1,128)} %param.11) | copy-start | bytes 49156
  7.6 19.1 %copy-start.7 = (s32[1024,4]{0,1:T(4,128)S(1)}, s32[1024,4]{0,1:T(4,128)}, u32[]{:S(2)}) copy-start(s32[1024,4]{0,1:T(4,128)} %param.12) | copy-start | bytes 49156
  7.6 19.6 %copy-start = (bf16[4,32,3584]{2,1,0:T(8,128)(2,1)S(1)}, bf16[4,32,3584]{2,1,0:T(8,128)(2,1)}, u32[]{:S(2)}) copy-start(bf16[4,32,3584]{2,1,0:T(8,128)(2,1)} %flux_ref.3) | copy-start | bytes 2752516
  7.6 19.6 %copy-start.2 = (f32[32,3584]{1,0:T(8,128)S(1)}, f32[32,3584]{1,0:T(8,128)}, u32[]{:S(2)}) copy-start(f32[32,3584]{1,0:T(8,128)} %coef_ref.3) | copy-start | bytes 1376260
  7.6 19.6 %copy-start.5 = (s32[4]{0:T(128)S(1)}, s32[4]{0:T(128)}, u32[]{:S(2)}) copy-start(s32[4]{0:T(128)} %steps_ref.1) | copy-start | bytes 52
  11.0 16.1 %copy-start.6 = (s32[64]{0:T(128)}, s32[64]{0:T(128)S(1)}, u32[]{:S(2)}) copy-start(s32[64]{0:T(128)S(1)} %get-tuple-element.14.place_ref) | copy-start | bytes 772
  11.0 43.9 %all-to-all-start = ((bf16[64,16,512]{2,1,0:T(8,128)(2,1)}), bf16[64,16,512]{2,1,0:T(8,128)(2,1)S(1)}, u32[]{:S(2)}, u32[]{:S(2)}) async-start(bf16[64,16,512]{2,1,0:T(8,128)(2,1)} %get-tuple-element.18), calls=%async_computation | async-start | bytes 2097152 | tf_op jit(solution)/shard_map/all_to_all | solution.py:288
  36.4 9.2 %collective-permute-start.2 = (bf16[32,3584]{1,0:T(8,128)(2,1)}, bf16[32,3584]{1,0:T(8,128)(2,1)S(1)}, u32[]{:S(2)}, u32[]{:S(2)}) collective-permute-start(bf16[32,3584]{1,0:T(8,128)(2,1)} %get-tuple-element.20), channel_id=1, source_target_pairs={{0,3},{1,0},{2,1},{3,2},{4,7},{5,4},{6,5},{7,6},{8,11},{9,8},{10,9... | collective-permute-start | bytes 688136 | tf_op jit(solution)/shard_map/ppermute | solution.py:306
  39.3 10.9 %collective-permute-start.3 = (bf16[32,3584]{1,0:T(8,128)(2,1)}, bf16[32,3584]{1,0:T(8,128)(2,1)S(1)}, u32[]{:S(2)}, u32[]{:S(2)}) collective-permute-start(bf16[32,3584]{1,0:T(8,128)(2,1)} %get-tuple-element.21), channel_id=1, source_target_pairs={{0,2},{1,3},{2,0},{3,1},{4,6},{5,7},{6,4},{7,5},{8,10},{9,11},{10,... | collective-permute-start | bytes 688136 | tf_op jit(solution)/shard_map/ppermute | solution.py:306
  39.6 11.6 %collective-permute-start.4 = (bf16[32,3584]{1,0:T(8,128)(2,1)}, bf16[32,3584]{1,0:T(8,128)(2,1)S(1)}, u32[]{:S(2)}, u32[]{:S(2)}) collective-permute-start(bf16[32,3584]{1,0:T(8,128)(2,1)} %get-tuple-element.22), channel_id=1, source_target_pairs={{0,1},{1,2},{2,3},{3,0},{4,5},{5,6},{6,7},{7,4},{8,9},{9,10},{10,1... | collective-permute-start | bytes 688136 | tf_op jit(solution)/shard_map/ppermute | solution.py:306
  75.5 5.4 %collective-permute-start.6 = (f32[16,16]{1,0:T(8,128)}, f32[16,16]{1,0:T(8,128)S(1)}, u32[]{:S(2)}, u32[]{:S(2)}) collective-permute-start(f32[16,16]{1,0:T(8,128)} %stations.1), channel_id=1, source_target_pairs={{0,2},{1,3},{2,0},{3,1},{4,6},{5,7},{6,4},{7,5},{8,10},{9,11},{10,... | collective-permute-start | bytes 3080 | tf_op jit(solution)/shard_map/ppermute | solution.py:335
  78.1 3.9 %collective-permute-start.7 = (f32[16,16]{1,0:T(8,128)}, f32[16,16]{1,0:T(8,128)S(1)}, u32[]{:S(2)}, u32[]{:S(2)}) collective-permute-start(f32[16,16]{1,0:T(8,128)} %stations.1), channel_id=1, source_target_pairs={{0,3},{1,2},{2,1},{3,0},{4,7},{5,6},{6,5},{7,4},{8,11},{9,10},{10,... | collective-permute-start | bytes 3080 | tf_op jit(solution)/shard_map/ppermute | solution.py:335
  80.2 3.9 %collective-permute-start.5 = (f32[16,16]{1,0:T(8,128)}, f32[16,16]{1,0:T(8,128)S(1)}, u32[]{:S(2)}, u32[]{:S(2)}) collective-permute-start(f32[16,16]{1,0:T(8,128)} %stations.1), channel_id=1, source_target_pairs={{0,1},{1,0},{2,3},{3,2},{4,5},{5,4},{6,7},{7,6},{8,9},{9,8},{10,11... | collective-permute-start | bytes 3080 | tf_op jit(solution)/shard_map/ppermute | solution.py:335

commit v3 on v2

--- a/solution.py
+++ b/solution.py
@@ -84,18 +84,29 @@
         copy.wait()
 
 
-def edge_kernel(flux_ref, coef_ref, last_ref, first_ref):
+def edge_kernel(core_ref, flux_ref, coef_ref, away_ref, beside_ref):
     samples, rows, _ = flux_ref.shape
-    for ref, low in ((last_ref, rows - HALO), (first_ref, 0)):
+
+    def fill(ref, low):
         ref[0:samples] = flux_ref[:, low : low + HALO]
         coef = coef_ref[low : low + HALO]
         head = coef.astype(jnp.bfloat16)
         ref[samples] = head
         ref[samples + 1] = (coef - head.astype(jnp.float32)).astype(jnp.bfloat16)
 
+    @pl.when(core_ref[0] == 0)
+    def _():
+        fill(away_ref, 0)
+        fill(beside_ref, rows - HALO)
+
+    @pl.when(core_ref[0] == 1)
+    def _():
+        fill(away_ref, rows - HALO)
+        fill(beside_ref, 0)
+
 
 def diffuse_kernel(
-    own_ref, steps_ref, flux_ref, above_ref, below_ref, coef_ref,
+    own_ref, core_ref, steps_ref, flux_ref, away_ref, beside_ref, coef_ref,
     out0_hbm, out1_hbm, out2_hbm, out3_hbm, even_ref, odd_ref, coefs_ref, out_ref, sems,
 ):
     own = own_ref[0]
@@ -103,14 +114,16 @@
     strips = lon // LANES
     tall = rows + 2 * HALO
     edge = jnp.zeros((HALO, LANES), jnp.float32)
+    away = pl.multiple_of(core_ref[0] * (HALO + rows), 8)
+    near = pl.multiple_of((1 - core_ref[0]) * (HALO + rows), 8)
     lane = lax.broadcasted_iota(jnp.int32, (8, LANES), 1)
     first_lane = lane == 0
     last_lane = lane == LANES - 1
 
     for strip in range(strips):
         at = slice(strip * LANES, (strip + 1) * LANES)
-        for ref, low in ((above_ref, 0), (below_ref, HALO + rows)):
-            coefs_ref[strip, low : low + HALO] = ref[samples, :, at].astype(jnp.float32) + ref[
+        for ref, low in ((away_ref, away), (beside_ref, near)):
+            coefs_ref[strip, pl.ds(low, HALO)] = ref[samples, :, at].astype(jnp.float32) + ref[
                 samples + 1, :, at
             ].astype(jnp.float32)
         coefs_ref[strip, HALO : HALO + rows] = coef_ref[:, at]
@@ -152,9 +165,9 @@
     def begin(sample, ref):
         for strip in range(strips):
             at = slice(strip * LANES, (strip + 1) * LANES)
-            ref[strip, HALO : 2 * HALO] = above_ref[sample, :, at].astype(jnp.float32)
+            ref[strip, pl.ds(HALO + away, HALO)] = away_ref[sample, :, at].astype(jnp.float32)
             ref[strip, 2 * HALO : 2 * HALO + rows] = flux_ref[sample, :, at].astype(jnp.float32)
-            ref[strip, 2 * HALO + rows : HALO + tall] = below_ref[sample, :, at].astype(jnp.float32)
+            ref[strip, pl.ds(HALO + near, HALO)] = beside_ref[sample, :, at].astype(jnp.float32)
 
     def evolve(sample, carry):
         even = even_ref.at[sample]
@@ -250,18 +263,19 @@
     part = lax.axis_index("sample")
     own = part.astype(jnp.int32).reshape(1)
     cells = rows * TILE_LON // PARTS
-    down = [(i, i + 1) for i in range(bands - 1)]
-    up = [(i + 1, i) for i in range(bands - 1)]
-
-    last, first = pl.pallas_call(
+    core = lax.rem(band, 2).astype(jnp.int32).reshape(1)
+    across = [(i, i + 1) for i in range(1, bands - 1, 2)] + [(i, i - 1) for i in range(2, bands, 2)]
+    within = [(i, i ^ 1) for i in range(bands)]
+
+    away, beside = pl.pallas_call(
         edge_kernel,
         out_shape=[jax.ShapeDtypeStruct((samples + 2, HALO, lon), jnp.bfloat16)] * 2,
-        in_specs=[spec(VMEM)] * 2,
+        in_specs=[spec(SMEM)] + [spec(VMEM)] * 2,
         out_specs=[spec(VMEM)] * 2,
         name="edges",
-    )(flux, coeff)
-    above = lax.ppermute(last, "station", down)
-    below = lax.ppermute(first, "station", up)
+    )(core, flux, coeff)
+    away = lax.ppermute(away, "station", across)
+    beside = lax.ppermute(beside, "station", within)
 
     src_all = tile_src[:, :, 0].T
     sent, place = pl.pallas_call(
@@ -283,14 +297,19 @@
         ],
         compiler_params=pltpu.CompilerParams(vmem_limit_bytes=24 * 2**20),
         name="pack",
-    )(own, band.astype(jnp.int32).reshape(1), tile_src.transpose(1, 2, 0), footprint)
-    sent, _, _ = lax.optimization_barrier((sent, above, below))
+    )(
+        own,
+        band.astype(jnp.int32).reshape(1),
+        pltpu.with_memory_space_constraint(tile_src.transpose(1, 2, 0), HBM),
+        pltpu.with_memory_space_constraint(footprint, HBM),
+    )
+    sent, _, _ = lax.optimization_barrier((sent, away, beside))
     arrived = lax.all_to_all(sent, "station", split_axis=0, concat_axis=0, tiled=True)
 
     finals = pl.pallas_call(
         diffuse_kernel,
         out_shape=[jax.ShapeDtypeStruct((samples * 8, lon), jnp.bfloat16)] * PARTS,
-        in_specs=[spec(SMEM), spec(SMEM)] + [spec(VMEM)] * 4,
+        in_specs=[spec(SMEM)] * 3 + [spec(VMEM)] * 4,
         out_specs=[spec(HBM)] * PARTS,
         scratch_shapes=[
             VMEM((samples, lon // LANES, rows + 4 * HALO, LANES), jnp.float32),
@@ -301,7 +320,7 @@
         ],
         compiler_params=pltpu.CompilerParams(vmem_limit_bytes=24 * 2**20),
         name="diffuse",
-    )(own, diff_steps, flux, above, below, coeff)
+    )(own, core, diff_steps, flux, away, beside, coeff)
     parts = [finals[0]] + [
         lax.ppermute(finals[turn], "sample", [(i, (i + turn) % PARTS) for i in range(PARTS)]) for turn in (3, 2, 1)
     ]

time: 86.2 us -> 84.3 us (0.978)
  local copies, waits for them, and re-layouts: 2.71 us -> 0.97 us
  waiting for transfers between devices: 16.5 us -> 14.8 us
  blocking collectives: 16.3 us -> 17.8 us
  starting transfers between devices: 28.9 us -> 30.1 us
    ppermute x3, starting transfers between devices: 5.52 us -> 7.74 us  [body(): lax.ppermute(finals[turn], 'sample', [(i, (i + turn) % PARTS) for i in ra...]
    all_to_all x1, starting transfers between devices: 15.7 us -> 13.7 us  [body(): lax.all_to_all(sent, 'station', split_axis=0, concat_axis=0, tiled=True)]
    unnamed x16 -> x12, local copies, waits for them, and re-layouts: 2.33 us -> 0.59 us
    all_to_all x1, waiting for transfers between devices: 3.7 us -> 2.26 us  [body(): lax.all_to_all(sent, 'station', split_axis=0, concat_axis=0, tiled=True)]
    all_to_all x1, blocking collectives: 16.3 us -> 17.8 us  [body(): lax.all_to_all(values.reshape(bands, CAP, LANES), 'station', split_axis=0...]
    ppermute x2, starting transfers between devices: 3.04 us -> 4.02 us  [the longest x1 3.34 us: body(): beside = lax.ppermute(beside, 'station', within)]
  transfers between devices with their start and end apart: 9 -> 9, of which waited for: 7 -> 7; matrix products, arithmetic and copies ran while one was open for 1% -> 1% of each run, Pallas kernels for 15% -> 14%
where the time goes in v3:
time: 84.3 us; the launch traced here: 83.9 us
  starting transfers between devices  30.1 us (36%)
  Pallas kernels  18.5 us (22%)
  blocking collectives  17.8 us (21%)
  waiting for transfers between devices  14.8 us (18%)
  other arithmetic  1.59 us (2%)
  local copies, waits for them, and re-layouts  0.97 us (1%)
    all_to_all x1, blocking collectives, body(): lax.all_to_all(values.reshape(bands, CAP, LANES), 'station', split_axis=0...  17.8 us
    all_to_all x1, starting transfers between devices, body(): lax.all_to_all(sent, 'station', split_axis=0, concat_axis=0, tiled=True)  13.7 us
    ppermute x3, waiting for transfers between devices, body(): lax.ppermute(finals[turn], 'sample', [(i, (i + turn) % PARTS) for i in ra...  8.99 us
    pallas_call x1, Pallas kernels, body(): pl.pallas_call(diffuse_kernel, out_shape=[jax.ShapeDtypeStruct((samples *...  8.44 us
    ppermute x3, starting transfers between devices, body(): lax.ppermute(finals[turn], 'sample', [(i, (i + turn) % PARTS) for i in ra...  7.74 us
    ppermute x3, starting transfers between devices, body(): lax.ppermute(share, 'sample', [(i, i ^ flip) for i in range(PARTS)])  4.7 us
    pallas_call x1, Pallas kernels, body(): pl.pallas_call(pack_kernel, out_shape=(jax.ShapeDtypeStruct((bands, 8 * C...  3.59 us
    ppermute x3, waiting for transfers between devices, body(): lax.ppermute(share, 'sample', [(i, i ^ flip) for i in range(PARTS)])  3.54 us
  transfers between devices with their start and end apart: 9, of which 7 were waited for; matrix products, arithmetic and copies ran while one was open for 1% of the time, Pallas kernels for 14%

profile of v3, /device:TPU:8, one launch (start us, length us, event | category | flops | bytes accessed | tf_op | source)
XLA Modules:
  0.0 83.9 jit_solution(14959645308980152091)
XLA Ops:
  0.0 2.2 %edges.1 = (bf16[6,8,3584]{2,1,0:T(8,128)(2,1)}, bf16[6,8,3584]{2,1,0:T(8,128)(2,1)}) custom-call(s32[1]{0:T(128)} %bitcast.9.core_ref, bf16[4,32,3584]{2,1,0:T(8,128)(2,1)} %flux_ref.3, f32[32,3584]{1,0:T(8,128)} %coef_ref.3), custom_call_target="tpu_custom_call" | custom-call | tf_op jit(solution)/shard_map/edges/pallas_call | solution.py:270
  2.2 0.7 collective-permute-start
  2.9 3.3 %collective-permute-start.1 = (bf16[6,8,3584]{2,1,0:T(8,128)(2,1)}, bf16[6,8,3584]{2,1,0:T(8,128)(2,1)S(1)}, u32[]{:S(2)}, u32[]{:S(2)}) collective-permute-start(bf16[6,8,3584]{2,1,0:T(8,128)(2,1)} %get-tuple-element.17), channel_id=1, source_target_pairs={{0,4},{4,0},{8,12},{12,8},{16,20},{20,16},{24,28},{28,24},{32,36},... | collective-permute-start | bytes 1032200 | tf_op jit(solution)/shard_map/ppermute | solution.py:278
  6.3 0.0 copy-start.4
  6.3 0.0 copy-start.5
  6.3 0.0 copy-start
  6.3 0.0 copy-start.1
  6.3 0.0 copy-start.3
  6.3 3.6 %pack.1 = (bf16[64,16,512]{2,1,0:T(8,128)(2,1)}, s32[64]{0:T(128)S(1)}) custom-call(s32[1]{0:T(128)} %bitcast.part_ref.own_ref, s32[1]{0:T(128)} %bitcast.1.band_ref, s32[4,1,1024]{2,1,0:T(1,128)} %bitcast.22, bf16[16,4,16384]{2,1,0:T(4,128)(2,1)} %prints_hbm.1), custom_call_target="tpu_custom_call" | custom-call | tf_op jit(solution)/shard_map/pack/pallas_call | solution.py:281
  9.9 0.0 copy-start.2
  9.9 0.6 copy-done.2
  10.5 0.0 collective-permute-done.away_ref
  10.5 0.0 collective-permute-done.1.beside_ref
  10.5 13.7 %all-to-all-start = ((bf16[64,16,512]{2,1,0:T(8,128)(2,1)}), bf16[64,16,512]{2,1,0:T(8,128)(2,1)S(1)}, u32[]{:S(2)}, u32[]{:S(2)}) async-start(bf16[64,16,512]{2,1,0:T(8,128)(2,1)} %get-tuple-element.18), calls=%async_computation | async-start | bytes 2097152 | tf_op jit(solution)/shard_map/all_to_all | solution.py:307
  24.2 0.0 copy-done.4
  24.2 0.0 copy-done.5
  24.2 0.1 reshape.58
  24.3 0.1 reshape.57
  24.4 0.1 reduce_max.19
  24.5 0.1 reduce_min.19
  24.6 0.0 copy-done
  24.6 0.0 copy-done.1
  24.6 0.0 copy-done.3
  24.6 8.4 %diffuse.1 = (bf16[32,3584]{1,0:T(8,128)(2,1)S(1)}, bf16[32,3584]{1,0:T(8,128)(2,1)}, bf16[32,3584]{1,0:T(8,128)(2,1)}, bf16[32,3584]{1,0:T(8,128)(2,1)}) custom-call(s32[1]{0:T(128)} %bitcast.part_ref.own_ref, s32[1]{0:T(128)} %bitcast.9.core_ref, s32[4]{0:T(128)S(1)} %copy-done.3, bf16[4,32,3584]{2,1,0:T(8,128)(2,1)S(1)} %copy-done, ...), custom_call_target="tpu_custom_call" | custom-call | tf_op jit(solution)/shard_map/diffuse/pallas_call | solution.py:309
  33.1 2.3 %collective-permute-start.2 = (bf16[32,3584]{1,0:T(8,128)(2,1)}, bf16[32,3584]{1,0:T(8,128)(2,1)S(1)}, u32[]{:S(2)}, u32[]{:S(2)}) collective-permute-start(bf16[32,3584]{1,0:T(8,128)(2,1)} %get-tuple-element.20), channel_id=1, source_target_pairs={{0,3},{1,0},{2,1},{3,2},{4,7},{5,4},{6,5},{7,6},{8,11},{9,8},{10,9... | collective-permute-start | bytes 688136 | tf_op jit(solution)/shard_map/ppermute | solution.py:325
  35.4 2.9 %collective-permute-start.3 = (bf16[32,3584]{1,0:T(8,128)(2,1)}, bf16[32,3584]{1,0:T(8,128)(2,1)S(1)}, u32[]{:S(2)}, u32[]{:S(2)}) collective-permute-start(bf16[32,3584]{1,0:T(8,128)(2,1)} %get-tuple-element.21), channel_id=1, source_target_pairs={{0,2},{1,3},{2,0},{3,1},{4,6},{5,7},{6,4},{7,5},{8,10},{9,11},{10,... | collective-permute-start | bytes 688136 | tf_op jit(solution)/shard_map/ppermute | solution.py:325
  38.3 2.5 %collective-permute-start.4 = (bf16[32,3584]{1,0:T(8,128)(2,1)}, bf16[32,3584]{1,0:T(8,128)(2,1)S(1)}, u32[]{:S(2)}, u32[]{:S(2)}) collective-permute-start(bf16[32,3584]{1,0:T(8,128)(2,1)} %get-tuple-element.22), channel_id=1, source_target_pairs={{0,1},{1,2},{2,3},{3,0},{4,5},{5,6},{6,7},{7,4},{8,9},{9,10},{10,1... | collective-permute-start | bytes 688136 | tf_op jit(solution)/shard_map/ppermute | solution.py:325
  40.9 0.1 copy.11
  41.0 0.1 reshape.59.loc_ref
  41.1 1.5 %collective-permute-done.2.refs_1_ = bf16[32,3584]{1,0:T(8,128)(2,1)S(1)} collective-permute-done((bf16[32,3584]{1,0:T(8,128)(2,1)}, bf16[32,3584]{1,0:T(8,128)(2,1)S(1)}, u32[]{:S(2)}, u32[]{:S(2)}) %collective-permute-start.2) | collective-permute-done | bytes 229408 | tf_op jit(solution)/shard_map/ppermute | solution.py:325
  42.6 6.6 %collective-permute-done.3.refs_2_ = bf16[32,3584]{1,0:T(8,128)(2,1)S(1)} collective-permute-done((bf16[32,3584]{1,0:T(8,128)(2,1)}, bf16[32,3584]{1,0:T(8,128)(2,1)S(1)}, u32[]{:S(2)}, u32[]{:S(2)}) %collective-permute-start.3) | collective-permute-done | bytes 229408 | tf_op jit(solution)/shard_map/ppermute | solution.py:325
  49.2 0.9 %collective-permute-done.4.refs_3_ = bf16[32,3584]{1,0:T(8,128)(2,1)S(1)} collective-permute-done((bf16[32,3584]{1,0:T(8,128)(2,1)}, bf16[32,3584]{1,0:T(8,128)(2,1)S(1)}, u32[]{:S(2)}, u32[]{:S(2)}) %collective-permute-start.4) | collective-permute-done | bytes 229408 | tf_op jit(solution)/shard_map/ppermute | solution.py:325
  50.1 2.3 %all-to-all-done.prints_ref = bf16[64,16,512]{2,1,0:T(8,128)(2,1)S(1)} async-done(((bf16[64,16,512]{2,1,0:T(8,128)(2,1)}), bf16[64,16,512]{2,1,0:T(8,128)(2,1)S(1)}, u32[]{:S(2)}, u32[]{:S(2)}) %all-to-all-start) | async-done | bytes 1048608 | tf_op jit(solution)/shard_map/all_to_all | solution.py:307
  52.3 2.6 %dots.1 = f32[128,128]{1,0:T(8,128)S(1)} custom-call(s32[1]{0:T(128)} %bitcast.part_ref.own_ref, s32[128]{0:T(128)S(1)} %reshape.59.loc_ref, bf16[64,16,512]{2,1,0:T(8,128)(2,1)S(1)} %all-to-all-done.prints_ref, bf16[32,3584]{1,0:T(8,128)(2,1)S(1)} %get-tuple-element.19.refs_0_, bf16[32,3584]{1,0:T(8,128)(2,1)S(1)} %collective-permute-done.2.refs_1_, ...), custom_call_target="tpu_custom_call" | custom-call | tf_op jit(solution)/shard_map/dots/pallas_call | solution.py:335
  54.9 17.8 %all_to_all.10 = f32[64,2,128]{2,1,0:T(2,128)} all-to-all(f32[64,2,128]{2,1,0:T(2,128)S(1)} %bitcast.20), channel_id=1, replica_groups=mesh['station'=64,'sample'=4] {'station'}, dimensions={0} | all-to-all | bytes 131072 | tf_op jit(solution)/shard_map/all_to_all | solution.py:345
  72.7 1.7 %stations.1 = f32[16,16]{1,0:T(8,128)} custom-call(s32[64]{0:T(128)} %copy-done.2, s32[16]{0:T(128)} %count_ref.1, f32[128,128]{1,0:T(8,128)} %bitcast.21), custom_call_target="tpu_custom_call" | custom-call | tf_op jit(solution)/shard_map/stations/pallas_call | solution.py:346
  74.4 2.6 %collective-permute-start.6 = (f32[16,16]{1,0:T(8,128)}, f32[16,16]{1,0:T(8,128)S(1)}, u32[]{:S(2)}, u32[]{:S(2)}) collective-permute-start(f32[16,16]{1,0:T(8,128)} %stations.1), channel_id=1, source_target_pairs={{0,2},{1,3},{2,0},{3,1},{4,6},{5,7},{6,4},{7,5},{8,10},{9,11},{10,... | collective-permute-start | bytes 3080 | tf_op jit(solution)/shard_map/ppermute | solution.py:354
  77.0 1.7 %collective-permute-start.7 = (f32[16,16]{1,0:T(8,128)}, f32[16,16]{1,0:T(8,128)S(1)}, u32[]{:S(2)}, u32[]{:S(2)}) collective-permute-start(f32[16,16]{1,0:T(8,128)} %stations.1), channel_id=1, source_target_pairs={{0,3},{1,2},{2,1},{3,0},{4,7},{5,6},{6,5},{7,4},{8,11},{9,10},{10,... | collective-permute-start | bytes 3080 | tf_op jit(solution)/shard_map/ppermute | solution.py:354
  78.8 0.3 collective-permute-start.5
  79.1 0.7 collective-permute-done.6
  79.8 1.1 %collective-permute-done.7 = f32[16,16]{1,0:T(8,128)S(1)} collective-permute-done((f32[16,16]{1,0:T(8,128)}, f32[16,16]{1,0:T(8,128)S(1)}, u32[]{:S(2)}, u32[]{:S(2)}) %collective-permute-start.7) | collective-permute-done | bytes 1056 | tf_op jit(solution)/shard_map/ppermute | solution.py:354
  80.9 1.7 %collective-permute-done.5 = f32[16,16]{1,0:T(8,128)S(1)} collective-permute-done((f32[16,16]{1,0:T(8,128)}, f32[16,16]{1,0:T(8,128)S(1)}, u32[]{:S(2)}, u32[]{:S(2)}) %collective-permute-start.5) | collective-permute-done | bytes 1056 | tf_op jit(solution)/shard_map/ppermute | solution.py:354
  82.6 1.3 %add_add_fusion = f32[16,16]{1,0:T(8,128)} fusion(f32[16,16]{1,0:T(8,128)S(1)} %collective-permute-done.6, f32[16,16]{1,0:T(8,128)S(1)} %collective-permute-done.7, f32[16,16]{1,0:T(8,128)} %stations.1, f32[16,16]{1,0:T(8,128)S(1)} %collective-permute-done.5), kind=kLoop, calls=%fused_computation.5 | loop fusion | flops 768 | bytes 5120 | tf_op jit(solution)/shard_map/add | solution.py:355
  (4 shorter events, 0.1 us)
Async XLA Ops:
  2.2 8.2 %collective-permute-start = (bf16[6,8,3584]{2,1,0:T(8,128)(2,1)}, bf16[6,8,3584]{2,1,0:T(8,128)(2,1)S(1)}, u32[]{:S(2)}, u32[]{:S(2)}) collective-permute-start(bf16[6,8,3584]{2,1,0:T(8,128)(2,1)} %get-tuple-element.16), channel_id=1, source_target_pairs={{4,8},{12,16},{20,24},{28,32},{36,40},{44,48},{52,56},{60,64},{68,... | collective-permute-start | bytes 1032200 | tf_op jit(solution)/shard_map/ppermute | solution.py:277
  2.9 7.6 %collective-permute-start.1 = (bf16[6,8,3584]{2,1,0:T(8,128)(2,1)}, bf16[6,8,3584]{2,1,0:T(8,128)(2,1)S(1)}, u32[]{:S(2)}, u32[]{:S(2)}) collective-permute-start(bf16[6,8,3584]{2,1,0:T(8,128)(2,1)} %get-tuple-element.17), channel_id=1, source_target_pairs={{0,4},{4,0},{8,12},{12,8},{16,20},{20,16},{24,28},{28,24},{32,36},... | collective-permute-start | bytes 1032200 | tf_op jit(solution)/shard_map/ppermute | solution.py:278
  6.3 17.9 %copy-start.4 = (s32[1024,4,1]{0,2,1:T(1,128)S(1)}, s32[1024,4,1]{0,2,1:T(1,128)}, u32[]{:S(2)}) copy-start(s32[1024,4,1]{0,2,1:T(1,128)} %param.11) | copy-start | bytes 49156
  6.3 17.9 %copy-start.5 = (s32[1024,4]{0,1:T(4,128)S(1)}, s32[1024,4]{0,1:T(4,128)}, u32[]{:S(2)}) copy-start(s32[1024,4]{0,1:T(4,128)} %param.12) | copy-start | bytes 49156
  6.3 18.4 %copy-start = (bf16[4,32,3584]{2,1,0:T(8,128)(2,1)S(1)}, bf16[4,32,3584]{2,1,0:T(8,128)(2,1)}, u32[]{:S(2)}) copy-start(bf16[4,32,3584]{2,1,0:T(8,128)(2,1)} %flux_ref.3) | copy-start | bytes 2752516
  6.3 18.4 %copy-start.1 = (f32[32,3584]{1,0:T(8,128)S(1)}, f32[32,3584]{1,0:T(8,128)}, u32[]{:S(2)}) copy-start(f32[32,3584]{1,0:T(8,128)} %coef_ref.3) | copy-start | bytes 1376260
  6.3 18.4 %copy-start.3 = (s32[4]{0:T(128)S(1)}, s32[4]{0:T(128)}, u32[]{:S(2)}) copy-start(s32[4]{0:T(128)} %steps_ref.1) | copy-start | bytes 52
  9.9 0.6 copy-start.2
  10.5 41.9 %all-to-all-start = ((bf16[64,16,512]{2,1,0:T(8,128)(2,1)}), bf16[64,16,512]{2,1,0:T(8,128)(2,1)S(1)}, u32[]{:S(2)}, u32[]{:S(2)}) async-start(bf16[64,16,512]{2,1,0:T(8,128)(2,1)} %get-tuple-element.18), calls=%async_computation | async-start | bytes 2097152 | tf_op jit(solution)/shard_map/all_to_all | solution.py:307
  33.1 9.5 %collective-permute-start.2 = (bf16[32,3584]{1,0:T(8,128)(2,1)}, bf16[32,3584]{1,0:T(8,128)(2,1)S(1)}, u32[]{:S(2)}, u32[]{:S(2)}) collective-permute-start(bf16[32,3584]{1,0:T(8,128)(2,1)} %get-tuple-element.20), channel_id=1, source_target_pairs={{0,3},{1,0},{2,1},{3,2},{4,7},{5,4},{6,5},{7,6},{8,11},{9,8},{10,9... | collective-permute-start | bytes 688136 | tf_op jit(solution)/shard_map/ppermute | solution.py:325
  35.4 13.7 %collective-permute-start.3 = (bf16[32,3584]{1,0:T(8,128)(2,1)}, bf16[32,3584]{1,0:T(8,128)(2,1)S(1)}, u32[]{:S(2)}, u32[]{:S(2)}) collective-permute-start(bf16[32,3584]{1,0:T(8,128)(2,1)} %get-tuple-element.21), channel_id=1, source_target_pairs={{0,2},{1,3},{2,0},{3,1},{4,6},{5,7},{6,4},{7,5},{8,10},{9,11},{10,... | collective-permute-start | bytes 688136 | tf_op jit(solution)/shard_map/ppermute | solution.py:325
  38.3 11.8 %collective-permute-start.4 = (bf16[32,3584]{1,0:T(8,128)(2,1)}, bf16[32,3584]{1,0:T(8,128)(2,1)S(1)}, u32[]{:S(2)}, u32[]{:S(2)}) collective-permute-start(bf16[32,3584]{1,0:T(8,128)(2,1)} %get-tuple-element.22), channel_id=1, source_target_pairs={{0,1},{1,2},{2,3},{3,0},{4,5},{5,6},{6,7},{7,4},{8,9},{9,10},{10,1... | collective-permute-start | bytes 688136 | tf_op jit(solution)/shard_map/ppermute | solution.py:325
  74.4 5.4 %collective-permute-start.6 = (f32[16,16]{1,0:T(8,128)}, f32[16,16]{1,0:T(8,128)S(1)}, u32[]{:S(2)}, u32[]{:S(2)}) collective-permute-start(f32[16,16]{1,0:T(8,128)} %stations.1), channel_id=1, source_target_pairs={{0,2},{1,3},{2,0},{3,1},{4,6},{5,7},{6,4},{7,5},{8,10},{9,11},{10,... | collective-permute-start | bytes 3080 | tf_op jit(solution)/shard_map/ppermute | solution.py:354
  77.0 3.9 %collective-permute-start.7 = (f32[16,16]{1,0:T(8,128)}, f32[16,16]{1,0:T(8,128)S(1)}, u32[]{:S(2)}, u32[]{:S(2)}) collective-permute-start(f32[16,16]{1,0:T(8,128)} %stations.1), channel_id=1, source_target_pairs={{0,3},{1,2},{2,1},{3,0},{4,7},{5,6},{6,5},{7,4},{8,11},{9,10},{10,... | collective-permute-start | bytes 3080 | tf_op jit(solution)/shard_map/ppermute | solution.py:354
  78.8 3.9 %collective-permute-start.5 = (f32[16,16]{1,0:T(8,128)}, f32[16,16]{1,0:T(8,128)S(1)}, u32[]{:S(2)}, u32[]{:S(2)}) collective-permute-start(f32[16,16]{1,0:T(8,128)} %stations.1), channel_id=1, source_target_pairs={{0,1},{1,0},{2,3},{3,2},{4,5},{5,4},{6,7},{7,6},{8,9},{9,8},{10,11... | collective-permute-start | bytes 3080 | tf_op jit(solution)/shard_map/ppermute | solution.py:354

commit v4 on v3

--- a/solution.py
+++ b/solution.py
@@ -23,16 +23,16 @@
 
 
 def pack_kernel(
-    part_ref, band_ref, src_hbm, prints_hbm, sent_hbm, place_ref,
+    src_hbm, prints_hbm, sent_hbm, place_ref,
     src_ref, held_ref, slot_ref, prints_ref, hot_ref, sent_ref, sems,
 ):
     bands, _, width = sent_ref.shape
     stations, _, cells = prints_ref.shape
     slots = stations * KT
-    low = pl.multiple_of(part_ref[0] * cells, cells)
+    low = pl.multiple_of(lax.axis_index("sample") * cells, cells)
     prints_in = pltpu.make_async_copy(prints_hbm.at[:, :, pl.ds(low, cells)], prints_ref, sems.at[0])
     prints_in.start()
-    first = band_ref[0] * stations
+    first = lax.axis_index("station") * stations
     low = pl.multiple_of(lax.div(first, LANES) * LANES, LANES)
     src_in = pltpu.make_async_copy(src_hbm.at[:, :, pl.ds(low, LANES)], src_ref, sems.at[1])
     src_in.start()
@@ -281,10 +281,10 @@
     sent, place = pl.pallas_call(
         pack_kernel,
         out_shape=(
-            jax.ShapeDtypeStruct((bands, 8 * CAP, TILE_LON), jnp.bfloat16),
-            jax.ShapeDtypeStruct((slots,), jnp.int32),
+            HBM((bands, 8 * CAP, TILE_LON), jnp.bfloat16),
+            HBM((slots,), jnp.int32),
         ),
-        in_specs=[spec(SMEM), spec(SMEM), spec(HBM), spec(HBM)],
+        in_specs=[spec(HBM), spec(HBM)],
         out_specs=(spec(HBM), spec(SMEM)),
         scratch_shapes=[
             SMEM((KT, 1, LANES), jnp.int32),
@@ -298,8 +298,6 @@
         compiler_params=pltpu.CompilerParams(vmem_limit_bytes=24 * 2**20),
         name="pack",
     )(
-        own,
-        band.astype(jnp.int32).reshape(1),
         pltpu.with_memory_space_constraint(tile_src.transpose(1, 2, 0), HBM),
         pltpu.with_memory_space_constraint(footprint, HBM),
     )
@@ -308,7 +306,7 @@
 
     finals = pl.pallas_call(
         diffuse_kernel,
-        out_shape=[jax.ShapeDtypeStruct((samples * 8, lon), jnp.bfloat16)] * PARTS,
+        out_shape=[HBM((samples * 8, lon), jnp.bfloat16)] * PARTS,
         in_specs=[spec(SMEM)] * 3 + [spec(VMEM)] * 4,
         out_specs=[spec(HBM)] * PARTS,
         scratch_shapes=[
@@ -325,8 +323,9 @@
         lax.ppermute(finals[turn], "sample", [(i, (i + turn) % PARTS) for i in range(PARTS)]) for turn in (3, 2, 1)
     ]
 
+    local, _ = lax.optimization_barrier((tile_local, finals[0]))
     order = jnp.arange(stations * bands, dtype=jnp.int32) % stations
-    code = (order[None, :] * KT + jnp.arange(KT, dtype=jnp.int32)[:, None]) * 8 + tile_local.T
+    code = (order[None, :] * KT + jnp.arange(KT, dtype=jnp.int32)[:, None]) * 8 + local.T
     named = src_all == band
     first = jnp.min(jnp.min(jnp.where(named, code, slots * 8), axis=0).reshape(bands, stations), axis=1)
     last = jnp.max(jnp.max(jnp.where(named, code, 0), axis=0).reshape(bands, stations), axis=1)

time: 84.3 us -> 85.3 us (1.012)
  Pallas kernels: 18.5 us -> 21.8 us
  starting transfers between devices: 30.1 us -> 27.2 us
    ppermute x3, starting transfers between devices: 7.74 us -> 4.43 us  [body(): lax.ppermute(finals[turn], 'sample', [(i, (i + turn) % PARTS) for i in ra...]
    pallas_call x2, Pallas kernels: 12 us -> 15.3 us  [the longest x1 11.8 us: body(): pl.pallas_call(diffuse_kernel, out_shape=[HBM((samples * 8, lon), jnp.bfl...]
  transfers between devices with their start and end apart: 9 -> 9, of which waited for: 7 -> 6; matrix products, arithmetic and copies ran while one was open for 1% -> 1% of each run, Pallas kernels for 14% -> 18%
where the time goes in v4:
time: 85.3 us; the launch traced here: 85.6 us
  starting transfers between devices  27.2 us (32%)
  Pallas kernels  21.8 us (26%)
  blocking collectives  18.4 us (22%)
  waiting for transfers between devices  15.1 us (18%)
  other arithmetic  1.58 us (2%)
  local copies, waits for them, and re-layouts  1.34 us (2%)
    all_to_all x1, blocking collectives, body(): lax.all_to_all(values.reshape(bands, CAP, LANES), 'station', split_axis=0...  18.4 us
    all_to_all x1, starting transfers between devices, body(): lax.all_to_all(sent, 'station', split_axis=0, concat_axis=0, tiled=True)  14.3 us
    pallas_call x1, Pallas kernels, body(): pl.pallas_call(diffuse_kernel, out_shape=[HBM((samples * 8, lon), jnp.bfl...  11.8 us
    ppermute x3, waiting for transfers between devices, body(): lax.ppermute(finals[turn], 'sample', [(i, (i + turn) % PARTS) for i in ra...  9.61 us
    ppermute x3, starting transfers between devices, body(): lax.ppermute(finals[turn], 'sample', [(i, (i + turn) % PARTS) for i in ra...  4.43 us
    ppermute x3, starting transfers between devices, body(): lax.ppermute(share, 'sample', [(i, i ^ flip) for i in range(PARTS)])  4.42 us
    ppermute x3, waiting for transfers between devices, body(): lax.ppermute(share, 'sample', [(i, i ^ flip) for i in range(PARTS)])  3.86 us
    pallas_call x1, Pallas kernels, body(): pl.pallas_call(pack_kernel, out_shape=(HBM((bands, 8 * CAP, TILE_LON), jn...  3.5 us
  transfers between devices with their start and end apart: 9, of which 6 were waited for; matrix products, arithmetic and copies ran while one was open for 1% of the time, Pallas kernels for 18%

profile of v4, /device:TPU:8, one launch (start us, length us, event | category | flops | bytes accessed | tf_op | source)
XLA Modules:
  0.0 85.6 jit_solution(8271357172656955312)
XLA Ops:
  0.0 2.2 %edges.1 = (bf16[6,8,3584]{2,1,0:T(8,128)(2,1)}, bf16[6,8,3584]{2,1,0:T(8,128)(2,1)}) custom-call(s32[1]{0:T(128)} %bitcast.4.core_ref, bf16[4,32,3584]{2,1,0:T(8,128)(2,1)} %flux_ref.3, f32[32,3584]{1,0:T(8,128)} %coef_ref.3), custom_call_target="tpu_custom_call" | custom-call | tf_op jit(solution)/shard_map/edges/pallas_call | solution.py:270
  2.2 0.7 collective-permute-start
  2.9 3.3 %collective-permute-start.1 = (bf16[6,8,3584]{2,1,0:T(8,128)(2,1)}, bf16[6,8,3584]{2,1,0:T(8,128)(2,1)S(1)}, u32[]{:S(2)}, u32[]{:S(2)}) collective-permute-start(bf16[6,8,3584]{2,1,0:T(8,128)(2,1)} %get-tuple-element.17), channel_id=1, source_target_pairs={{0,4},{4,0},{8,12},{12,8},{16,20},{20,16},{24,28},{28,24},{32,36},... | collective-permute-start | bytes 1032200 | tf_op jit(solution)/shard_map/ppermute | solution.py:278
  6.3 0.0 copy-start
  6.3 0.0 copy-start.1
  6.3 0.0 copy-start.3
  6.3 3.5 %pack.1 = (bf16[64,16,512]{2,1,0:T(8,128)(2,1)}, s32[64]{0:T(128)}) custom-call(s32[4,1,1024]{2,1,0:T(1,128)} %bitcast.21, bf16[16,4,16384]{2,1,0:T(4,128)(2,1)} %prints_hbm.1), custom_call_target="tpu_custom_call" | custom-call | tf_op jit(solution)/shard_map/pack/pallas_call | solution.py:281
  9.8 0.0 copy-start.4
  9.8 0.0 copy-start.5
  9.8 0.0 collective-permute-done.away_ref
  9.8 0.0 collective-permute-done.1.beside_ref
  9.8 14.3 %all-to-all-start = ((bf16[64,16,512]{2,1,0:T(8,128)(2,1)}), bf16[64,16,512]{2,1,0:T(8,128)(2,1)S(1)}, u32[]{:S(2)}, u32[]{:S(2)}) async-start(bf16[64,16,512]{2,1,0:T(8,128)(2,1)} %get-tuple-element.21), calls=%async_computation | async-start | bytes 2097152 | tf_op jit(solution)/shard_map/all_to_all | solution.py:305
  24.2 0.0 copy-done
  24.2 0.0 copy-done.1
  24.2 0.0 copy-done.3
  24.2 11.8 %diffuse.1 = (bf16[32,3584]{1,0:T(8,128)(2,1)}, bf16[32,3584]{1,0:T(8,128)(2,1)}, bf16[32,3584]{1,0:T(8,128)(2,1)}, bf16[32,3584]{1,0:T(8,128)(2,1)}) custom-call(s32[1]{0:T(128)} %bitcast.1.own_ref, s32[1]{0:T(128)} %bitcast.4.core_ref, s32[4]{0:T(128)S(1)} %copy-done.3, bf16[4,32,3584]{2,1,0:T(8,128)(2,1)S(1)} %copy-done, ...), custom_call_target="tpu_custom_call" | custom-call | tf_op jit(solution)/shard_map/diffuse/pallas_call | solution.py:307
  36.0 0.0 copy-done.4
  36.0 0.0 copy-done.5
  36.1 0.1 reshape.54
  36.1 0.1 reshape.55
  36.2 0.0 collective-permute-start.2
  36.2 1.9 %collective-permute-start.3 = (bf16[32,3584]{1,0:T(8,128)(2,1)}, bf16[32,3584]{1,0:T(8,128)(2,1)S(1)}, u32[]{:S(2)}, u32[]{:S(2)}) collective-permute-start(bf16[32,3584]{1,0:T(8,128)(2,1)} %get-tuple-element.23), channel_id=1, source_target_pairs={{0,2},{1,3},{2,0},{3,1},{4,6},{5,7},{6,4},{7,5},{8,10},{9,11},{10,... | collective-permute-start | bytes 688136 | tf_op jit(solution)/shard_map/ppermute | solution.py:323
  38.1 2.5 %collective-permute-start.4 = (bf16[32,3584]{1,0:T(8,128)(2,1)}, bf16[32,3584]{1,0:T(8,128)(2,1)S(1)}, u32[]{:S(2)}, u32[]{:S(2)}) collective-permute-start(bf16[32,3584]{1,0:T(8,128)(2,1)} %get-tuple-element.24), channel_id=1, source_target_pairs={{0,1},{1,2},{2,3},{3,0},{4,5},{5,6},{6,7},{7,4},{8,9},{9,10},{10,1... | collective-permute-start | bytes 688136 | tf_op jit(solution)/shard_map/ppermute | solution.py:323
  40.6 0.1 reduce_min.19
  40.8 0.1 reduce_max.19
  40.9 0.1 copy.11
  41.0 0.1 reshape.56.loc_ref
  41.1 3.4 %collective-permute-done.2.refs_1_ = bf16[32,3584]{1,0:T(8,128)(2,1)S(1)} collective-permute-done((bf16[32,3584]{1,0:T(8,128)(2,1)}, bf16[32,3584]{1,0:T(8,128)(2,1)S(1)}, u32[]{:S(2)}, u32[]{:S(2)}) %collective-permute-start.2) | collective-permute-done | bytes 229408 | tf_op jit(solution)/shard_map/ppermute | solution.py:323
  44.5 4.4 %collective-permute-done.3.refs_2_ = bf16[32,3584]{1,0:T(8,128)(2,1)S(1)} collective-permute-done((bf16[32,3584]{1,0:T(8,128)(2,1)}, bf16[32,3584]{1,0:T(8,128)(2,1)S(1)}, u32[]{:S(2)}, u32[]{:S(2)}) %collective-permute-start.3) | collective-permute-done | bytes 229408 | tf_op jit(solution)/shard_map/ppermute | solution.py:323
  49.0 1.8 %collective-permute-done.4.refs_3_ = bf16[32,3584]{1,0:T(8,128)(2,1)S(1)} collective-permute-done((bf16[32,3584]{1,0:T(8,128)(2,1)}, bf16[32,3584]{1,0:T(8,128)(2,1)S(1)}, u32[]{:S(2)}, u32[]{:S(2)}) %collective-permute-start.4) | collective-permute-done | bytes 229408 | tf_op jit(solution)/shard_map/ppermute | solution.py:323
  50.7 1.6 %all-to-all-done.prints_ref = bf16[64,16,512]{2,1,0:T(8,128)(2,1)S(1)} async-done(((bf16[64,16,512]{2,1,0:T(8,128)(2,1)}), bf16[64,16,512]{2,1,0:T(8,128)(2,1)S(1)}, u32[]{:S(2)}, u32[]{:S(2)}) %all-to-all-start) | async-done | bytes 1048608 | tf_op jit(solution)/shard_map/all_to_all | solution.py:305
  52.3 0.0 copy-start.2
  52.3 0.9 %copy-done.2 = bf16[32,3584]{1,0:T(8,128)(2,1)S(1)} copy-done((bf16[32,3584]{1,0:T(8,128)(2,1)S(1)}, bf16[32,3584]{1,0:T(8,128)(2,1)}, u32[]{:S(2)}) %copy-start.2) | copy-done | bytes 229400
  53.3 2.6 %dots.1 = f32[128,128]{1,0:T(8,128)S(1)} custom-call(s32[1]{0:T(128)} %bitcast.1.own_ref, s32[128]{0:T(128)S(1)} %reshape.56.loc_ref, bf16[64,16,512]{2,1,0:T(8,128)(2,1)S(1)} %all-to-all-done.prints_ref, bf16[32,3584]{1,0:T(8,128)(2,1)S(1)} %copy-done.2, bf16[32,3584]{1,0:T(8,128)(2,1)S(1)} %collective-permute-done.2.refs_1_, ...), custom_call_target="tpu_custom_call" | custom-call | tf_op jit(solution)/shard_map/dots/pallas_call | solution.py:334
  55.9 18.4 %all_to_all.10 = f32[64,2,128]{2,1,0:T(2,128)} all-to-all(f32[64,2,128]{2,1,0:T(2,128)S(1)} %bitcast.19), channel_id=1, replica_groups=mesh['station'=64,'sample'=4] {'station'}, dimensions={0} | all-to-all | bytes 131072 | tf_op jit(solution)/shard_map/all_to_all | solution.py:344
  74.3 1.7 %stations.1 = f32[16,16]{1,0:T(8,128)} custom-call(s32[64]{0:T(128)} %get-tuple-element.15.place_ref, s32[16]{0:T(128)} %count_ref.1, f32[128,128]{1,0:T(8,128)} %bitcast.20), custom_call_target="tpu_custom_call" | custom-call | tf_op jit(solution)/shard_map/stations/pallas_call | solution.py:345
  76.0 1.4 %collective-permute-start.7 = (f32[16,16]{1,0:T(8,128)}, f32[16,16]{1,0:T(8,128)S(1)}, u32[]{:S(2)}, u32[]{:S(2)}) collective-permute-start(f32[16,16]{1,0:T(8,128)} %stations.1), channel_id=1, source_target_pairs={{0,3},{1,2},{2,1},{3,0},{4,7},{5,6},{6,5},{7,4},{8,11},{9,10},{10,... | collective-permute-start | bytes 3080 | tf_op jit(solution)/shard_map/ppermute | solution.py:353
  77.4 3.0 %collective-permute-start.6 = (f32[16,16]{1,0:T(8,128)}, f32[16,16]{1,0:T(8,128)S(1)}, u32[]{:S(2)}, u32[]{:S(2)}) collective-permute-start(f32[16,16]{1,0:T(8,128)} %stations.1), channel_id=1, source_target_pairs={{0,2},{1,3},{2,0},{3,1},{4,6},{5,7},{6,4},{7,5},{8,10},{9,11},{10,... | collective-permute-start | bytes 3080 | tf_op jit(solution)/shard_map/ppermute | solution.py:353
  80.4 0.0 collective-permute-start.5
  80.4 0.0 collective-permute-done.7
  80.4 2.4 %collective-permute-done.6 = f32[16,16]{1,0:T(8,128)S(1)} collective-permute-done((f32[16,16]{1,0:T(8,128)}, f32[16,16]{1,0:T(8,128)S(1)}, u32[]{:S(2)}, u32[]{:S(2)}) %collective-permute-start.6) | collective-permute-done | bytes 1056 | tf_op jit(solution)/shard_map/ppermute | solution.py:353
  82.8 1.5 %collective-permute-done.5 = f32[16,16]{1,0:T(8,128)S(1)} collective-permute-done((f32[16,16]{1,0:T(8,128)}, f32[16,16]{1,0:T(8,128)S(1)}, u32[]{:S(2)}, u32[]{:S(2)}) %collective-permute-start.5) | collective-permute-done | bytes 1056 | tf_op jit(solution)/shard_map/ppermute | solution.py:353
  84.3 1.3 %add_add_fusion = f32[16,16]{1,0:T(8,128)} fusion(f32[16,16]{1,0:T(8,128)S(1)} %collective-permute-done.6, f32[16,16]{1,0:T(8,128)S(1)} %collective-permute-done.7, f32[16,16]{1,0:T(8,128)} %stations.1, f32[16,16]{1,0:T(8,128)S(1)} %collective-permute-done.5), kind=kLoop, calls=%fused_computation.5 | loop fusion | flops 768 | bytes 5120 | tf_op jit(solution)/shard_map/add | solution.py:354
  (4 shorter events, 0.1 us)
Async XLA Ops:
  2.2 7.6 %collective-permute-start = (bf16[6,8,3584]{2,1,0:T(8,128)(2,1)}, bf16[6,8,3584]{2,1,0:T(8,128)(2,1)S(1)}, u32[]{:S(2)}, u32[]{:S(2)}) collective-permute-start(bf16[6,8,3584]{2,1,0:T(8,128)(2,1)} %get-tuple-element.16), channel_id=1, source_target_pairs={{4,8},{12,16},{20,24},{28,32},{36,40},{44,48},{52,56},{60,64},{68,... | collective-permute-start | bytes 1032200 | tf_op jit(solution)/shard_map/ppermute | solution.py:277
  2.9 6.9 %collective-permute-start.1 = (bf16[6,8,3584]{2,1,0:T(8,128)(2,1)}, bf16[6,8,3584]{2,1,0:T(8,128)(2,1)S(1)}, u32[]{:S(2)}, u32[]{:S(2)}) collective-permute-start(bf16[6,8,3584]{2,1,0:T(8,128)(2,1)} %get-tuple-element.17), channel_id=1, source_target_pairs={{0,4},{4,0},{8,12},{12,8},{16,20},{20,16},{24,28},{28,24},{32,36},... | collective-permute-start | bytes 1032200 | tf_op jit(solution)/shard_map/ppermute | solution.py:278
  6.3 17.9 %copy-start = (bf16[4,32,3584]{2,1,0:T(8,128)(2,1)S(1)}, bf16[4,32,3584]{2,1,0:T(8,128)(2,1)}, u32[]{:S(2)}) copy-start(bf16[4,32,3584]{2,1,0:T(8,128)(2,1)} %flux_ref.3) | copy-start | bytes 2752516
  6.3 17.9 %copy-start.1 = (f32[32,3584]{1,0:T(8,128)S(1)}, f32[32,3584]{1,0:T(8,128)}, u32[]{:S(2)}) copy-start(f32[32,3584]{1,0:T(8,128)} %coef_ref.3) | copy-start | bytes 1376260
  6.3 17.9 %copy-start.3 = (s32[4]{0:T(128)S(1)}, s32[4]{0:T(128)}, u32[]{:S(2)}) copy-start(s32[4]{0:T(128)} %steps_ref.1) | copy-start | bytes 52
  9.8 26.2 %copy-start.4 = (s32[1024,4,1]{0,2,1:T(1,128)S(1)}, s32[1024,4,1]{0,2,1:T(1,128)}, u32[]{:S(2)}) copy-start(s32[1024,4,1]{0,2,1:T(1,128)} %param.11) | copy-start | bytes 49156
  9.8 26.2 %copy-start.5 = (s32[1024,4]{0,1:T(4,128)S(1)}, s32[1024,4]{0,1:T(4,128)}, u32[]{:S(2)}) copy-start(s32[1024,4]{0,1:T(4,128)} %param.12) | copy-start | bytes 49156
  9.8 42.5 %all-to-all-start = ((bf16[64,16,512]{2,1,0:T(8,128)(2,1)}), bf16[64,16,512]{2,1,0:T(8,128)(2,1)S(1)}, u32[]{:S(2)}, u32[]{:S(2)}) async-start(bf16[64,16,512]{2,1,0:T(8,128)(2,1)} %get-tuple-element.21), calls=%async_computation | async-start | bytes 2097152 | tf_op jit(solution)/shard_map/all_to_all | solution.py:305
  36.2 8.3 %collective-permute-start.2 = (bf16[32,3584]{1,0:T(8,128)(2,1)}, bf16[32,3584]{1,0:T(8,128)(2,1)S(1)}, u32[]{:S(2)}, u32[]{:S(2)}) collective-permute-start(bf16[32,3584]{1,0:T(8,128)(2,1)} %get-tuple-element.22), channel_id=1, source_target_pairs={{0,3},{1,0},{2,1},{3,2},{4,7},{5,4},{6,5},{7,6},{8,11},{9,8},{10,9... | collective-permute-start | bytes 688136 | tf_op jit(solution)/shard_map/ppermute | solution.py:323
  36.2 12.7 %collective-permute-start.3 = (bf16[32,3584]{1,0:T(8,128)(2,1)}, bf16[32,3584]{1,0:T(8,128)(2,1)S(1)}, u32[]{:S(2)}, u32[]{:S(2)}) collective-permute-start(bf16[32,3584]{1,0:T(8,128)(2,1)} %get-tuple-element.23), channel_id=1, source_target_pairs={{0,2},{1,3},{2,0},{3,1},{4,6},{5,7},{6,4},{7,5},{8,10},{9,11},{10,... | collective-permute-start | bytes 688136 | tf_op jit(solution)/shard_map/ppermute | solution.py:323
  38.1 12.6 %collective-permute-start.4 = (bf16[32,3584]{1,0:T(8,128)(2,1)}, bf16[32,3584]{1,0:T(8,128)(2,1)S(1)}, u32[]{:S(2)}, u32[]{:S(2)}) collective-permute-start(bf16[32,3584]{1,0:T(8,128)(2,1)} %get-tuple-element.24), channel_id=1, source_target_pairs={{0,1},{1,2},{2,3},{3,0},{4,5},{5,6},{6,7},{7,4},{8,9},{9,10},{10,1... | collective-permute-start | bytes 688136 | tf_op jit(solution)/shard_map/ppermute | solution.py:323
  52.3 0.9 %copy-start.2 = (bf16[32,3584]{1,0:T(8,128)(2,1)S(1)}, bf16[32,3584]{1,0:T(8,128)(2,1)}, u32[]{:S(2)}) copy-start(bf16[32,3584]{1,0:T(8,128)(2,1)} %get-tuple-element.18.refs_0_) | copy-start | bytes 688132
  76.0 4.4 %collective-permute-start.7 = (f32[16,16]{1,0:T(8,128)}, f32[16,16]{1,0:T(8,128)S(1)}, u32[]{:S(2)}, u32[]{:S(2)}) collective-permute-start(f32[16,16]{1,0:T(8,128)} %stations.1), channel_id=1, source_target_pairs={{0,3},{1,2},{2,1},{3,0},{4,7},{5,6},{6,5},{7,4},{8,11},{9,10},{10,... | collective-permute-start | bytes 3080 | tf_op jit(solution)/shard_map/ppermute | solution.py:353
  77.4 5.4 %collective-permute-start.6 = (f32[16,16]{1,0:T(8,128)}, f32[16,16]{1,0:T(8,128)S(1)}, u32[]{:S(2)}, u32[]{:S(2)}) collective-permute-start(f32[16,16]{1,0:T(8,128)} %stations.1), channel_id=1, source_target_pairs={{0,2},{1,3},{2,0},{3,1},{4,6},{5,7},{6,4},{7,5},{8,10},{9,11},{10,... | collective-permute-start | bytes 3080 | tf_op jit(solution)/shard_map/ppermute | solution.py:353
  80.4 3.9 %collective-permute-start.5 = (f32[16,16]{1,0:T(8,128)}, f32[16,16]{1,0:T(8,128)S(1)}, u32[]{:S(2)}, u32[]{:S(2)}) collective-permute-start(f32[16,16]{1,0:T(8,128)} %stations.1), channel_id=1, source_target_pairs={{0,1},{1,0},{2,3},{3,2},{4,5},{5,4},{6,7},{7,6},{8,9},{9,8},{10,11... | collective-permute-start | bytes 3080 | tf_op jit(solution)/shard_map/ppermute | solution.py:353

commit v5 on v4

--- a/solution.py
+++ b/solution.py
@@ -269,7 +269,7 @@
 
     away, beside = pl.pallas_call(
         edge_kernel,
-        out_shape=[jax.ShapeDtypeStruct((samples + 2, HALO, lon), jnp.bfloat16)] * 2,
+        out_shape=[VMEM((samples + 2, HALO, lon), jnp.bfloat16)] * 2,
         in_specs=[spec(SMEM)] + [spec(VMEM)] * 2,
         out_specs=[spec(VMEM)] * 2,
         name="edges",
@@ -306,7 +306,8 @@
 
     finals = pl.pallas_call(
         diffuse_kernel,
-        out_shape=[HBM((samples * 8, lon), jnp.bfloat16)] * PARTS,
+        out_shape=[jax.ShapeDtypeStruct((samples * 8, lon), jnp.bfloat16)]
+        + [HBM((samples * 8, lon), jnp.bfloat16)] * (PARTS - 1),
         in_specs=[spec(SMEM)] * 3 + [spec(VMEM)] * 4,
         out_specs=[spec(HBM)] * PARTS,
         scratch_shapes=[
@@ -331,6 +332,7 @@
     last = jnp.max(jnp.max(jnp.where(named, code, 0), axis=0).reshape(bands, stations), axis=1)
     loc = jnp.stack([first & 7, last & 7], axis=1)
 
+    parts = [pltpu.with_memory_space_constraint(each, VMEM) for each in parts]
     values = pl.pallas_call(
         dots_kernel,
         out_shape=jax.ShapeDtypeStruct((bands * CAP, LANES), jnp.float32),
@@ -342,14 +344,15 @@
     )(own, loc.reshape(-1), arrived, *parts)
 
     back = lax.all_to_all(values.reshape(bands, CAP, LANES), "station", split_axis=0, concat_axis=0, tiled=True)
+    back = pltpu.with_memory_space_constraint(back.reshape(bands * CAP, LANES), VMEM)
     share = pl.pallas_call(
         station_kernel,
-        out_shape=jax.ShapeDtypeStruct((stations, 16), jnp.float32),
+        out_shape=VMEM((stations, 16), jnp.float32),
         in_specs=[spec(SMEM), spec(SMEM), spec(VMEM)],
         out_specs=spec(VMEM),
         scratch_shapes=[VMEM((stations, LANES), jnp.float32)],
         name="stations",
-    )(place, tile_count, back.reshape(bands * CAP, LANES))
+    )(place, tile_count, back)
     others = [lax.ppermute(share, "sample", [(i, i ^ flip) for i in range(PARTS)]) for flip in (1, 2, 3)]
     return (share + others[0]) + (others[1] + others[2])
 

time: 85.3 us -> 81.5 us (0.955); the launches traced: 85.6 us -> 80.5 us
  Pallas kernels: 21.8 us -> 17.3 us
  starting transfers between devices: 27.2 us -> 29.4 us
  blocking collectives: 18.4 us -> 16.4 us
  local copies, waits for them, and re-layouts: 1.34 us -> 0.4 us
    pallas_call x3, Pallas kernels: 15.7 us -> 11.2 us  [the longest x1 8.94 us: body(): pl.pallas_call(diffuse_kernel, out_shape=[jax.ShapeDtypeStruct((samples *...]
    all_to_all x1, blocking collectives: 18.4 us -> 16.4 us  [body(): lax.all_to_all(values.reshape(bands, CAP, LANES), 'station', split_axis=0...]
    all_to_all x1, waiting for transfers between devices: 1.6 us -> 3.5 us  [body(): lax.all_to_all(sent, 'station', split_axis=0, concat_axis=0, tiled=True)]
    ppermute x3, starting transfers between devices: 4.43 us -> 6.24 us  [body(): lax.ppermute(finals[turn], 'sample', [(i, (i + turn) % PARTS) for i in ra...]
    unnamed x12 -> x10, local copies, waits for them, and re-layouts: 0.96 us -> 0.02 us
    ppermute x3, waiting for transfers between devices: 9.61 us -> 8.75 us  [body(): lax.ppermute(finals[turn], 'sample', [(i, (i + turn) % PARTS) for i in ra...]
  transfers between devices with their start and end apart: 9 -> 9, of which waited for: 6 -> 6; matrix products, arithmetic and copies ran while one was open for 1% -> 1% of each run, Pallas kernels for 18% -> 15%
where the time goes in v5:
time: 81.5 us; the launch traced here: 80.5 us
  starting transfers between devices  29.4 us (36%)
  Pallas kernels  17.3 us (21%)
  blocking collectives  16.4 us (20%)
  waiting for transfers between devices  15.9 us (20%)
  other arithmetic  0.88 us (1%)
    all_to_all x1, blocking collectives, body(): lax.all_to_all(values.reshape(bands, CAP, LANES), 'station', split_axis=0...  16.4 us
    all_to_all x1, starting transfers between devices, body(): lax.all_to_all(sent, 'station', split_axis=0, concat_axis=0, tiled=True)  14.1 us
    pallas_call x1, Pallas kernels, body(): pl.pallas_call(diffuse_kernel, out_shape=[jax.ShapeDtypeStruct((samples *...  8.94 us
    ppermute x3, waiting for transfers between devices, body(): lax.ppermute(finals[turn], 'sample', [(i, (i + turn) % PARTS) for i in ra...  8.75 us
    ppermute x3, starting transfers between devices, body(): lax.ppermute(finals[turn], 'sample', [(i, (i + turn) % PARTS) for i in ra...  6.24 us
    ppermute x3, starting transfers between devices, body(): lax.ppermute(share, 'sample', [(i, i ^ flip) for i in range(PARTS)])  5 us
    ppermute x3, waiting for transfers between devices, body(): lax.ppermute(share, 'sample', [(i, i ^ flip) for i in range(PARTS)])  3.65 us
    pallas_call x1, Pallas kernels, body(): pl.pallas_call(pack_kernel, out_shape=(HBM((bands, 8 * CAP, TILE_LON), jn...  3.51 us
  transfers between devices with their start and end apart: 9, of which 6 were waited for; matrix products, arithmetic and copies ran while one was open for 1% of the time, Pallas kernels for 15%

profile of v5, /device:TPU:8, one launch (start us, length us, event | category | flops | bytes accessed | tf_op | source)
XLA Modules:
  0.0 80.5 jit_solution(3102910928219398893)
XLA Ops:
  0.0 1.4 %edges.1 = (bf16[6,8,3584]{2,1,0:T(8,128)(2,1)S(1)}, bf16[6,8,3584]{2,1,0:T(8,128)(2,1)S(1)}) custom-call(s32[1]{0:T(128)} %bitcast.4.core_ref, bf16[4,32,3584]{2,1,0:T(8,128)(2,1)} %flux_ref.3, f32[32,3584]{1,0:T(8,128)} %coef_ref.3), custom_call_target="tpu_custom_call" | custom-call | tf_op jit(solution)/shard_map/edges/pallas_call | solution.py:270
  1.4 0.7 collective-permute-start
  2.1 3.3 %collective-permute-start.1 = (bf16[6,8,3584]{2,1,0:T(8,128)(2,1)S(1)}, bf16[6,8,3584]{2,1,0:T(8,128)(2,1)S(1)}, u32[]{:S(2)}, u32[]{:S(2)}) collective-permute-start(bf16[6,8,3584]{2,1,0:T(8,128)(2,1)S(1)} %get-tuple-element.17), channel_id=1, source_target_pairs={{0,4},{4,0},{8,12},{12,8},{16,20},{20,16},{24,28},{28,24},{32,36},... | collective-permute-start | bytes 1032200 | tf_op jit(solution)/shard_map/ppermute | solution.py:278
  5.4 0.0 copy-start
  5.4 0.0 copy-start.1
  5.4 0.0 copy-start.2
  5.4 3.5 %pack.1 = (bf16[64,16,512]{2,1,0:T(8,128)(2,1)}, s32[64]{0:T(128)}) custom-call(s32[4,1,1024]{2,1,0:T(1,128)} %bitcast.21, bf16[16,4,16384]{2,1,0:T(4,128)(2,1)} %prints_hbm.1), custom_call_target="tpu_custom_call" | custom-call | tf_op jit(solution)/shard_map/pack/pallas_call | solution.py:281
  8.9 0.0 copy-start.3
  8.9 0.0 copy-start.4
  8.9 0.0 collective-permute-done.away_ref
  9.0 0.0 collective-permute-done.1.beside_ref
  9.0 14.1 %all-to-all-start = ((bf16[64,16,512]{2,1,0:T(8,128)(2,1)}), bf16[64,16,512]{2,1,0:T(8,128)(2,1)S(1)}, u32[]{:S(2)}, u32[]{:S(2)}) async-start(bf16[64,16,512]{2,1,0:T(8,128)(2,1)} %get-tuple-element.21), calls=%async_computation | async-start | bytes 2097152 | tf_op jit(solution)/shard_map/all_to_all | solution.py:305
  23.1 0.0 copy-done
  23.1 0.0 copy-done.1
  23.1 0.0 copy-done.2
  23.1 8.9 %diffuse.1 = (bf16[32,3584]{1,0:T(8,128)(2,1)S(1)}, bf16[32,3584]{1,0:T(8,128)(2,1)}, bf16[32,3584]{1,0:T(8,128)(2,1)}, bf16[32,3584]{1,0:T(8,128)(2,1)}) custom-call(s32[1]{0:T(128)} %bitcast.1.own_ref, s32[1]{0:T(128)} %bitcast.4.core_ref, s32[4]{0:T(128)S(1)} %copy-done.2, bf16[4,32,3584]{2,1,0:T(8,128)(2,1)S(1)} %copy-done, ...), custom_call_target="tpu_custom_call" | custom-call | tf_op jit(solution)/shard_map/diffuse/pallas_call | solution.py:307
  32.1 0.0 copy-done.3
  32.1 0.0 copy-done.4
  32.1 0.1 reshape.54
  32.2 0.1 reshape.55
  32.3 0.5 collective-permute-start.2
  32.8 3.4 %collective-permute-start.3 = (bf16[32,3584]{1,0:T(8,128)(2,1)}, bf16[32,3584]{1,0:T(8,128)(2,1)S(1)}, u32[]{:S(2)}, u32[]{:S(2)}) collective-permute-start(bf16[32,3584]{1,0:T(8,128)(2,1)} %get-tuple-element.23), channel_id=1, source_target_pairs={{0,2},{1,3},{2,0},{3,1},{4,6},{5,7},{6,4},{7,5},{8,10},{9,11},{10,... | collective-permute-start | bytes 688136 | tf_op jit(solution)/shard_map/ppermute | solution.py:324
  36.2 2.3 %collective-permute-start.4 = (bf16[32,3584]{1,0:T(8,128)(2,1)}, bf16[32,3584]{1,0:T(8,128)(2,1)S(1)}, u32[]{:S(2)}, u32[]{:S(2)}) collective-permute-start(bf16[32,3584]{1,0:T(8,128)(2,1)} %get-tuple-element.24), channel_id=1, source_target_pairs={{0,1},{1,2},{2,3},{3,0},{4,5},{5,6},{6,7},{7,4},{8,9},{9,10},{10,1... | collective-permute-start | bytes 688136 | tf_op jit(solution)/shard_map/ppermute | solution.py:324
  38.5 0.1 reduce_min.19
  38.6 0.1 reduce_max.19
  38.8 0.1 copy.11
  38.9 0.1 reshape.56.loc_ref
  39.0 1.8 %collective-permute-done.2.refs_1_ = bf16[32,3584]{1,0:T(8,128)(2,1)S(1)} collective-permute-done((bf16[32,3584]{1,0:T(8,128)(2,1)}, bf16[32,3584]{1,0:T(8,128)(2,1)S(1)}, u32[]{:S(2)}, u32[]{:S(2)}) %collective-permute-start.2) | collective-permute-done | bytes 229408 | tf_op jit(solution)/shard_map/ppermute | solution.py:324
  40.8 6.1 %collective-permute-done.3.refs_2_ = bf16[32,3584]{1,0:T(8,128)(2,1)S(1)} collective-permute-done((bf16[32,3584]{1,0:T(8,128)(2,1)}, bf16[32,3584]{1,0:T(8,128)(2,1)S(1)}, u32[]{:S(2)}, u32[]{:S(2)}) %collective-permute-start.3) | collective-permute-done | bytes 229408 | tf_op jit(solution)/shard_map/ppermute | solution.py:324
  46.9 0.9 %collective-permute-done.4.refs_3_ = bf16[32,3584]{1,0:T(8,128)(2,1)S(1)} collective-permute-done((bf16[32,3584]{1,0:T(8,128)(2,1)}, bf16[32,3584]{1,0:T(8,128)(2,1)S(1)}, u32[]{:S(2)}, u32[]{:S(2)}) %collective-permute-start.4) | collective-permute-done | bytes 229408 | tf_op jit(solution)/shard_map/ppermute | solution.py:324
  47.8 3.5 %all-to-all-done.prints_ref = bf16[64,16,512]{2,1,0:T(8,128)(2,1)S(1)} async-done(((bf16[64,16,512]{2,1,0:T(8,128)(2,1)}), bf16[64,16,512]{2,1,0:T(8,128)(2,1)S(1)}, u32[]{:S(2)}, u32[]{:S(2)}) %all-to-all-start) | async-done | bytes 1048608 | tf_op jit(solution)/shard_map/all_to_all | solution.py:305
  51.3 2.6 %dots.1 = f32[128,128]{1,0:T(8,128)S(1)} custom-call(s32[1]{0:T(128)} %bitcast.1.own_ref, s32[128]{0:T(128)S(1)} %reshape.56.loc_ref, bf16[64,16,512]{2,1,0:T(8,128)(2,1)S(1)} %all-to-all-done.prints_ref, bf16[32,3584]{1,0:T(8,128)(2,1)S(1)} %get-tuple-element.18.refs_0_, bf16[32,3584]{1,0:T(8,128)(2,1)S(1)} %collective-permute-done.2.refs_1_, ...), custom_call_target="tpu_custom_call" | custom-call | tf_op jit(solution)/shard_map/dots/pallas_call | solution.py:336
  53.9 16.4 %all_to_all.10 = f32[64,2,128]{2,1,0:T(2,128)S(1)} all-to-all(f32[64,2,128]{2,1,0:T(2,128)S(1)} %bitcast.19), channel_id=1, replica_groups=mesh['station'=64,'sample'=4] {'station'}, dimensions={0} | all-to-all | bytes 131072 | tf_op jit(solution)/shard_map/all_to_all | solution.py:346
  70.3 0.9 %stations.1 = f32[16,16]{1,0:T(8,128)S(1)} custom-call(s32[64]{0:T(128)} %get-tuple-element.15.place_ref, s32[16]{0:T(128)} %count_ref.1, f32[128,128]{1,0:T(8,128)S(1)} %bitcast.20), custom_call_target="tpu_custom_call" | custom-call | tf_op jit(solution)/shard_map/stations/pallas_call | solution.py:348
  71.2 1.4 %collective-permute-start.7 = (f32[16,16]{1,0:T(8,128)S(1)}, f32[16,16]{1,0:T(8,128)S(1)}, u32[]{:S(2)}, u32[]{:S(2)}) collective-permute-start(f32[16,16]{1,0:T(8,128)S(1)} %stations.1), channel_id=1, source_target_pairs={{0,3},{1,2},{2,1},{3,0},{4,7},{5,6},{6,5},{7,4},{8,11},{9,10},{10,... | collective-permute-start | bytes 3080 | tf_op jit(solution)/shard_map/ppermute | solution.py:356
  72.6 3.6 %collective-permute-start.6 = (f32[16,16]{1,0:T(8,128)S(1)}, f32[16,16]{1,0:T(8,128)S(1)}, u32[]{:S(2)}, u32[]{:S(2)}) collective-permute-start(f32[16,16]{1,0:T(8,128)S(1)} %stations.1), channel_id=1, source_target_pairs={{0,2},{1,3},{2,0},{3,1},{4,6},{5,7},{6,4},{7,5},{8,10},{9,11},{10,... | collective-permute-start | bytes 3080 | tf_op jit(solution)/shard_map/ppermute | solution.py:356
  76.2 0.0 collective-permute-start.5
  76.2 0.0 collective-permute-done.7
  76.2 1.6 %collective-permute-done.6 = f32[16,16]{1,0:T(8,128)S(1)} collective-permute-done((f32[16,16]{1,0:T(8,128)S(1)}, f32[16,16]{1,0:T(8,128)S(1)}, u32[]{:S(2)}, u32[]{:S(2)}) %collective-permute-start.6) | collective-permute-done | bytes 1056 | tf_op jit(solution)/shard_map/ppermute | solution.py:356
  77.8 2.0 %collective-permute-done.5 = f32[16,16]{1,0:T(8,128)S(1)} collective-permute-done((f32[16,16]{1,0:T(8,128)S(1)}, f32[16,16]{1,0:T(8,128)S(1)}, u32[]{:S(2)}, u32[]{:S(2)}) %collective-permute-start.5) | collective-permute-done | bytes 1056 | tf_op jit(solution)/shard_map/ppermute | solution.py:356
  79.9 0.6 add_add_fusion
  (4 shorter events, 0.1 us)
Async XLA Ops:
  1.4 7.6 %collective-permute-start = (bf16[6,8,3584]{2,1,0:T(8,128)(2,1)S(1)}, bf16[6,8,3584]{2,1,0:T(8,128)(2,1)S(1)}, u32[]{:S(2)}, u32[]{:S(2)}) collective-permute-start(bf16[6,8,3584]{2,1,0:T(8,128)(2,1)S(1)} %get-tuple-element.16), channel_id=1, source_target_pairs={{4,8},{12,16},{20,24},{28,32},{36,40},{44,48},{52,56},{60,64},{68,... | collective-permute-start | bytes 1032200 | tf_op jit(solution)/shard_map/ppermute | solution.py:277
  2.1 6.9 %collective-permute-start.1 = (bf16[6,8,3584]{2,1,0:T(8,128)(2,1)S(1)}, bf16[6,8,3584]{2,1,0:T(8,128)(2,1)S(1)}, u32[]{:S(2)}, u32[]{:S(2)}) collective-permute-start(bf16[6,8,3584]{2,1,0:T(8,128)(2,1)S(1)} %get-tuple-element.17), channel_id=1, source_target_pairs={{0,4},{4,0},{8,12},{12,8},{16,20},{20,16},{24,28},{28,24},{32,36},... | collective-permute-start | bytes 1032200 | tf_op jit(solution)/shard_map/ppermute | solution.py:278
  5.4 17.7 %copy-start = (bf16[4,32,3584]{2,1,0:T(8,128)(2,1)S(1)}, bf16[4,32,3584]{2,1,0:T(8,128)(2,1)}, u32[]{:S(2)}) copy-start(bf16[4,32,3584]{2,1,0:T(8,128)(2,1)} %flux_ref.3) | copy-start | bytes 2752516
  5.4 17.7 %copy-start.1 = (f32[32,3584]{1,0:T(8,128)S(1)}, f32[32,3584]{1,0:T(8,128)}, u32[]{:S(2)}) copy-start(f32[32,3584]{1,0:T(8,128)} %coef_ref.3) | copy-start | bytes 1376260
  5.4 17.7 %copy-start.2 = (s32[4]{0:T(128)S(1)}, s32[4]{0:T(128)}, u32[]{:S(2)}) copy-start(s32[4]{0:T(128)} %steps_ref.1) | copy-start | bytes 52
  8.9 23.2 %copy-start.3 = (s32[1024,4,1]{0,2,1:T(1,128)S(1)}, s32[1024,4,1]{0,2,1:T(1,128)}, u32[]{:S(2)}) copy-start(s32[1024,4,1]{0,2,1:T(1,128)} %param.11) | copy-start | bytes 49156
  8.9 23.2 %copy-start.4 = (s32[1024,4]{0,1:T(4,128)S(1)}, s32[1024,4]{0,1:T(4,128)}, u32[]{:S(2)}) copy-start(s32[1024,4]{0,1:T(4,128)} %param.12) | copy-start | bytes 49156
  9.0 42.3 %all-to-all-start = ((bf16[64,16,512]{2,1,0:T(8,128)(2,1)}), bf16[64,16,512]{2,1,0:T(8,128)(2,1)S(1)}, u32[]{:S(2)}, u32[]{:S(2)}) async-start(bf16[64,16,512]{2,1,0:T(8,128)(2,1)} %get-tuple-element.21), calls=%async_computation | async-start | bytes 2097152 | tf_op jit(solution)/shard_map/all_to_all | solution.py:305
  32.3 8.5 %collective-permute-start.2 = (bf16[32,3584]{1,0:T(8,128)(2,1)}, bf16[32,3584]{1,0:T(8,128)(2,1)S(1)}, u32[]{:S(2)}, u32[]{:S(2)}) collective-permute-start(bf16[32,3584]{1,0:T(8,128)(2,1)} %get-tuple-element.22), channel_id=1, source_target_pairs={{0,3},{1,0},{2,1},{3,2},{4,7},{5,4},{6,5},{7,6},{8,11},{9,8},{10,9... | collective-permute-start | bytes 688136 | tf_op jit(solution)/shard_map/ppermute | solution.py:324
  32.8 14.1 %collective-permute-start.3 = (bf16[32,3584]{1,0:T(8,128)(2,1)}, bf16[32,3584]{1,0:T(8,128)(2,1)S(1)}, u32[]{:S(2)}, u32[]{:S(2)}) collective-permute-start(bf16[32,3584]{1,0:T(8,128)(2,1)} %get-tuple-element.23), channel_id=1, source_target_pairs={{0,2},{1,3},{2,0},{3,1},{4,6},{5,7},{6,4},{7,5},{8,10},{9,11},{10,... | collective-permute-start | bytes 688136 | tf_op jit(solution)/shard_map/ppermute | solution.py:324
  36.2 11.6 %collective-permute-start.4 = (bf16[32,3584]{1,0:T(8,128)(2,1)}, bf16[32,3584]{1,0:T(8,128)(2,1)S(1)}, u32[]{:S(2)}, u32[]{:S(2)}) collective-permute-start(bf16[32,3584]{1,0:T(8,128)(2,1)} %get-tuple-element.24), channel_id=1, source_target_pairs={{0,1},{1,2},{2,3},{3,0},{4,5},{5,6},{6,7},{7,4},{8,9},{9,10},{10,1... | collective-permute-start | bytes 688136 | tf_op jit(solution)/shard_map/ppermute | solution.py:324
  71.2 5.0 %collective-permute-start.7 = (f32[16,16]{1,0:T(8,128)S(1)}, f32[16,16]{1,0:T(8,128)S(1)}, u32[]{:S(2)}, u32[]{:S(2)}) collective-permute-start(f32[16,16]{1,0:T(8,128)S(1)} %stations.1), channel_id=1, source_target_pairs={{0,3},{1,2},{2,1},{3,0},{4,7},{5,6},{6,5},{7,4},{8,11},{9,10},{10,... | collective-permute-start | bytes 3080 | tf_op jit(solution)/shard_map/ppermute | solution.py:356
  72.6 5.2 %collective-permute-start.6 = (f32[16,16]{1,0:T(8,128)S(1)}, f32[16,16]{1,0:T(8,128)S(1)}, u32[]{:S(2)}, u32[]{:S(2)}) collective-permute-start(f32[16,16]{1,0:T(8,128)S(1)} %stations.1), channel_id=1, source_target_pairs={{0,2},{1,3},{2,0},{3,1},{4,6},{5,7},{6,4},{7,5},{8,10},{9,11},{10,... | collective-permute-start | bytes 3080 | tf_op jit(solution)/shard_map/ppermute | solution.py:356
  76.2 3.7 %collective-permute-start.5 = (f32[16,16]{1,0:T(8,128)S(1)}, f32[16,16]{1,0:T(8,128)S(1)}, u32[]{:S(2)}, u32[]{:S(2)}) collective-permute-start(f32[16,16]{1,0:T(8,128)S(1)} %stations.1), channel_id=1, source_target_pairs={{0,1},{1,0},{2,3},{3,2},{4,5},{5,4},{6,7},{7,6},{8,9},{9,8},{10,11... | collective-permute-start | bytes 3080 | tf_op jit(solution)/shard_map/ppermute | solution.py:356

commit v6 on v5

--- a/solution.py
+++ b/solution.py
@@ -23,8 +23,8 @@
 
 
 def pack_kernel(
-    src_hbm, prints_hbm, sent_hbm, place_ref,
-    src_ref, held_ref, slot_ref, prints_ref, hot_ref, sent_ref, sems,
+    src_hbm, prints_hbm, sent_hbm, place_hbm,
+    place_ref, src_ref, held_ref, slot_ref, prints_ref, hot_ref, sent_ref, sems,
 ):
     bands, _, width = sent_ref.shape
     stations, _, cells = prints_ref.shape
@@ -57,6 +57,8 @@
         return carry
 
     lax.fori_loop(0, stations, assign, 0)
+    copies = [pltpu.make_async_copy(place_ref, place_hbm, sems.at[6])]
+    copies[0].start()
 
     row = lax.broadcasted_iota(jnp.int32, (8, width), 0)
     offset = lax.broadcasted_iota(jnp.int32, (8, width), 1) - slots * row
@@ -72,7 +74,6 @@
     flat = prints_ref[...].reshape(slots, cells)
     stacked = jnp.concatenate([flat[:, r * width : (r + 1) * width] for r in range(8)], axis=0)
     some = bands // 4
-    copies = []
     for turn in range(4):
         at = slice(turn * some, (turn + 1) * some)
         hot = hot_ref[at].reshape(some * 16, slots * 8)
@@ -84,8 +85,9 @@
         copy.wait()
 
 
-def edge_kernel(core_ref, flux_ref, coef_ref, away_ref, beside_ref):
+def edge_kernel(flux_ref, coef_ref, away_ref, beside_ref):
     samples, rows, _ = flux_ref.shape
+    core = lax.rem(lax.axis_index("station"), 2)
 
     def fill(ref, low):
         ref[0:samples] = flux_ref[:, low : low + HALO]
@@ -94,28 +96,31 @@
         ref[samples] = head
         ref[samples + 1] = (coef - head.astype(jnp.float32)).astype(jnp.bfloat16)
 
-    @pl.when(core_ref[0] == 0)
+    @pl.when(core == 0)
     def _():
         fill(away_ref, 0)
         fill(beside_ref, rows - HALO)
 
-    @pl.when(core_ref[0] == 1)
+    @pl.when(core == 1)
     def _():
         fill(away_ref, rows - HALO)
         fill(beside_ref, 0)
 
 
 def diffuse_kernel(
-    own_ref, core_ref, steps_ref, flux_ref, away_ref, beside_ref, coef_ref,
-    out0_hbm, out1_hbm, out2_hbm, out3_hbm, even_ref, odd_ref, coefs_ref, out_ref, sems,
+    steps_hbm, flux_ref, away_ref, beside_ref, coef_ref,
+    out0_hbm, out1_hbm, out2_hbm, out3_hbm, steps_ref, even_ref, odd_ref, coefs_ref, out_ref, sems,
 ):
-    own = own_ref[0]
+    steps_in = pltpu.make_async_copy(steps_hbm, steps_ref, sems.at[PARTS])
+    steps_in.start()
+    own = lax.axis_index("sample")
+    core = lax.rem(lax.axis_index("station"), 2)
     samples, rows, lon = flux_ref.shape
     strips = lon // LANES
     tall = rows + 2 * HALO
     edge = jnp.zeros((HALO, LANES), jnp.float32)
-    away = pl.multiple_of(core_ref[0] * (HALO + rows), 8)
-    near = pl.multiple_of((1 - core_ref[0]) * (HALO + rows), 8)
+    away = pl.multiple_of(core * (HALO + rows), 8)
+    near = pl.multiple_of((1 - core) * (HALO + rows), 8)
     lane = lax.broadcasted_iota(jnp.int32, (8, LANES), 1)
     first_lane = lane == 0
     last_lane = lane == LANES - 1
@@ -191,6 +196,7 @@
         lax.fori_loop(0, half, two, 0)
         return carry
 
+    steps_in.wait()
     lax.fori_loop(0, samples, evolve, 0)
 
     copies = []
@@ -208,9 +214,11 @@
         copy.wait()
 
 
-def dots_kernel(own_ref, loc_ref, prints_ref, *refs):
+def dots_kernel(loc_hbm, prints_ref, *refs):
     parts = refs[:PARTS]
-    out_ref, sums_ref = refs[PARTS:]
+    out_ref, loc_ref, sums_ref, sems = refs[PARTS:]
+    loc_in = pltpu.make_async_copy(loc_hbm, loc_ref, sems.at[0])
+    loc_in.start()
     bands, _, width = prints_ref.shape
     slots = bands * CAP
     prints = prints_ref[...].reshape(slots * 8, width)
@@ -225,7 +233,8 @@
     same = lax.rem(lax.broadcasted_iota(jnp.int32, (8, LANES), 1), 8) == lax.broadcasted_iota(
         jnp.int32, (8, LANES), 0
     )
-    shift = 32 * own_ref[0]
+    shift = 32 * lax.axis_index("sample")
+    loc_in.wait()
 
     def pick(group, carry):
         at = pl.multiple_of(group * 8, 8)
@@ -260,20 +269,17 @@
     slots = stations * KT
     bands = lax.axis_size("station")
     band = lax.axis_index("station")
-    part = lax.axis_index("sample")
-    own = part.astype(jnp.int32).reshape(1)
     cells = rows * TILE_LON // PARTS
-    core = lax.rem(band, 2).astype(jnp.int32).reshape(1)
     across = [(i, i + 1) for i in range(1, bands - 1, 2)] + [(i, i - 1) for i in range(2, bands, 2)]
     within = [(i, i ^ 1) for i in range(bands)]
 
     away, beside = pl.pallas_call(
         edge_kernel,
         out_shape=[VMEM((samples + 2, HALO, lon), jnp.bfloat16)] * 2,
-        in_specs=[spec(SMEM)] + [spec(VMEM)] * 2,
+        in_specs=[spec(VMEM)] * 2,
         out_specs=[spec(VMEM)] * 2,
         name="edges",
-    )(core, flux, coeff)
+    )(flux, coeff)
     away = lax.ppermute(away, "station", across)
     beside = lax.ppermute(beside, "station", within)
 
@@ -285,15 +291,16 @@
             HBM((slots,), jnp.int32),
         ),
         in_specs=[spec(HBM), spec(HBM)],
-        out_specs=(spec(HBM), spec(SMEM)),
+        out_specs=(spec(HBM), spec(HBM)),
         scratch_shapes=[
+            SMEM((slots,), jnp.int32),
             SMEM((KT, 1, LANES), jnp.int32),
             SMEM((bands,), jnp.int32),
             SMEM((CAP * bands,), jnp.int32),
             VMEM((stations, KT, cells), jnp.bfloat16),
             VMEM((bands, 8 * CAP, 8 * slots), jnp.bfloat16),
             VMEM((bands, 8 * CAP, TILE_LON), jnp.bfloat16),
-            pltpu.SemaphoreType.DMA((6,)),
+            pltpu.SemaphoreType.DMA((7,)),
         ],
         compiler_params=pltpu.CompilerParams(vmem_limit_bytes=24 * 2**20),
         name="pack",
@@ -308,18 +315,19 @@
         diffuse_kernel,
         out_shape=[jax.ShapeDtypeStruct((samples * 8, lon), jnp.bfloat16)]
         + [HBM((samples * 8, lon), jnp.bfloat16)] * (PARTS - 1),
-        in_specs=[spec(SMEM)] * 3 + [spec(VMEM)] * 4,
+        in_specs=[spec(HBM)] + [spec(VMEM)] * 4,
         out_specs=[spec(HBM)] * PARTS,
         scratch_shapes=[
+            SMEM((samples,), jnp.int32),
             VMEM((samples, lon // LANES, rows + 4 * HALO, LANES), jnp.float32),
             VMEM((lon // LANES, rows + 4 * HALO, LANES), jnp.float32),
             VMEM((lon // LANES, rows + 2 * HALO, LANES), jnp.float32),
             VMEM((PARTS, samples * 8, lon), jnp.bfloat16),
-            pltpu.SemaphoreType.DMA((PARTS,)),
+            pltpu.SemaphoreType.DMA((PARTS + 1,)),
         ],
         compiler_params=pltpu.CompilerParams(vmem_limit_bytes=24 * 2**20),
         name="diffuse",
-    )(own, core, diff_steps, flux, away, beside, coeff)
+    )(diff_steps, flux, away, beside, coeff)
     parts = [finals[0]] + [
         lax.ppermute(finals[turn], "sample", [(i, (i + turn) % PARTS) for i in range(PARTS)]) for turn in (3, 2, 1)
     ]
@@ -336,12 +344,16 @@
     values = pl.pallas_call(
         dots_kernel,
         out_shape=jax.ShapeDtypeStruct((bands * CAP, LANES), jnp.float32),
-        in_specs=[spec(SMEM)] * 2 + [spec(VMEM)] * (1 + PARTS),
+        in_specs=[spec(HBM)] + [spec(VMEM)] * (1 + PARTS),
         out_specs=spec(VMEM),
-        scratch_shapes=[VMEM((TILES_DEV, bands * CAP, 8, LANES), jnp.float32)],
+        scratch_shapes=[
+            SMEM((bands * CAP,), jnp.int32),
+            VMEM((TILES_DEV, bands * CAP, 8, LANES), jnp.float32),
+            pltpu.SemaphoreType.DMA((1,)),
+        ],
         compiler_params=pltpu.CompilerParams(vmem_limit_bytes=24 * 2**20),
         name="dots",
-    )(own, loc.reshape(-1), arrived, *parts)
+    )(loc.reshape(-1), arrived, *parts)
 
     back = lax.all_to_all(values.reshape(bands, CAP, LANES), "station", split_axis=0, concat_axis=0, tiled=True)
     back = pltpu.with_memory_space_constraint(back.reshape(bands * CAP, LANES), VMEM)

time: 81.5 us -> 80 us (0.982); the launches traced: 80.5 us -> 80.1 us
  blocking collectives: 16.4 us -> 17.5 us
    ppermute x3, waiting for transfers between devices: 8.75 us -> 9.97 us  [body(): lax.ppermute(finals[turn], 'sample', [(i, (i + turn) % PARTS) for i in ra...]
    all_to_all x1, blocking collectives: 16.4 us -> 17.5 us  [body(): lax.all_to_all(values.reshape(bands, CAP, LANES), 'station', split_axis=0...]
    all_to_all x1, waiting for transfers between devices: 3.5 us -> 2.42 us  [body(): lax.all_to_all(sent, 'station', split_axis=0, concat_axis=0, tiled=True)]
    ppermute x3, starting transfers between devices: 5 us -> 4.11 us  [body(): lax.ppermute(share, 'sample', [(i, i ^ flip) for i in range(PARTS)])]
where the time goes in v6:
time: 80 us; the launch traced here: 80.1 us
  starting transfers between devices  28.6 us (36%)
  blocking collectives  17.5 us (22%)
  Pallas kernels  16.6 us (21%)
  waiting for transfers between devices  16 us (20%)
  other arithmetic  0.89 us (1%)
    all_to_all x1, blocking collectives, body(): lax.all_to_all(values.reshape(bands, CAP, LANES), 'station', split_axis=0...  17.5 us
    all_to_all x1, starting transfers between devices, body(): lax.all_to_all(sent, 'station', split_axis=0, concat_axis=0, tiled=True)  14.6 us
    ppermute x3, waiting for transfers between devices, body(): lax.ppermute(finals[turn], 'sample', [(i, (i + turn) % PARTS) for i in ra...  9.97 us
    pallas_call x1, Pallas kernels, body(): pl.pallas_call(diffuse_kernel, out_shape=[jax.ShapeDtypeStruct((samples *...  9.23 us
    ppermute x3, starting transfers between devices, body(): lax.ppermute(finals[turn], 'sample', [(i, (i + turn) % PARTS) for i in ra...  5.81 us
    ppermute x3, starting transfers between devices, body(): lax.ppermute(share, 'sample', [(i, i ^ flip) for i in range(PARTS)])  4.11 us
    ppermute x3, waiting for transfers between devices, body(): lax.ppermute(share, 'sample', [(i, i ^ flip) for i in range(PARTS)])  3.61 us
    ppermute x1, starting transfers between devices, body(): beside = lax.ppermute(beside, 'station', within)  3.35 us
  transfers between devices with their start and end apart: 9, of which 6 were waited for; matrix products, arithmetic and copies ran while one was open for 1% of the time, Pallas kernels for 15%

profile of v6, /device:TPU:8, one launch (start us, length us, event | category | flops | bytes accessed | tf_op | source)
XLA Modules:
  0.0 80.1 jit_solution(3979478655692570292)
XLA Ops:
  0.0 1.3 %edges.1 = (bf16[6,8,3584]{2,1,0:T(8,128)(2,1)S(1)}, bf16[6,8,3584]{2,1,0:T(8,128)(2,1)S(1)}) custom-call(bf16[4,32,3584]{2,1,0:T(8,128)(2,1)} %flux_ref.3, f32[32,3584]{1,0:T(8,128)} %coef_ref.3), custom_call_target="tpu_custom_call" | custom-call | tf_op jit(solution)/shard_map/edges/pallas_call | solution.py:276
  1.4 0.7 collective-permute-start
  2.0 3.3 %collective-permute-start.1 = (bf16[6,8,3584]{2,1,0:T(8,128)(2,1)S(1)}, bf16[6,8,3584]{2,1,0:T(8,128)(2,1)S(1)}, u32[]{:S(2)}, u32[]{:S(2)}) collective-permute-start(bf16[6,8,3584]{2,1,0:T(8,128)(2,1)S(1)} %get-tuple-element.17), channel_id=1, source_target_pairs={{0,4},{4,0},{8,12},{12,8},{16,20},{20,16},{24,28},{28,24},{32,36},... | collective-permute-start | bytes 1032200 | tf_op jit(solution)/shard_map/ppermute | solution.py:284
  5.4 0.0 copy-start
  5.4 0.0 copy-start.1
  5.4 0.0 copy-start.2
  5.4 3.0 %pack.1 = (bf16[64,16,512]{2,1,0:T(8,128)(2,1)}, s32[64]{0:T(128)}) custom-call(s32[4,1,1024]{2,1,0:T(1,128)} %bitcast.19, bf16[16,4,16384]{2,1,0:T(4,128)(2,1)} %prints_hbm.1), custom_call_target="tpu_custom_call" | custom-call | tf_op jit(solution)/shard_map/pack/pallas_call | solution.py:287
  8.4 0.0 copy-start.3
  8.4 0.0 copy-start.4
  8.4 0.0 collective-permute-done.away_ref
  8.5 0.0 collective-permute-done.1.beside_ref
  8.5 14.6 %all-to-all-start = ((bf16[64,16,512]{2,1,0:T(8,128)(2,1)}), bf16[64,16,512]{2,1,0:T(8,128)(2,1)S(1)}, u32[]{:S(2)}, u32[]{:S(2)}) async-start(bf16[64,16,512]{2,1,0:T(8,128)(2,1)} %get-tuple-element.21), calls=%async_computation | async-start | bytes 2097152 | tf_op jit(solution)/shard_map/all_to_all | solution.py:312
  23.1 0.0 copy-done
  23.1 0.0 copy-done.1
  23.1 0.0 copy-done.2
  23.1 9.2 %diffuse.1 = (bf16[32,3584]{1,0:T(8,128)(2,1)S(1)}, bf16[32,3584]{1,0:T(8,128)(2,1)}, bf16[32,3584]{1,0:T(8,128)(2,1)}, bf16[32,3584]{1,0:T(8,128)(2,1)}) custom-call(s32[4]{0:T(128)S(1)} %copy-done.2, bf16[4,32,3584]{2,1,0:T(8,128)(2,1)S(1)} %copy-done, bf16[6,8,3584]{2,1,0:T(8,128)(2,1)S(1)} %collective-permute-done.away_ref, ...), custom_call_target="tpu_custom_call" | custom-call | tf_op jit(solution)/shard_map/diffuse/pallas_call | solution.py:314
  32.4 0.0 copy-done.3
  32.4 0.0 copy-done.4
  32.4 0.1 reshape.46
  32.5 0.1 reshape.47
  32.6 1.8 %collective-permute-start.2 = (bf16[32,3584]{1,0:T(8,128)(2,1)}, bf16[32,3584]{1,0:T(8,128)(2,1)S(1)}, u32[]{:S(2)}, u32[]{:S(2)}) collective-permute-start(bf16[32,3584]{1,0:T(8,128)(2,1)} %get-tuple-element.22), channel_id=1, source_target_pairs={{0,3},{1,0},{2,1},{3,2},{4,7},{5,4},{6,5},{7,6},{8,11},{9,8},{10,9... | collective-permute-start | bytes 688136 | tf_op jit(solution)/shard_map/ppermute | solution.py:332
  34.4 3.0 %collective-permute-start.3 = (bf16[32,3584]{1,0:T(8,128)(2,1)}, bf16[32,3584]{1,0:T(8,128)(2,1)S(1)}, u32[]{:S(2)}, u32[]{:S(2)}) collective-permute-start(bf16[32,3584]{1,0:T(8,128)(2,1)} %get-tuple-element.23), channel_id=1, source_target_pairs={{0,2},{1,3},{2,0},{3,1},{4,6},{5,7},{6,4},{7,5},{8,10},{9,11},{10,... | collective-permute-start | bytes 688136 | tf_op jit(solution)/shard_map/ppermute | solution.py:332
  37.4 0.9 %collective-permute-start.4 = (bf16[32,3584]{1,0:T(8,128)(2,1)}, bf16[32,3584]{1,0:T(8,128)(2,1)S(1)}, u32[]{:S(2)}, u32[]{:S(2)}) collective-permute-start(bf16[32,3584]{1,0:T(8,128)(2,1)} %get-tuple-element.24), channel_id=1, source_target_pairs={{0,1},{1,2},{2,3},{3,0},{4,5},{5,6},{6,7},{7,4},{8,9},{9,10},{10,1... | collective-permute-start | bytes 688136 | tf_op jit(solution)/shard_map/ppermute | solution.py:332
  38.4 0.1 reduce_min.19
  38.5 0.1 reduce_max.19
  38.6 0.1 copy.11
  38.7 0.1 reshape.48.loc_hbm
  38.9 3.1 %collective-permute-done.2.refs_1_ = bf16[32,3584]{1,0:T(8,128)(2,1)S(1)} collective-permute-done((bf16[32,3584]{1,0:T(8,128)(2,1)}, bf16[32,3584]{1,0:T(8,128)(2,1)S(1)}, u32[]{:S(2)}, u32[]{:S(2)}) %collective-permute-start.2) | collective-permute-done | bytes 229408 | tf_op jit(solution)/shard_map/ppermute | solution.py:332
  42.0 6.1 %collective-permute-done.3.refs_2_ = bf16[32,3584]{1,0:T(8,128)(2,1)S(1)} collective-permute-done((bf16[32,3584]{1,0:T(8,128)(2,1)}, bf16[32,3584]{1,0:T(8,128)(2,1)S(1)}, u32[]{:S(2)}, u32[]{:S(2)}) %collective-permute-start.3) | collective-permute-done | bytes 229408 | tf_op jit(solution)/shard_map/ppermute | solution.py:332
  48.1 0.7 collective-permute-done.4.refs_3_
  48.9 2.4 %all-to-all-done.prints_ref = bf16[64,16,512]{2,1,0:T(8,128)(2,1)S(1)} async-done(((bf16[64,16,512]{2,1,0:T(8,128)(2,1)}), bf16[64,16,512]{2,1,0:T(8,128)(2,1)S(1)}, u32[]{:S(2)}, u32[]{:S(2)}) %all-to-all-start) | async-done | bytes 1048608 | tf_op jit(solution)/shard_map/all_to_all | solution.py:312
  51.3 2.1 %dots.1 = f32[128,128]{1,0:T(8,128)S(1)} custom-call(s32[128]{0:T(128)S(1)} %reshape.48.loc_hbm, bf16[64,16,512]{2,1,0:T(8,128)(2,1)S(1)} %all-to-all-done.prints_ref, bf16[32,3584]{1,0:T(8,128)(2,1)S(1)} %get-tuple-element.18.refs_0_, bf16[32,3584]{1,0:T(8,128)(2,1)S(1)} %collective-permute-done.2.refs_1_, ...), custom_call_target="tpu_custom_call" | custom-call | tf_op jit(solution)/shard_map/dots/pallas_call | solution.py:344
  53.3 17.5 %all_to_all.10 = f32[64,2,128]{2,1,0:T(2,128)S(1)} all-to-all(f32[64,2,128]{2,1,0:T(2,128)S(1)} %bitcast.17), channel_id=1, replica_groups=mesh['station'=64,'sample'=4] {'station'}, dimensions={0} | all-to-all | bytes 131072 | tf_op jit(solution)/shard_map/all_to_all | solution.py:358
  70.9 0.9 %stations.1 = f32[16,16]{1,0:T(8,128)S(1)} custom-call(s32[64]{0:T(128)} %get-tuple-element.15.place_ref, s32[16]{0:T(128)} %count_ref.1, f32[128,128]{1,0:T(8,128)S(1)} %bitcast.18), custom_call_target="tpu_custom_call" | custom-call | tf_op jit(solution)/shard_map/stations/pallas_call | solution.py:360
  71.8 1.4 %collective-permute-start.7 = (f32[16,16]{1,0:T(8,128)S(1)}, f32[16,16]{1,0:T(8,128)S(1)}, u32[]{:S(2)}, u32[]{:S(2)}) collective-permute-start(f32[16,16]{1,0:T(8,128)S(1)} %stations.1), channel_id=1, source_target_pairs={{0,3},{1,2},{2,1},{3,0},{4,7},{5,6},{6,5},{7,4},{8,11},{9,10},{10,... | collective-permute-start | bytes 3080 | tf_op jit(solution)/shard_map/ppermute | solution.py:368
  73.2 2.6 %collective-permute-start.6 = (f32[16,16]{1,0:T(8,128)S(1)}, f32[16,16]{1,0:T(8,128)S(1)}, u32[]{:S(2)}, u32[]{:S(2)}) collective-permute-start(f32[16,16]{1,0:T(8,128)S(1)} %stations.1), channel_id=1, source_target_pairs={{0,2},{1,3},{2,0},{3,1},{4,6},{5,7},{6,4},{7,5},{8,10},{9,11},{10,... | collective-permute-start | bytes 3080 | tf_op jit(solution)/shard_map/ppermute | solution.py:368
  75.9 0.0 collective-permute-start.5
  75.9 0.0 collective-permute-done.7
  75.9 2.5 %collective-permute-done.6 = f32[16,16]{1,0:T(8,128)S(1)} collective-permute-done((f32[16,16]{1,0:T(8,128)S(1)}, f32[16,16]{1,0:T(8,128)S(1)}, u32[]{:S(2)}, u32[]{:S(2)}) %collective-permute-start.6) | collective-permute-done | bytes 1056 | tf_op jit(solution)/shard_map/ppermute | solution.py:368
  78.4 1.1 %collective-permute-done.5 = f32[16,16]{1,0:T(8,128)S(1)} collective-permute-done((f32[16,16]{1,0:T(8,128)S(1)}, f32[16,16]{1,0:T(8,128)S(1)}, u32[]{:S(2)}, u32[]{:S(2)}) %collective-permute-start.5) | collective-permute-done | bytes 1056 | tf_op jit(solution)/shard_map/ppermute | solution.py:368
  79.5 0.6 add_add_fusion
  (4 shorter events, 0.1 us)
Async XLA Ops:
  1.4 7.1 %collective-permute-start = (bf16[6,8,3584]{2,1,0:T(8,128)(2,1)S(1)}, bf16[6,8,3584]{2,1,0:T(8,128)(2,1)S(1)}, u32[]{:S(2)}, u32[]{:S(2)}) collective-permute-start(bf16[6,8,3584]{2,1,0:T(8,128)(2,1)S(1)} %get-tuple-element.16), channel_id=1, source_target_pairs={{4,8},{12,16},{20,24},{28,32},{36,40},{44,48},{52,56},{60,64},{68,... | collective-permute-start | bytes 1032200 | tf_op jit(solution)/shard_map/ppermute | solution.py:283
  2.0 6.4 %collective-permute-start.1 = (bf16[6,8,3584]{2,1,0:T(8,128)(2,1)S(1)}, bf16[6,8,3584]{2,1,0:T(8,128)(2,1)S(1)}, u32[]{:S(2)}, u32[]{:S(2)}) collective-permute-start(bf16[6,8,3584]{2,1,0:T(8,128)(2,1)S(1)} %get-tuple-element.17), channel_id=1, source_target_pairs={{0,4},{4,0},{8,12},{12,8},{16,20},{20,16},{24,28},{28,24},{32,36},... | collective-permute-start | bytes 1032200 | tf_op jit(solution)/shard_map/ppermute | solution.py:284
  5.4 17.7 %copy-start = (bf16[4,32,3584]{2,1,0:T(8,128)(2,1)S(1)}, bf16[4,32,3584]{2,1,0:T(8,128)(2,1)}, u32[]{:S(2)}) copy-start(bf16[4,32,3584]{2,1,0:T(8,128)(2,1)} %flux_ref.3) | copy-start | bytes 2752516
  5.4 17.7 %copy-start.1 = (f32[32,3584]{1,0:T(8,128)S(1)}, f32[32,3584]{1,0:T(8,128)}, u32[]{:S(2)}) copy-start(f32[32,3584]{1,0:T(8,128)} %coef_ref.3) | copy-start | bytes 1376260
  5.4 17.7 %copy-start.2 = (s32[4]{0:T(128)S(1)}, s32[4]{0:T(128)}, u32[]{:S(2)}) copy-start(s32[4]{0:T(128)} %steps_hbm.1) | copy-start | bytes 52
  8.4 23.9 %copy-start.3 = (s32[1024,4,1]{0,2,1:T(1,128)S(1)}, s32[1024,4,1]{0,2,1:T(1,128)}, u32[]{:S(2)}) copy-start(s32[1024,4,1]{0,2,1:T(1,128)} %param.11) | copy-start | bytes 49156
  8.4 23.9 %copy-start.4 = (s32[1024,4]{0,1:T(4,128)S(1)}, s32[1024,4]{0,1:T(4,128)}, u32[]{:S(2)}) copy-start(s32[1024,4]{0,1:T(4,128)} %param.12) | copy-start | bytes 49156
  8.5 42.8 %all-to-all-start = ((bf16[64,16,512]{2,1,0:T(8,128)(2,1)}), bf16[64,16,512]{2,1,0:T(8,128)(2,1)S(1)}, u32[]{:S(2)}, u32[]{:S(2)}) async-start(bf16[64,16,512]{2,1,0:T(8,128)(2,1)} %get-tuple-element.21), calls=%async_computation | async-start | bytes 2097152 | tf_op jit(solution)/shard_map/all_to_all | solution.py:312
  32.6 9.4 %collective-permute-start.2 = (bf16[32,3584]{1,0:T(8,128)(2,1)}, bf16[32,3584]{1,0:T(8,128)(2,1)S(1)}, u32[]{:S(2)}, u32[]{:S(2)}) collective-permute-start(bf16[32,3584]{1,0:T(8,128)(2,1)} %get-tuple-element.22), channel_id=1, source_target_pairs={{0,3},{1,0},{2,1},{3,2},{4,7},{5,4},{6,5},{7,6},{8,11},{9,8},{10,9... | collective-permute-start | bytes 688136 | tf_op jit(solution)/shard_map/ppermute | solution.py:332
  34.4 13.7 %collective-permute-start.3 = (bf16[32,3584]{1,0:T(8,128)(2,1)}, bf16[32,3584]{1,0:T(8,128)(2,1)S(1)}, u32[]{:S(2)}, u32[]{:S(2)}) collective-permute-start(bf16[32,3584]{1,0:T(8,128)(2,1)} %get-tuple-element.23), channel_id=1, source_target_pairs={{0,2},{1,3},{2,0},{3,1},{4,6},{5,7},{6,4},{7,5},{8,10},{9,11},{10,... | collective-permute-start | bytes 688136 | tf_op jit(solution)/shard_map/ppermute | solution.py:332
  37.4 11.4 %collective-permute-start.4 = (bf16[32,3584]{1,0:T(8,128)(2,1)}, bf16[32,3584]{1,0:T(8,128)(2,1)S(1)}, u32[]{:S(2)}, u32[]{:S(2)}) collective-permute-start(bf16[32,3584]{1,0:T(8,128)(2,1)} %get-tuple-element.24), channel_id=1, source_target_pairs={{0,1},{1,2},{2,3},{3,0},{4,5},{5,6},{6,7},{7,4},{8,9},{9,10},{10,1... | collective-permute-start | bytes 688136 | tf_op jit(solution)/shard_map/ppermute | solution.py:332
  71.8 4.1 %collective-permute-start.7 = (f32[16,16]{1,0:T(8,128)S(1)}, f32[16,16]{1,0:T(8,128)S(1)}, u32[]{:S(2)}, u32[]{:S(2)}) collective-permute-start(f32[16,16]{1,0:T(8,128)S(1)} %stations.1), channel_id=1, source_target_pairs={{0,3},{1,2},{2,1},{3,0},{4,7},{5,6},{6,5},{7,4},{8,11},{9,10},{10,... | collective-permute-start | bytes 3080 | tf_op jit(solution)/shard_map/ppermute | solution.py:368
  73.2 5.2 %collective-permute-start.6 = (f32[16,16]{1,0:T(8,128)S(1)}, f32[16,16]{1,0:T(8,128)S(1)}, u32[]{:S(2)}, u32[]{:S(2)}) collective-permute-start(f32[16,16]{1,0:T(8,128)S(1)} %stations.1), channel_id=1, source_target_pairs={{0,2},{1,3},{2,0},{3,1},{4,6},{5,7},{6,4},{7,5},{8,10},{9,11},{10,... | collective-permute-start | bytes 3080 | tf_op jit(solution)/shard_map/ppermute | solution.py:368
  75.9 3.7 %collective-permute-start.5 = (f32[16,16]{1,0:T(8,128)S(1)}, f32[16,16]{1,0:T(8,128)S(1)}, u32[]{:S(2)}, u32[]{:S(2)}) collective-permute-start(f32[16,16]{1,0:T(8,128)S(1)} %stations.1), channel_id=1, source_target_pairs={{0,1},{1,0},{2,3},{3,2},{4,5},{5,4},{6,7},{7,6},{8,9},{9,8},{10,11... | collective-permute-start | bytes 3080 | tf_op jit(solution)/shard_map/ppermute | solution.py:368

commit v7 on v6

--- a/solution.py
+++ b/solution.py
@@ -201,7 +201,7 @@
 
     copies = []
     for turn, out_hbm in ((2, out2_hbm), (1, out1_hbm), (3, out3_hbm), (0, out0_hbm)):
-        low = pl.multiple_of(2 * HALO + 8 * lax.rem(own + turn, PARTS), 8)
+        low = pl.multiple_of(2 * HALO + 8 * (own ^ turn), 8)
         for pair in range(samples // 2):
             for strip in range(strips):
                 both = [even_ref[2 * pair + side, strip, pl.ds(low, 8)] for side in range(2)]
@@ -233,7 +233,8 @@
     same = lax.rem(lax.broadcasted_iota(jnp.int32, (8, LANES), 1), 8) == lax.broadcasted_iota(
         jnp.int32, (8, LANES), 0
     )
-    shift = 32 * lax.axis_index("sample")
+    own = lax.axis_index("sample")
+    odd_block = lax.rem(lax.div(lax.broadcasted_iota(jnp.int32, (8, LANES), 1), 32), 2) == 1
     loc_in.wait()
 
     def pick(group, carry):
@@ -241,7 +242,10 @@
         rows = [
             jnp.sum(jnp.where(same, sums_ref[loc_ref[at + i], at + i], 0.0), axis=0, keepdims=True) for i in range(8)
         ]
-        out_ref[pl.ds(at, 8)] = pltpu.roll(jnp.concatenate(rows, axis=0), shift, 1)
+        found = jnp.concatenate(rows, axis=0)
+        swapped = jnp.where(odd_block, pltpu.roll(found, 32, 1), pltpu.roll(found, LANES - 32, 1))
+        found = jnp.where((own & 1) == 1, swapped, found)
+        out_ref[pl.ds(at, 8)] = jnp.where((own & 2) == 2, pltpu.roll(found, 64, 1), found)
         return carry
 
     lax.fori_loop(0, slots // 8, pick, 0, unroll=2)
@@ -329,7 +333,7 @@
         name="diffuse",
     )(diff_steps, flux, away, beside, coeff)
     parts = [finals[0]] + [
-        lax.ppermute(finals[turn], "sample", [(i, (i + turn) % PARTS) for i in range(PARTS)]) for turn in (3, 2, 1)
+        lax.ppermute(finals[turn], "sample", [(i, i ^ turn) for i in range(PARTS)]) for turn in range(1, PARTS)
     ]
 
     local, _ = lax.optimization_barrier((tile_local, finals[0]))

time: 80 us -> 81.8 us (1.022)
  waiting for transfers between devices: 16 us -> 17.6 us
    ppermute x3, starting transfers between devices: 5.81 us -> 4.26 us  [body(): lax.ppermute(finals[turn], 'sample', [(i, i ^ turn) for i in range(PARTS)])]
    ppermute x3, waiting for transfers between devices: 9.97 us -> 11.4 us  [body(): lax.ppermute(finals[turn], 'sample', [(i, i ^ turn) for i in range(PARTS)])]
    ppermute x3, starting transfers between devices: 4.11 us -> 5.55 us  [body(): lax.ppermute(share, 'sample', [(i, i ^ flip) for i in range(PARTS)])]
where the time goes in v7:
time: 81.8 us; the launch traced here: 82.1 us
  starting transfers between devices  28.4 us (35%)
  waiting for transfers between devices  17.6 us (22%)
  blocking collectives  17.5 us (21%)
  Pallas kernels  17.1 us (21%)
  other arithmetic  0.89 us (1%)
    all_to_all x1, blocking collectives, body(): lax.all_to_all(values.reshape(bands, CAP, LANES), 'station', split_axis=0...  17.5 us
    all_to_all x1, starting transfers between devices, body(): lax.all_to_all(sent, 'station', split_axis=0, concat_axis=0, tiled=True)  14.6 us
    ppermute x3, waiting for transfers between devices, body(): lax.ppermute(finals[turn], 'sample', [(i, i ^ turn) for i in range(PARTS)])  11.4 us
    pallas_call x1, Pallas kernels, body(): pl.pallas_call(diffuse_kernel, out_shape=[jax.ShapeDtypeStruct((samples *...  9.23 us
    ppermute x3, starting transfers between devices, body(): lax.ppermute(share, 'sample', [(i, i ^ flip) for i in range(PARTS)])  5.55 us
    ppermute x3, starting transfers between devices, body(): lax.ppermute(finals[turn], 'sample', [(i, i ^ turn) for i in range(PARTS)])  4.26 us
    ppermute x3, waiting for transfers between devices, body(): lax.ppermute(share, 'sample', [(i, i ^ flip) for i in range(PARTS)])  3.65 us
    ppermute x1, starting transfers between devices, body(): beside = lax.ppermute(beside, 'station', within)  3.35 us
  transfers between devices with their start and end apart: 9, of which 6 were waited for; matrix products, arithmetic and copies ran while one was open for 1% of the time, Pallas kernels for 15%

profile of v7, /device:TPU:8, one launch (start us, length us, event | category | flops | bytes accessed | tf_op | source)
XLA Modules:
  0.0 82.1 jit_solution(9452664481626276550)
XLA Ops:
  0.0 1.3 %edges.1 = (bf16[6,8,3584]{2,1,0:T(8,128)(2,1)S(1)}, bf16[6,8,3584]{2,1,0:T(8,128)(2,1)S(1)}) custom-call(bf16[4,32,3584]{2,1,0:T(8,128)(2,1)} %flux_ref.3, f32[32,3584]{1,0:T(8,128)} %coef_ref.3), custom_call_target="tpu_custom_call" | custom-call | tf_op jit(solution)/shard_map/edges/pallas_call | solution.py:280
  1.4 0.7 collective-permute-start
  2.0 3.3 %collective-permute-start.1 = (bf16[6,8,3584]{2,1,0:T(8,128)(2,1)S(1)}, bf16[6,8,3584]{2,1,0:T(8,128)(2,1)S(1)}, u32[]{:S(2)}, u32[]{:S(2)}) collective-permute-start(bf16[6,8,3584]{2,1,0:T(8,128)(2,1)S(1)} %get-tuple-element.17), channel_id=1, source_target_pairs={{0,4},{4,0},{8,12},{12,8},{16,20},{20,16},{24,28},{28,24},{32,36},... | collective-permute-start | bytes 1032200 | tf_op jit(solution)/shard_map/ppermute | solution.py:288
  5.4 0.0 copy-start
  5.4 0.0 copy-start.1
  5.4 0.0 copy-start.2
  5.4 3.0 %pack.1 = (bf16[64,16,512]{2,1,0:T(8,128)(2,1)}, s32[64]{0:T(128)}) custom-call(s32[4,1,1024]{2,1,0:T(1,128)} %bitcast.19, bf16[16,4,16384]{2,1,0:T(4,128)(2,1)} %prints_hbm.1), custom_call_target="tpu_custom_call" | custom-call | tf_op jit(solution)/shard_map/pack/pallas_call | solution.py:291
  8.4 0.0 copy-start.3
  8.4 0.0 copy-start.4
  8.4 0.0 collective-permute-done.away_ref
  8.5 0.0 collective-permute-done.1.beside_ref
  8.5 14.6 %all-to-all-start = ((bf16[64,16,512]{2,1,0:T(8,128)(2,1)}), bf16[64,16,512]{2,1,0:T(8,128)(2,1)S(1)}, u32[]{:S(2)}, u32[]{:S(2)}) async-start(bf16[64,16,512]{2,1,0:T(8,128)(2,1)} %get-tuple-element.21), calls=%async_computation | async-start | bytes 2097152 | tf_op jit(solution)/shard_map/all_to_all | solution.py:316
  23.1 0.0 copy-done
  23.1 0.0 copy-done.1
  23.1 0.0 copy-done.2
  23.1 9.2 %diffuse.1 = (bf16[32,3584]{1,0:T(8,128)(2,1)S(1)}, bf16[32,3584]{1,0:T(8,128)(2,1)}, bf16[32,3584]{1,0:T(8,128)(2,1)}, bf16[32,3584]{1,0:T(8,128)(2,1)}) custom-call(s32[4]{0:T(128)S(1)} %copy-done.2, bf16[4,32,3584]{2,1,0:T(8,128)(2,1)S(1)} %copy-done, bf16[6,8,3584]{2,1,0:T(8,128)(2,1)S(1)} %collective-permute-done.away_ref, ...), custom_call_target="tpu_custom_call" | custom-call | tf_op jit(solution)/shard_map/diffuse/pallas_call | solution.py:318
  32.4 0.0 copy-done.3
  32.4 0.0 copy-done.4
  32.4 0.1 reshape.46
  32.5 0.1 reshape.47
  32.6 0.5 collective-permute-start.2
  33.1 3.4 %collective-permute-start.3 = (bf16[32,3584]{1,0:T(8,128)(2,1)}, bf16[32,3584]{1,0:T(8,128)(2,1)S(1)}, u32[]{:S(2)}, u32[]{:S(2)}) collective-permute-start(bf16[32,3584]{1,0:T(8,128)(2,1)} %get-tuple-element.23), channel_id=1, source_target_pairs={{0,2},{1,3},{2,0},{3,1},{4,6},{5,7},{6,4},{7,5},{8,10},{9,11},{10,... | collective-permute-start | bytes 688136 | tf_op jit(solution)/shard_map/ppermute | solution.py:336
  36.5 0.3 collective-permute-start.4
  36.8 0.1 reduce_min.19
  37.0 0.1 reduce_max.19
  37.1 0.1 copy.11
  37.2 0.1 reshape.48.loc_hbm
  37.3 3.9 %collective-permute-done.2.refs_1_ = bf16[32,3584]{1,0:T(8,128)(2,1)S(1)} collective-permute-done((bf16[32,3584]{1,0:T(8,128)(2,1)}, bf16[32,3584]{1,0:T(8,128)(2,1)S(1)}, u32[]{:S(2)}, u32[]{:S(2)}) %collective-permute-start.2) | collective-permute-done | bytes 229408 | tf_op jit(solution)/shard_map/ppermute | solution.py:336
  41.3 6.0 %collective-permute-done.3.refs_2_ = bf16[32,3584]{1,0:T(8,128)(2,1)S(1)} collective-permute-done((bf16[32,3584]{1,0:T(8,128)(2,1)}, bf16[32,3584]{1,0:T(8,128)(2,1)S(1)}, u32[]{:S(2)}, u32[]{:S(2)}) %collective-permute-start.3) | collective-permute-done | bytes 229408 | tf_op jit(solution)/shard_map/ppermute | solution.py:336
  47.3 1.5 %collective-permute-done.4.refs_3_ = bf16[32,3584]{1,0:T(8,128)(2,1)S(1)} collective-permute-done((bf16[32,3584]{1,0:T(8,128)(2,1)}, bf16[32,3584]{1,0:T(8,128)(2,1)S(1)}, u32[]{:S(2)}, u32[]{:S(2)}) %collective-permute-start.4) | collective-permute-done | bytes 229408 | tf_op jit(solution)/shard_map/ppermute | solution.py:336
  48.8 2.5 %all-to-all-done.prints_ref = bf16[64,16,512]{2,1,0:T(8,128)(2,1)S(1)} async-done(((bf16[64,16,512]{2,1,0:T(8,128)(2,1)}), bf16[64,16,512]{2,1,0:T(8,128)(2,1)S(1)}, u32[]{:S(2)}, u32[]{:S(2)}) %all-to-all-start) | async-done | bytes 1048608 | tf_op jit(solution)/shard_map/all_to_all | solution.py:316
  51.3 2.6 %dots.1 = f32[128,128]{1,0:T(8,128)S(1)} custom-call(s32[128]{0:T(128)S(1)} %reshape.48.loc_hbm, bf16[64,16,512]{2,1,0:T(8,128)(2,1)S(1)} %all-to-all-done.prints_ref, bf16[32,3584]{1,0:T(8,128)(2,1)S(1)} %get-tuple-element.18.refs_0_, bf16[32,3584]{1,0:T(8,128)(2,1)S(1)} %collective-permute-done.2.refs_1_, ...), custom_call_target="tpu_custom_call" | custom-call | tf_op jit(solution)/shard_map/dots/pallas_call | solution.py:348
  53.9 17.5 %all_to_all.10 = f32[64,2,128]{2,1,0:T(2,128)S(1)} all-to-all(f32[64,2,128]{2,1,0:T(2,128)S(1)} %bitcast.17), channel_id=1, replica_groups=mesh['station'=64,'sample'=4] {'station'}, dimensions={0} | all-to-all | bytes 131072 | tf_op jit(solution)/shard_map/all_to_all | solution.py:362
  71.4 0.9 %stations.1 = f32[16,16]{1,0:T(8,128)S(1)} custom-call(s32[64]{0:T(128)} %get-tuple-element.15.place_ref, s32[16]{0:T(128)} %count_ref.1, f32[128,128]{1,0:T(8,128)S(1)} %bitcast.18), custom_call_target="tpu_custom_call" | custom-call | tf_op jit(solution)/shard_map/stations/pallas_call | solution.py:364
  72.3 0.5 collective-permute-start.7
  72.8 5.1 %collective-permute-start.6 = (f32[16,16]{1,0:T(8,128)S(1)}, f32[16,16]{1,0:T(8,128)S(1)}, u32[]{:S(2)}, u32[]{:S(2)}) collective-permute-start(f32[16,16]{1,0:T(8,128)S(1)} %stations.1), channel_id=1, source_target_pairs={{0,2},{1,3},{2,0},{3,1},{4,6},{5,7},{6,4},{7,5},{8,10},{9,11},{10,... | collective-permute-start | bytes 3080 | tf_op jit(solution)/shard_map/ppermute | solution.py:372
  77.8 0.0 collective-permute-start.5
  77.8 0.0 collective-permute-done.7
  77.8 1.6 %collective-permute-done.6 = f32[16,16]{1,0:T(8,128)S(1)} collective-permute-done((f32[16,16]{1,0:T(8,128)S(1)}, f32[16,16]{1,0:T(8,128)S(1)}, u32[]{:S(2)}, u32[]{:S(2)}) %collective-permute-start.6) | collective-permute-done | bytes 1056 | tf_op jit(solution)/shard_map/ppermute | solution.py:372
  79.5 2.0 %collective-permute-done.5 = f32[16,16]{1,0:T(8,128)S(1)} collective-permute-done((f32[16,16]{1,0:T(8,128)S(1)}, f32[16,16]{1,0:T(8,128)S(1)}, u32[]{:S(2)}, u32[]{:S(2)}) %collective-permute-start.5) | collective-permute-done | bytes 1056 | tf_op jit(solution)/shard_map/ppermute | solution.py:372
  81.5 0.6 add_add_fusion
  (4 shorter events, 0.1 us)
Async XLA Ops:
  1.4 7.1 %collective-permute-start = (bf16[6,8,3584]{2,1,0:T(8,128)(2,1)S(1)}, bf16[6,8,3584]{2,1,0:T(8,128)(2,1)S(1)}, u32[]{:S(2)}, u32[]{:S(2)}) collective-permute-start(bf16[6,8,3584]{2,1,0:T(8,128)(2,1)S(1)} %get-tuple-element.16), channel_id=1, source_target_pairs={{4,8},{12,16},{20,24},{28,32},{36,40},{44,48},{52,56},{60,64},{68,... | collective-permute-start | bytes 1032200 | tf_op jit(solution)/shard_map/ppermute | solution.py:287
  2.0 6.4 %collective-permute-start.1 = (bf16[6,8,3584]{2,1,0:T(8,128)(2,1)S(1)}, bf16[6,8,3584]{2,1,0:T(8,128)(2,1)S(1)}, u32[]{:S(2)}, u32[]{:S(2)}) collective-permute-start(bf16[6,8,3584]{2,1,0:T(8,128)(2,1)S(1)} %get-tuple-element.17), channel_id=1, source_target_pairs={{0,4},{4,0},{8,12},{12,8},{16,20},{20,16},{24,28},{28,24},{32,36},... | collective-permute-start | bytes 1032200 | tf_op jit(solution)/shard_map/ppermute | solution.py:288
  5.4 17.7 %copy-start = (bf16[4,32,3584]{2,1,0:T(8,128)(2,1)S(1)}, bf16[4,32,3584]{2,1,0:T(8,128)(2,1)}, u32[]{:S(2)}) copy-start(bf16[4,32,3584]{2,1,0:T(8,128)(2,1)} %flux_ref.3) | copy-start | bytes 2752516
  5.4 17.7 %copy-start.1 = (f32[32,3584]{1,0:T(8,128)S(1)}, f32[32,3584]{1,0:T(8,128)}, u32[]{:S(2)}) copy-start(f32[32,3584]{1,0:T(8,128)} %coef_ref.3) | copy-start | bytes 1376260
  5.4 17.7 %copy-start.2 = (s32[4]{0:T(128)S(1)}, s32[4]{0:T(128)}, u32[]{:S(2)}) copy-start(s32[4]{0:T(128)} %steps_hbm.1) | copy-start | bytes 52
  8.4 23.9 %copy-start.3 = (s32[1024,4,1]{0,2,1:T(1,128)S(1)}, s32[1024,4,1]{0,2,1:T(1,128)}, u32[]{:S(2)}) copy-start(s32[1024,4,1]{0,2,1:T(1,128)} %param.11) | copy-start | bytes 49156
  8.4 23.9 %copy-start.4 = (s32[1024,4]{0,1:T(4,128)S(1)}, s32[1024,4]{0,1:T(4,128)}, u32[]{:S(2)}) copy-start(s32[1024,4]{0,1:T(4,128)} %param.12) | copy-start | bytes 49156
  8.5 42.8 %all-to-all-start = ((bf16[64,16,512]{2,1,0:T(8,128)(2,1)}), bf16[64,16,512]{2,1,0:T(8,128)(2,1)S(1)}, u32[]{:S(2)}, u32[]{:S(2)}) async-start(bf16[64,16,512]{2,1,0:T(8,128)(2,1)} %get-tuple-element.21), calls=%async_computation | async-start | bytes 2097152 | tf_op jit(solution)/shard_map/all_to_all | solution.py:316
  32.6 8.7 %collective-permute-start.2 = (bf16[32,3584]{1,0:T(8,128)(2,1)}, bf16[32,3584]{1,0:T(8,128)(2,1)S(1)}, u32[]{:S(2)}, u32[]{:S(2)}) collective-permute-start(bf16[32,3584]{1,0:T(8,128)(2,1)} %get-tuple-element.22), channel_id=1, source_target_pairs={{0,1},{1,0},{2,3},{3,2},{4,5},{5,4},{6,7},{7,6},{8,9},{9,8},{10,11... | collective-permute-start | bytes 688136 | tf_op jit(solution)/shard_map/ppermute | solution.py:336
  33.1 14.3 %collective-permute-start.3 = (bf16[32,3584]{1,0:T(8,128)(2,1)}, bf16[32,3584]{1,0:T(8,128)(2,1)S(1)}, u32[]{:S(2)}, u32[]{:S(2)}) collective-permute-start(bf16[32,3584]{1,0:T(8,128)(2,1)} %get-tuple-element.23), channel_id=1, source_target_pairs={{0,2},{1,3},{2,0},{3,1},{4,6},{5,7},{6,4},{7,5},{8,10},{9,11},{10,... | collective-permute-start | bytes 688136 | tf_op jit(solution)/shard_map/ppermute | solution.py:336
  36.5 12.3 %collective-permute-start.4 = (bf16[32,3584]{1,0:T(8,128)(2,1)}, bf16[32,3584]{1,0:T(8,128)(2,1)S(1)}, u32[]{:S(2)}, u32[]{:S(2)}) collective-permute-start(bf16[32,3584]{1,0:T(8,128)(2,1)} %get-tuple-element.24), channel_id=1, source_target_pairs={{0,3},{1,2},{2,1},{3,0},{4,7},{5,6},{6,5},{7,4},{8,11},{9,10},{10,... | collective-permute-start | bytes 688136 | tf_op jit(solution)/shard_map/ppermute | solution.py:336
  72.3 5.6 %collective-permute-start.7 = (f32[16,16]{1,0:T(8,128)S(1)}, f32[16,16]{1,0:T(8,128)S(1)}, u32[]{:S(2)}, u32[]{:S(2)}) collective-permute-start(f32[16,16]{1,0:T(8,128)S(1)} %stations.1), channel_id=1, source_target_pairs={{0,3},{1,2},{2,1},{3,0},{4,7},{5,6},{6,5},{7,4},{8,11},{9,10},{10,... | collective-permute-start | bytes 3080 | tf_op jit(solution)/shard_map/ppermute | solution.py:372
  72.8 6.7 %collective-permute-start.6 = (f32[16,16]{1,0:T(8,128)S(1)}, f32[16,16]{1,0:T(8,128)S(1)}, u32[]{:S(2)}, u32[]{:S(2)}) collective-permute-start(f32[16,16]{1,0:T(8,128)S(1)} %stations.1), channel_id=1, source_target_pairs={{0,2},{1,3},{2,0},{3,1},{4,6},{5,7},{6,4},{7,5},{8,10},{9,11},{10,... | collective-permute-start | bytes 3080 | tf_op jit(solution)/shard_map/ppermute | solution.py:372
  77.8 3.7 %collective-permute-start.5 = (f32[16,16]{1,0:T(8,128)S(1)}, f32[16,16]{1,0:T(8,128)S(1)}, u32[]{:S(2)}, u32[]{:S(2)}) collective-permute-start(f32[16,16]{1,0:T(8,128)S(1)} %stations.1), channel_id=1, source_target_pairs={{0,1},{1,0},{2,3},{3,2},{4,5},{5,4},{6,7},{7,6},{8,9},{9,8},{10,11... | collective-permute-start | bytes 3080 | tf_op jit(solution)/shard_map/ppermute | solution.py:372

commit v8 on v7

--- a/solution.py
+++ b/solution.py
@@ -233,8 +233,6 @@
     same = lax.rem(lax.broadcasted_iota(jnp.int32, (8, LANES), 1), 8) == lax.broadcasted_iota(
         jnp.int32, (8, LANES), 0
     )
-    own = lax.axis_index("sample")
-    odd_block = lax.rem(lax.div(lax.broadcasted_iota(jnp.int32, (8, LANES), 1), 32), 2) == 1
     loc_in.wait()
 
     def pick(group, carry):
@@ -242,10 +240,7 @@
         rows = [
             jnp.sum(jnp.where(same, sums_ref[loc_ref[at + i], at + i], 0.0), axis=0, keepdims=True) for i in range(8)
         ]
-        found = jnp.concatenate(rows, axis=0)
-        swapped = jnp.where(odd_block, pltpu.roll(found, 32, 1), pltpu.roll(found, LANES - 32, 1))
-        found = jnp.where((own & 1) == 1, swapped, found)
-        out_ref[pl.ds(at, 8)] = jnp.where((own & 2) == 2, pltpu.roll(found, 64, 1), found)
+        out_ref[pl.ds(at, 8)] = jnp.concatenate(rows, axis=0)
         return carry
 
     lax.fori_loop(0, slots // 8, pick, 0, unroll=2)
@@ -261,7 +256,8 @@
         sums_ref[station : station + 1] = jnp.where(0 < count_ref[station], total, 0.0)
     lane = lax.broadcasted_iota(jnp.int32, (LANES, 16), 0)
     sample = lax.broadcasted_iota(jnp.int32, (LANES, 16), 1)
-    fold = (lax.div(lane, 8) == sample).astype(jnp.float32)
+    own = lax.axis_index("sample")
+    fold = ((lax.div(lane, 8) ^ (4 * own)) == sample).astype(jnp.float32)
     out_ref[...] = jnp.dot(
         sums_ref[...], fold, precision=lax.Precision.HIGHEST, preferred_element_type=jnp.float32
     )

time: 81.8 us -> 80.3 us (0.982); the launches traced: 82.1 us -> 79.6 us
  blocking collectives: 17.5 us -> 16.1 us
    ppermute x3, waiting for transfers between devices: 11.4 us -> 9.89 us  [body(): lax.ppermute(finals[turn], 'sample', [(i, i ^ turn) for i in range(PARTS)])]
    all_to_all x1, blocking collectives: 17.5 us -> 16.1 us  [body(): lax.all_to_all(values.reshape(bands, CAP, LANES), 'station', split_axis=0...]
    all_to_all x1, waiting for transfers between devices: 2.48 us -> 3.84 us  [body(): lax.all_to_all(sent, 'station', split_axis=0, concat_axis=0, tiled=True)]
    pallas_call x1, Pallas kernels: 2.63 us -> 1.56 us  [body(): pl.pallas_call(dots_kernel, out_shape=jax.ShapeDtypeStruct((bands * CAP,...]
    pallas_call x1, Pallas kernels: 9.23 us -> 10.2 us  [body(): pl.pallas_call(diffuse_kernel, out_shape=[jax.ShapeDtypeStruct((samples *...]
  transfers between devices with their start and end apart: 9 -> 9, of which waited for: 6 -> 6; matrix products, arithmetic and copies ran while one was open for 1% -> 1% of each run, Pallas kernels for 15% -> 17%
where the time goes in v8:
time: 80.3 us; the launch traced here: 79.6 us
  starting transfers between devices  27.6 us (34%)
  waiting for transfers between devices  17.4 us (22%)
  Pallas kernels  17 us (21%)
  blocking collectives  16.1 us (20%)
  other arithmetic  0.89 us (1%)
    all_to_all x1, blocking collectives, body(): lax.all_to_all(values.reshape(bands, CAP, LANES), 'station', split_axis=0...  16.1 us
    all_to_all x1, starting transfers between devices, body(): lax.all_to_all(sent, 'station', split_axis=0, concat_axis=0, tiled=True)  14.6 us
    pallas_call x1, Pallas kernels, body(): pl.pallas_call(diffuse_kernel, out_shape=[jax.ShapeDtypeStruct((samples *...  10.2 us
    ppermute x3, waiting for transfers between devices, body(): lax.ppermute(finals[turn], 'sample', [(i, i ^ turn) for i in range(PARTS)])  9.89 us
    ppermute x3, starting transfers between devices, body(): lax.ppermute(share, 'sample', [(i, i ^ flip) for i in range(PARTS)])  5.45 us
    all_to_all x1, waiting for transfers between devices, body(): lax.all_to_all(sent, 'station', split_axis=0, concat_axis=0, tiled=True)  3.84 us
    ppermute x3, waiting for transfers between devices, body(): lax.ppermute(share, 'sample', [(i, i ^ flip) for i in range(PARTS)])  3.65 us
    ppermute x3, starting transfers between devices, body(): lax.ppermute(finals[turn], 'sample', [(i, i ^ turn) for i in range(PARTS)])  3.52 us
  transfers between devices with their start and end apart: 9, of which 6 were waited for; matrix products, arithmetic and copies ran while one was open for 1% of the time, Pallas kernels for 17%

profile of v8, /device:TPU:8, one launch (start us, length us, event | category | flops | bytes accessed | tf_op | source)
XLA Modules:
  0.0 79.6 jit_solution(380594934687592678)
XLA Ops:
  0.0 1.3 %edges.1 = (bf16[6,8,3584]{2,1,0:T(8,128)(2,1)S(1)}, bf16[6,8,3584]{2,1,0:T(8,128)(2,1)S(1)}) custom-call(bf16[4,32,3584]{2,1,0:T(8,128)(2,1)} %flux_ref.3, f32[32,3584]{1,0:T(8,128)} %coef_ref.3), custom_call_target="tpu_custom_call" | custom-call | tf_op jit(solution)/shard_map/edges/pallas_call | solution.py:276
  1.4 0.7 collective-permute-start
  2.0 3.3 %collective-permute-start.1 = (bf16[6,8,3584]{2,1,0:T(8,128)(2,1)S(1)}, bf16[6,8,3584]{2,1,0:T(8,128)(2,1)S(1)}, u32[]{:S(2)}, u32[]{:S(2)}) collective-permute-start(bf16[6,8,3584]{2,1,0:T(8,128)(2,1)S(1)} %get-tuple-element.17), channel_id=1, source_target_pairs={{0,4},{4,0},{8,12},{12,8},{16,20},{20,16},{24,28},{28,24},{32,36},... | collective-permute-start | bytes 1032200 | tf_op jit(solution)/shard_map/ppermute | solution.py:284
  5.4 0.0 copy-start
  5.4 0.0 copy-start.1
  5.4 0.0 copy-start.2
  5.4 3.0 %pack.1 = (bf16[64,16,512]{2,1,0:T(8,128)(2,1)}, s32[64]{0:T(128)}) custom-call(s32[4,1,1024]{2,1,0:T(1,128)} %bitcast.19, bf16[16,4,16384]{2,1,0:T(4,128)(2,1)} %prints_hbm.1), custom_call_target="tpu_custom_call" | custom-call | tf_op jit(solution)/shard_map/pack/pallas_call | solution.py:287
  8.4 0.0 copy-start.3
  8.4 0.0 copy-start.4
  8.4 0.0 collective-permute-done.away_ref
  8.5 0.0 collective-permute-done.1.beside_ref
  8.5 14.6 %all-to-all-start = ((bf16[64,16,512]{2,1,0:T(8,128)(2,1)}), bf16[64,16,512]{2,1,0:T(8,128)(2,1)S(1)}, u32[]{:S(2)}, u32[]{:S(2)}) async-start(bf16[64,16,512]{2,1,0:T(8,128)(2,1)} %get-tuple-element.21), calls=%async_computation | async-start | bytes 2097152 | tf_op jit(solution)/shard_map/all_to_all | solution.py:312
  23.1 0.0 copy-done
  23.1 0.0 copy-done.1
  23.1 0.0 copy-done.2
  23.1 10.2 %diffuse.1 = (bf16[32,3584]{1,0:T(8,128)(2,1)S(1)}, bf16[32,3584]{1,0:T(8,128)(2,1)}, bf16[32,3584]{1,0:T(8,128)(2,1)}, bf16[32,3584]{1,0:T(8,128)(2,1)}) custom-call(s32[4]{0:T(128)S(1)} %copy-done.2, bf16[4,32,3584]{2,1,0:T(8,128)(2,1)S(1)} %copy-done, bf16[6,8,3584]{2,1,0:T(8,128)(2,1)S(1)} %collective-permute-done.away_ref, ...), custom_call_target="tpu_custom_call" | custom-call | tf_op jit(solution)/shard_map/diffuse/pallas_call | solution.py:314
  33.3 0.0 copy-done.3
  33.3 0.0 copy-done.4
  33.4 0.1 reshape.46
  33.4 0.1 reshape.47
  33.5 0.8 %collective-permute-start.2 = (bf16[32,3584]{1,0:T(8,128)(2,1)}, bf16[32,3584]{1,0:T(8,128)(2,1)S(1)}, u32[]{:S(2)}, u32[]{:S(2)}) collective-permute-start(bf16[32,3584]{1,0:T(8,128)(2,1)} %get-tuple-element.22), channel_id=1, source_target_pairs={{0,1},{1,0},{2,3},{3,2},{4,5},{5,4},{6,7},{7,6},{8,9},{9,8},{10,11... | collective-permute-start | bytes 688136 | tf_op jit(solution)/shard_map/ppermute | solution.py:332
  34.3 0.9 %collective-permute-start.3 = (bf16[32,3584]{1,0:T(8,128)(2,1)}, bf16[32,3584]{1,0:T(8,128)(2,1)S(1)}, u32[]{:S(2)}, u32[]{:S(2)}) collective-permute-start(bf16[32,3584]{1,0:T(8,128)(2,1)} %get-tuple-element.23), channel_id=1, source_target_pairs={{0,2},{1,3},{2,0},{3,1},{4,6},{5,7},{6,4},{7,5},{8,10},{9,11},{10,... | collective-permute-start | bytes 688136 | tf_op jit(solution)/shard_map/ppermute | solution.py:332
  35.2 1.8 %collective-permute-start.4 = (bf16[32,3584]{1,0:T(8,128)(2,1)}, bf16[32,3584]{1,0:T(8,128)(2,1)S(1)}, u32[]{:S(2)}, u32[]{:S(2)}) collective-permute-start(bf16[32,3584]{1,0:T(8,128)(2,1)} %get-tuple-element.24), channel_id=1, source_target_pairs={{0,3},{1,2},{2,1},{3,0},{4,7},{5,6},{6,5},{7,4},{8,11},{9,10},{10,... | collective-permute-start | bytes 688136 | tf_op jit(solution)/shard_map/ppermute | solution.py:332
  37.0 0.1 reduce_min.19
  37.2 0.1 reduce_max.19
  37.3 0.1 copy.11
  37.4 0.1 reshape.48.loc_hbm
  37.5 4.7 %collective-permute-done.2.refs_1_ = bf16[32,3584]{1,0:T(8,128)(2,1)S(1)} collective-permute-done((bf16[32,3584]{1,0:T(8,128)(2,1)}, bf16[32,3584]{1,0:T(8,128)(2,1)S(1)}, u32[]{:S(2)}, u32[]{:S(2)}) %collective-permute-start.2) | collective-permute-done | bytes 229408 | tf_op jit(solution)/shard_map/ppermute | solution.py:332
  42.2 3.8 %collective-permute-done.3.refs_2_ = bf16[32,3584]{1,0:T(8,128)(2,1)S(1)} collective-permute-done((bf16[32,3584]{1,0:T(8,128)(2,1)}, bf16[32,3584]{1,0:T(8,128)(2,1)S(1)}, u32[]{:S(2)}, u32[]{:S(2)}) %collective-permute-start.3) | collective-permute-done | bytes 229408 | tf_op jit(solution)/shard_map/ppermute | solution.py:332
  46.0 1.4 %collective-permute-done.4.refs_3_ = bf16[32,3584]{1,0:T(8,128)(2,1)S(1)} collective-permute-done((bf16[32,3584]{1,0:T(8,128)(2,1)}, bf16[32,3584]{1,0:T(8,128)(2,1)S(1)}, u32[]{:S(2)}, u32[]{:S(2)}) %collective-permute-start.4) | collective-permute-done | bytes 229408 | tf_op jit(solution)/shard_map/ppermute | solution.py:332
  47.4 3.8 %all-to-all-done.prints_ref = bf16[64,16,512]{2,1,0:T(8,128)(2,1)S(1)} async-done(((bf16[64,16,512]{2,1,0:T(8,128)(2,1)}), bf16[64,16,512]{2,1,0:T(8,128)(2,1)S(1)}, u32[]{:S(2)}, u32[]{:S(2)}) %all-to-all-start) | async-done | bytes 1048608 | tf_op jit(solution)/shard_map/all_to_all | solution.py:312
  51.3 1.6 %dots.1 = f32[128,128]{1,0:T(8,128)S(1)} custom-call(s32[128]{0:T(128)S(1)} %reshape.48.loc_hbm, bf16[64,16,512]{2,1,0:T(8,128)(2,1)S(1)} %all-to-all-done.prints_ref, bf16[32,3584]{1,0:T(8,128)(2,1)S(1)} %get-tuple-element.18.refs_0_, bf16[32,3584]{1,0:T(8,128)(2,1)S(1)} %collective-permute-done.2.refs_1_, ...), custom_call_target="tpu_custom_call" | custom-call | tf_op jit(solution)/shard_map/dots/pallas_call | solution.py:344
  52.8 16.1 %all_to_all.10 = f32[64,2,128]{2,1,0:T(2,128)S(1)} all-to-all(f32[64,2,128]{2,1,0:T(2,128)S(1)} %bitcast.17), channel_id=1, replica_groups=mesh['station'=64,'sample'=4] {'station'}, dimensions={0} | all-to-all | bytes 131072 | tf_op jit(solution)/shard_map/all_to_all | solution.py:358
  68.9 0.9 %stations.1 = f32[16,16]{1,0:T(8,128)S(1)} custom-call(s32[64]{0:T(128)} %get-tuple-element.15.place_ref, s32[16]{0:T(128)} %count_ref.1, f32[128,128]{1,0:T(8,128)S(1)} %bitcast.18), custom_call_target="tpu_custom_call" | custom-call | tf_op jit(solution)/shard_map/stations/pallas_call | solution.py:360
  69.9 1.8 %collective-permute-start.7 = (f32[16,16]{1,0:T(8,128)S(1)}, f32[16,16]{1,0:T(8,128)S(1)}, u32[]{:S(2)}, u32[]{:S(2)}) collective-permute-start(f32[16,16]{1,0:T(8,128)S(1)} %stations.1), channel_id=1, source_target_pairs={{0,3},{1,2},{2,1},{3,0},{4,7},{5,6},{6,5},{7,4},{8,11},{9,10},{10,... | collective-permute-start | bytes 3080 | tf_op jit(solution)/shard_map/ppermute | solution.py:368
  71.6 3.7 %collective-permute-start.6 = (f32[16,16]{1,0:T(8,128)S(1)}, f32[16,16]{1,0:T(8,128)S(1)}, u32[]{:S(2)}, u32[]{:S(2)}) collective-permute-start(f32[16,16]{1,0:T(8,128)S(1)} %stations.1), channel_id=1, source_target_pairs={{0,2},{1,3},{2,0},{3,1},{4,6},{5,7},{6,4},{7,5},{8,10},{9,11},{10,... | collective-permute-start | bytes 3080 | tf_op jit(solution)/shard_map/ppermute | solution.py:368
  75.3 0.0 collective-permute-start.5
  75.3 0.0 collective-permute-done.7
  75.3 1.6 %collective-permute-done.6 = f32[16,16]{1,0:T(8,128)S(1)} collective-permute-done((f32[16,16]{1,0:T(8,128)S(1)}, f32[16,16]{1,0:T(8,128)S(1)}, u32[]{:S(2)}, u32[]{:S(2)}) %collective-permute-start.6) | collective-permute-done | bytes 1056 | tf_op jit(solution)/shard_map/ppermute | solution.py:368
  76.9 2.0 %collective-permute-done.5 = f32[16,16]{1,0:T(8,128)S(1)} collective-permute-done((f32[16,16]{1,0:T(8,128)S(1)}, f32[16,16]{1,0:T(8,128)S(1)}, u32[]{:S(2)}, u32[]{:S(2)}) %collective-permute-start.5) | collective-permute-done | bytes 1056 | tf_op jit(solution)/shard_map/ppermute | solution.py:368
  79.0 0.6 add_add_fusion
  (4 shorter events, 0.1 us)
Async XLA Ops:
  1.4 7.1 %collective-permute-start = (bf16[6,8,3584]{2,1,0:T(8,128)(2,1)S(1)}, bf16[6,8,3584]{2,1,0:T(8,128)(2,1)S(1)}, u32[]{:S(2)}, u32[]{:S(2)}) collective-permute-start(bf16[6,8,3584]{2,1,0:T(8,128)(2,1)S(1)} %get-tuple-element.16), channel_id=1, source_target_pairs={{4,8},{12,16},{20,24},{28,32},{36,40},{44,48},{52,56},{60,64},{68,... | collective-permute-start | bytes 1032200 | tf_op jit(solution)/shard_map/ppermute | solution.py:283
  2.0 6.4 %collective-permute-start.1 = (bf16[6,8,3584]{2,1,0:T(8,128)(2,1)S(1)}, bf16[6,8,3584]{2,1,0:T(8,128)(2,1)S(1)}, u32[]{:S(2)}, u32[]{:S(2)}) collective-permute-start(bf16[6,8,3584]{2,1,0:T(8,128)(2,1)S(1)} %get-tuple-element.17), channel_id=1, source_target_pairs={{0,4},{4,0},{8,12},{12,8},{16,20},{20,16},{24,28},{28,24},{32,36},... | collective-permute-start | bytes 1032200 | tf_op jit(solution)/shard_map/ppermute | solution.py:284
  5.4 17.7 %copy-start = (bf16[4,32,3584]{2,1,0:T(8,128)(2,1)S(1)}, bf16[4,32,3584]{2,1,0:T(8,128)(2,1)}, u32[]{:S(2)}) copy-start(bf16[4,32,3584]{2,1,0:T(8,128)(2,1)} %flux_ref.3) | copy-start | bytes 2752516
  5.4 17.7 %copy-start.1 = (f32[32,3584]{1,0:T(8,128)S(1)}, f32[32,3584]{1,0:T(8,128)}, u32[]{:S(2)}) copy-start(f32[32,3584]{1,0:T(8,128)} %coef_ref.3) | copy-start | bytes 1376260
  5.4 17.7 %copy-start.2 = (s32[4]{0:T(128)S(1)}, s32[4]{0:T(128)}, u32[]{:S(2)}) copy-start(s32[4]{0:T(128)} %steps_hbm.1) | copy-start | bytes 52
  8.4 24.9 %copy-start.3 = (s32[1024,4,1]{0,2,1:T(1,128)S(1)}, s32[1024,4,1]{0,2,1:T(1,128)}, u32[]{:S(2)}) copy-start(s32[1024,4,1]{0,2,1:T(1,128)} %param.11) | copy-start | bytes 49156
  8.4 24.9 %copy-start.4 = (s32[1024,4]{0,1:T(4,128)S(1)}, s32[1024,4]{0,1:T(4,128)}, u32[]{:S(2)}) copy-start(s32[1024,4]{0,1:T(4,128)} %param.12) | copy-start | bytes 49156
  8.5 42.8 %all-to-all-start = ((bf16[64,16,512]{2,1,0:T(8,128)(2,1)}), bf16[64,16,512]{2,1,0:T(8,128)(2,1)S(1)}, u32[]{:S(2)}, u32[]{:S(2)}) async-start(bf16[64,16,512]{2,1,0:T(8,128)(2,1)} %get-tuple-element.21), calls=%async_computation | async-start | bytes 2097152 | tf_op jit(solution)/shard_map/all_to_all | solution.py:312
  33.5 8.7 %collective-permute-start.2 = (bf16[32,3584]{1,0:T(8,128)(2,1)}, bf16[32,3584]{1,0:T(8,128)(2,1)S(1)}, u32[]{:S(2)}, u32[]{:S(2)}) collective-permute-start(bf16[32,3584]{1,0:T(8,128)(2,1)} %get-tuple-element.22), channel_id=1, source_target_pairs={{0,1},{1,0},{2,3},{3,2},{4,5},{5,4},{6,7},{7,6},{8,9},{9,8},{10,11... | collective-permute-start | bytes 688136 | tf_op jit(solution)/shard_map/ppermute | solution.py:332
  34.3 11.7 %collective-permute-start.3 = (bf16[32,3584]{1,0:T(8,128)(2,1)}, bf16[32,3584]{1,0:T(8,128)(2,1)S(1)}, u32[]{:S(2)}, u32[]{:S(2)}) collective-permute-start(bf16[32,3584]{1,0:T(8,128)(2,1)} %get-tuple-element.23), channel_id=1, source_target_pairs={{0,2},{1,3},{2,0},{3,1},{4,6},{5,7},{6,4},{7,5},{8,10},{9,11},{10,... | collective-permute-start | bytes 688136 | tf_op jit(solution)/shard_map/ppermute | solution.py:332
  35.2 12.2 %collective-permute-start.4 = (bf16[32,3584]{1,0:T(8,128)(2,1)}, bf16[32,3584]{1,0:T(8,128)(2,1)S(1)}, u32[]{:S(2)}, u32[]{:S(2)}) collective-permute-start(bf16[32,3584]{1,0:T(8,128)(2,1)} %get-tuple-element.24), channel_id=1, source_target_pairs={{0,3},{1,2},{2,1},{3,0},{4,7},{5,6},{6,5},{7,4},{8,11},{9,10},{10,... | collective-permute-start | bytes 688136 | tf_op jit(solution)/shard_map/ppermute | solution.py:332
  69.9 5.5 %collective-permute-start.7 = (f32[16,16]{1,0:T(8,128)S(1)}, f32[16,16]{1,0:T(8,128)S(1)}, u32[]{:S(2)}, u32[]{:S(2)}) collective-permute-start(f32[16,16]{1,0:T(8,128)S(1)} %stations.1), channel_id=1, source_target_pairs={{0,3},{1,2},{2,1},{3,0},{4,7},{5,6},{6,5},{7,4},{8,11},{9,10},{10,... | collective-permute-start | bytes 3080 | tf_op jit(solution)/shard_map/ppermute | solution.py:368
  71.6 5.3 %collective-permute-start.6 = (f32[16,16]{1,0:T(8,128)S(1)}, f32[16,16]{1,0:T(8,128)S(1)}, u32[]{:S(2)}, u32[]{:S(2)}) collective-permute-start(f32[16,16]{1,0:T(8,128)S(1)} %stations.1), channel_id=1, source_target_pairs={{0,2},{1,3},{2,0},{3,1},{4,6},{5,7},{6,4},{7,5},{8,10},{9,11},{10,... | collective-permute-start | bytes 3080 | tf_op jit(solution)/shard_map/ppermute | solution.py:368
  75.3 3.7 %collective-permute-start.5 = (f32[16,16]{1,0:T(8,128)S(1)}, f32[16,16]{1,0:T(8,128)S(1)}, u32[]{:S(2)}, u32[]{:S(2)}) collective-permute-start(f32[16,16]{1,0:T(8,128)S(1)} %stations.1), channel_id=1, source_target_pairs={{0,1},{1,0},{2,3},{3,2},{4,5},{5,4},{6,7},{7,6},{8,9},{9,8},{10,11... | collective-permute-start | bytes 3080 | tf_op jit(solution)/shard_map/ppermute | solution.py:368
